TPU v7x, 512 devices: a whole 4x4x16 slice. The times are simulated.
512 devices in a mesh: dp: 16 (over x, z_hi), seq: 32 (over y, z_lo, core).
Axes of the slice: x: 4, y: 4, z: 16 (z_hi: 4, z_lo: 4; z = z_hi * 4 + z_lo), core: 2. Of those that a mesh axis runs over, the one named last changes fastest.
Arguments:
- attention_queries: bfloat16 [16, 32, 128, 1536], P('dp', 'seq'), may hold values from -40 to 40
- attention_keys: bfloat16 [16, 32, 128, 1536], P('dp', 'seq'), may hold values from -40 to 40
- attention_values: bfloat16 [16, 32, 128, 1536], P('dp', 'seq'), may hold values from -6 to 6
- cotangent: bfloat16 [16, 32, 128, 1536], P('dp', 'seq'), may hold values from -1.5 to 1.5
- frozen_output_weight: bfloat16 [2, 1536, 1536], P(None, 'dp'), may hold values from -0.15625 to 0.15625
- adapter_down_factor: bfloat16 [2, 1536, 64], P(None, 'dp'), may hold values from -0.15625 to 0.15625
- adapter_up_factor: bfloat16 [2, 64, 1536], P(None, None, 'dp'), may hold values from -0.75 to 0.75
Outputs:
- blended: bfloat16 [16, 32, 128, 1536], P('dp', 'seq')
- grad_query: bfloat16 [16, 32, 128, 1536], P('dp', 'seq')
- grad_key: bfloat16 [16, 32, 128, 1536], P('dp', 'seq')
- grad_value: bfloat16 [16, 32, 128, 1536], P('dp', 'seq')
- grad_down: float32 [2, 1536, 64], P(None, 'dp')
- grad_up: float32 [2, 64, 1536], P(None, None, 'dp')
All inputs are finite; a program needn't handle non-finite values.
Results may differ from a plain program's by a relative error of at most 0.029.
Values may be sent and summed in bfloat16 or wider, within the bound.
No kernel may reach another device: no remote copies, remote signals or barrier semaphores. Data moves between devices by JAX's collectives and lax.ppermute only.
A program may use at most 128 MiB of HBM per device.

v0:
```python
import jax
import jax.numpy as jnp
from jax import lax
from jax.sharding import PartitionSpec as P

HDIM = 128


adapter_gain = 2.0


def attend(query_heads, key_heads, value_heads):
    scale_factor = HDIM ** (-0.5)
    scores = (
        jnp.einsum("blhe,bmhe->bhlm", query_heads, key_heads, preferred_element_type=jnp.float32)
        * scale_factor
    )
    attention = jax.nn.softmax(scores, axis=-1)
    rounded = attention.astype(jnp.bfloat16)
    blended = jnp.einsum(
        "bhlm,bmhe->blhe", rounded, value_heads, preferred_element_type=jnp.float32
    )
    return (attention, blended.astype(jnp.bfloat16))


def attend_back(query_heads, key_heads, value_heads, attention, upstream):
    scale_factor = HDIM ** (-0.5)
    rounded = attention.astype(jnp.bfloat16)
    grad_value = jnp.einsum(
        "bhlm,blhe->bmhe", rounded, upstream, preferred_element_type=jnp.float32
    )
    grad_attention = jnp.einsum(
        "blhe,bmhe->bhlm", upstream, value_heads, preferred_element_type=jnp.float32
    )
    centre = jnp.sum(attention * grad_attention, axis=-1, keepdims=True)
    grad_scores = (attention * (grad_attention - centre) * scale_factor).astype(jnp.bfloat16)
    grad_query = jnp.einsum(
        "bhlm,bmhe->blhe", grad_scores, key_heads, preferred_element_type=jnp.float32
    )
    grad_key = jnp.einsum(
        "bhlm,blhe->bmhe", grad_scores, query_heads, preferred_element_type=jnp.float32
    )
    return (grad_query, grad_key, grad_value)


def reduce_trailing(left, right):
    return lax.dot_general(
        left, right, (((1,), (1,)), ((), ())), preferred_element_type=jnp.float32
    )


def reduce_leading(left, right):
    return lax.dot_general(
        left, right, (((0,), (0,)), ((), ())), preferred_element_type=jnp.float32
    )


def local(
    attention_queries,
    attention_keys,
    attention_values,
    cotangent,
    frozen_output_weight,
    adapter_down_factor,
    adapter_up_factor,
):
    clip_count, frame_local, patch_count, feature_count = attention_queries.shape
    model_width = cotangent.shape[-1]
    head_count = feature_count // HDIM
    row_count = clip_count * frame_local * patch_count
    whole_weight, complete_down_factor, complete_up_factor = (
        lax.all_gather(frozen_output_weight, "dp", axis=1, tiled=True),
        lax.all_gather(adapter_down_factor, "dp", axis=1, tiled=True),
        lax.all_gather(adapter_up_factor, "dp", axis=2, tiled=True),
    )

    def to_heads(tensor):
        return tensor.reshape(-1, patch_count, head_count, HDIM)

    query_heads, key_heads, value_heads = (
        to_heads(attention_queries),
        to_heads(attention_keys),
        to_heads(attention_values),
    )
    spatial_probs, spatial_out = attend(query_heads, key_heads, value_heads)
    patch_query, patch_key, patch_value = (
        lax.all_to_all(attention_queries, "seq", split_axis=2, concat_axis=1, tiled=True),
        lax.all_to_all(attention_keys, "seq", split_axis=2, concat_axis=1, tiled=True),
        lax.all_to_all(attention_values, "seq", split_axis=2, concat_axis=1, tiled=True),
    )
    frame_count, patch_local = (patch_query.shape[1], patch_query.shape[2])

    def to_time(tensor):
        tensor = tensor.reshape(clip_count, frame_count, patch_local, head_count, HDIM)
        return jnp.transpose(tensor, (0, 2, 1, 3, 4)).reshape(
            clip_count * patch_local, frame_count, head_count, HDIM
        )

    def from_time(tensor):
        tensor = tensor.reshape(clip_count, patch_local, frame_count, head_count, HDIM)
        return jnp.transpose(tensor, (0, 2, 1, 3, 4)).reshape(
            clip_count, frame_count, patch_local, head_count * HDIM
        )

    time_query, time_key, time_value = (
        to_time(patch_query),
        to_time(patch_key),
        to_time(patch_value),
    )
    temporal_probs, temporal_out = attend(time_query, time_key, time_value)
    returned = lax.all_to_all(
        from_time(temporal_out), "seq", split_axis=1, concat_axis=2, tiled=True
    )
    attention_branches = (
        spatial_out.reshape(row_count, feature_count),
        returned.reshape(row_count, feature_count),
    )
    flattened_upstream = cotangent.reshape(row_count, model_width)
    summed_total = jnp.zeros((row_count, model_width), jnp.float32)
    down_factor_gradients, up_factor_gradients, upstreams = ([], [], [])
    for branch_member in range(2):
        reduced_rank_product = jnp.dot(
            attention_branches[branch_member],
            complete_down_factor[branch_member],
            preferred_element_type=jnp.float32,
        ).astype(jnp.bfloat16)
        summed_total = (
            summed_total
            + jnp.dot(
                attention_branches[branch_member],
                whole_weight[branch_member],
                preferred_element_type=jnp.float32,
            )
            + adapter_gain
            * jnp.dot(
                reduced_rank_product,
                complete_up_factor[branch_member],
                preferred_element_type=jnp.float32,
            )
        )
        backward_rank = reduce_trailing(
            flattened_upstream, complete_up_factor[branch_member]
        ).astype(jnp.bfloat16)
        branch_gradient = reduce_trailing(
            flattened_upstream, whole_weight[branch_member]
        ) + adapter_gain * reduce_trailing(backward_rank, complete_down_factor[branch_member])
        upstreams.append(branch_gradient.astype(jnp.bfloat16))
        up_factor_gradients.append(
            adapter_gain * reduce_leading(reduced_rank_product, flattened_upstream)
        )
        down_factor_gradients.append(
            adapter_gain * reduce_leading(attention_branches[branch_member], backward_rank)
        )
    blended = summed_total.astype(jnp.bfloat16).reshape(
        clip_count, frame_local, patch_count, model_width
    )
    space_grads = attend_back(
        query_heads, key_heads, value_heads, spatial_probs, to_heads(upstreams[0])
    )
    time_upstream = lax.all_to_all(
        upstreams[1].reshape(clip_count, frame_local, patch_count, feature_count),
        "seq",
        split_axis=2,
        concat_axis=1,
        tiled=True,
    )
    time_grads = attend_back(
        time_query, time_key, time_value, temporal_probs, to_time(time_upstream)
    )
    sent_query, sent_key, sent_value = (
        from_time(time_grads[0].astype(jnp.bfloat16)),
        from_time(time_grads[1].astype(jnp.bfloat16)),
        from_time(time_grads[2].astype(jnp.bfloat16)),
    )
    back_query, back_key, back_value = (
        lax.all_to_all(sent_query, "seq", split_axis=1, concat_axis=2, tiled=True),
        lax.all_to_all(sent_key, "seq", split_axis=1, concat_axis=2, tiled=True),
        lax.all_to_all(sent_value, "seq", split_axis=1, concat_axis=2, tiled=True),
    )

    def combine(space, arrived):
        space = space.reshape(clip_count, frame_local, patch_count, feature_count)
        return (space + arrived.astype(jnp.float32)).astype(jnp.bfloat16)

    grad_query = combine(space_grads[0], back_query)
    grad_key = combine(space_grads[1], back_key)
    grad_value = combine(space_grads[2], back_value)
    local_down = jnp.stack(down_factor_gradients)
    local_up = jnp.stack(up_factor_gradients)
    framed_down, framed_up = (
        lax.psum(local_down.astype(jnp.bfloat16), "seq").astype(jnp.float32),
        lax.psum(local_up.astype(jnp.bfloat16), "seq").astype(jnp.float32),
    )
    grad_down, grad_up = (
        lax.psum_scatter(
            framed_down.astype(jnp.bfloat16), "dp", scatter_dimension=1, tiled=True
        ).astype(jnp.float32),
        lax.psum_scatter(
            framed_up.astype(jnp.bfloat16), "dp", scatter_dimension=2, tiled=True
        ).astype(jnp.float32),
    )
    return (blended, grad_query, grad_key, grad_value, grad_down, grad_up)


def solution(mesh):
    in_specs = (
        P("dp", "seq", None, None),
        P("dp", "seq", None, None),
        P("dp", "seq", None, None),
        P("dp", "seq", None, None),
        P(None, "dp", None),
        P(None, "dp", None),
        P(None, None, "dp"),
    )
    out_specs = (
        P("dp", "seq", None, None),
        P("dp", "seq", None, None),
        P("dp", "seq", None, None),
        P("dp", "seq", None, None),
        P(None, "dp", None),
        P(None, None, "dp"),
    )
    return jax.shard_map(local, mesh=mesh, in_specs=in_specs, out_specs=out_specs, check_vma=False)
```

profile of v0, /device:TPU:1, one launch (start us, length us, event | category | flops | bytes accessed | tf_op | source)
XLA Modules:
  0.0 846.2 jit_solution(1873505409013054221)
XLA Ops:
  7.9 1.6 copy.245
  10.1 3.0 reduce.16
  13.2 1.0 reshape.323
  14.2 10.4 %all-to-all-start = ((bf16[32,2,3072]{2,1,0:T(2,128)(2,1)}), bf16[32,2,3072]{2,1,0:T(2,128)(2,1)S(1)}, u32[]{:S(2)}, u32[]{:S(2)}) async-start(bf16[32,2,3072]{2,1,0:T(2,128)(2,1)} %reshape.323), calls=%async_computation | async-start | bytes 786432 | tf_op jit(solution)/shard_map/all_to_all | solution.py:87
  24.6 1.6 copy.244
  26.2 3.0 reduce.15
  29.2 1.0 reshape.321
  30.2 8.5 %all-to-all-done = bf16[32,2,3072]{2,1,0:T(2,128)(2,1)S(1)} async-done(((bf16[32,2,3072]{2,1,0:T(2,128)(2,1)}), bf16[32,2,3072]{2,1,0:T(2,128)(2,1)S(1)}, u32[]{:S(2)}, u32[]{:S(2)}) %all-to-all-start) | async-done | bytes 393248 | tf_op jit(solution)/shard_map/all_to_all | solution.py:87
  38.7 3.7 all-to-all-start.1
  42.4 1.6 copy.243
  44.0 3.0 reduce.14
  47.1 1.0 reshape.319
  48.1 34.5 %all-to-all-done.1 = bf16[32,2,3072]{2,1,0:T(2,128)(2,1)S(1)} async-done(((bf16[32,2,3072]{2,1,0:T(2,128)(2,1)}), bf16[32,2,3072]{2,1,0:T(2,128)(2,1)S(1)}, u32[]{:S(2)}, u32[]{:S(2)}) %all-to-all-start.1) | async-done | bytes 393248 | tf_op jit(solution)/shard_map/all_to_all | solution.py:88
  82.6 5.2 all-to-all-start.2
  92.3 158.1 %all_gather.10 = bf16[2,1536,64]{2,0,1:T(2,128)(2,1)S(1)} all-gather(bf16[2,96,64]{2,0,1:T(2,128)(2,1)S(1)} %copy.132), channel_id=1, replica_groups=mesh['dp'=16,'seq'=32] {'dp'}, dimensions={1}, use_global_device_ids=true | all-gather | bytes 417792 | tf_op jit(solution)/shard_map/all_gather | solution.py:73
  250.4 1.1 fusion.114
  252.5 88.2 %all_gather.11 = bf16[2,64,1536]{1,0,2:T(2,128)(2,1)S(1)} all-gather(bf16[2,64,96]{1,0,2:T(2,128)(2,1)S(1)} %copy.134), channel_id=1, replica_groups=mesh['dp'=16,'seq'=32] {'dp'}, dimensions={2}, use_global_device_ids=true | all-gather | bytes 417792 | tf_op jit(solution)/shard_map/all_gather | solution.py:74
  340.7 1.1 fusion.113
  342.6 2.2 bitcast_reduce_fusion
  344.9 1.1 reshape.278
  346.3 2.2 bitcast_reduce_fusion.1
  348.5 1.1 reshape.280
  349.6 2.7 reshape.320
  352.4 2.2 bitcast_reduce_fusion.2
  354.9 2.1 fusion.115
  359.4 34.3 %all-to-all-start.3 = ((bf16[1,32,4,1536]{3,2,0,1:T(4,128)(2,1)}), bf16[1,32,4,1536]{3,2,0,1:T(4,128)(2,1)S(1)}, u32[]{:S(2)}, u32[]{:S(2)}) async-start(bf16[1,32,4,1536]{3,2,0,1:T(4,128)(2,1)} %reshape.305), calls=%async_computation.3 | async-start | bytes 786432 | tf_op jit(solution)/shard_map/all_to_all | solution.py:111
  394.0 2.4 fusion.120
  396.5 1.9 convolution_convert_fusion.1
  398.6 3.9 fusion.6
  403.5 3.0 reduce.17
  406.5 1.0 reshape.317
  407.7 7.6 all-to-all-start.4
  417.1 1.1 reshape.311
  421.3 1.1 reshape.309
  422.4 7.0 all-to-all-done.4
  429.4 2.7 reshape.318
  432.1 2.2 bitcast_reduce_fusion.3
  434.6 1.6 fusion.54
  437.1 2.1 fusion.40
  439.4 0.9 reshape.307
  440.3 4.4 all-to-all-start.6
  444.7 81.5 %reduce-scatter.9.cloned.1.call-done = bf16[96,128]{1,0:T(8,128)(2,1)} async-done(((bf16[1536,128]{1,0:T(8,128)(2,1)}), bf16[96,128]{1,0:T(8,128)(2,1)}) %reduce-scatter.9.cloned.1.call-update) | async-done | bytes 24592
  527.2 110.7 %reduce-scatter.7.cloned.1.call-done = bf16[96,128]{1,0:T(8,128)(2,1)} async-done(((bf16[1536,128]{1,0:T(8,128)(2,1)}), bf16[96,128]{1,0:T(8,128)(2,1)}) %reduce-scatter.7.cloned.1.call-update) | async-done | bytes 24592
  638.8 130.2 %all-reduce = (bf16[2,96,64]{1,2,0:T(8,128)(2,1)S(1)}, bf16[2,64,96]{2,1,0:T(8,128)(2,1)S(1)}) all-reduce(bf16[2,96,64]{1,2,0:T(8,128)(2,1)S(1)} %copy.183, bf16[2,64,96]{2,1,0:T(8,128)(2,1)S(1)} %copy.185), channel_id=1, replica_groups=mesh['dp'=16,'seq'=32] {'seq'}, use_global_device_ids=true, to_apply=%region_6.0 | all-reduce | flops 24576 | bytes 98304 | tf_op jit(solution)/shard_map/psum | solution.py:191
  770.2 4.0 fusion.4
  774.7 2.2 fusion.121
  777.0 3.4 fusion.39
  780.4 1.2 copy.179
  782.5 10.7 %all-to-all-start.5 = ((bf16[1,32,4,1536]{3,2,0,1:T(4,128)(2,1)}), bf16[1,32,4,1536]{3,2,0,1:T(4,128)(2,1)}, u32[]{:S(2)}, u32[]{:S(2)}) async-start(bf16[1,32,4,1536]{3,2,0,1:T(4,128)(2,1)} %reshape.306), calls=%async_computation.5 | async-start | bytes 786432 | tf_op jit(solution)/shard_map/all_to_all | solution.py:176
  793.2 3.3 fusion.43
  796.5 2.5 fusion.90
  799.1 3.2 fusion.5
  802.3 4.0 fusion.7
  806.9 0.9 reshape.308
  807.9 7.8 all-to-all-start.7
  815.7 3.2 fusion.42
  818.9 2.3 copy.164
  821.2 2.3 copy.160
  823.4 2.3 copy.156
  825.7 1.5 fusion.12
  827.2 2.0 fusion.17
  829.2 1.8 reshape.302
  832.6 1.8 reshape.303
  836.0 1.8 reshape.304
  (96 shorter events, 28.1 us)
Async XLA Ops:
  7.2 386.6 %copy-start = (bf16[1,1,128,1536]{3,2,1,0:T(8,128)(2,1)S(1)}, bf16[1,1,128,1536]{3,2,1,0:T(8,128)(2,1)}, u32[]{:S(2)}) copy-start(bf16[1,1,128,1536]{3,2,1,0:T(8,128)(2,1)} %param.10) | copy-start | bytes 1179652
  7.2 80.6 %copy-start.4 = (bf16[1,1,128,1536]{3,2,1,0:T(8,128)(2,1)S(1)}, bf16[1,1,128,1536]{3,2,1,0:T(8,128)(2,1)}, u32[]{:S(2)}) copy-start(bf16[1,1,128,1536]{3,2,1,0:T(8,128)(2,1)} %param.7) | copy-start | bytes 1179652
  7.2 81.5 %copy-start.5 = (bf16[1,1,128,1536]{3,2,1,0:T(8,128)(2,1)S(1)}, bf16[1,1,128,1536]{3,2,1,0:T(8,128)(2,1)}, u32[]{:S(2)}) copy-start(bf16[1,1,128,1536]{3,2,1,0:T(8,128)(2,1)} %param.8) | copy-start | bytes 1179652
  7.2 82.4 %copy-start.6 = (bf16[1,1,128,1536]{3,2,1,0:T(8,128)(2,1)S(1)}, bf16[1,1,128,1536]{3,2,1,0:T(8,128)(2,1)}, u32[]{:S(2)}) copy-start(bf16[1,1,128,1536]{3,2,1,0:T(8,128)(2,1)} %param.9) | copy-start | bytes 1179652
  7.2 391.4 %all-gather.2.cloned.1.call-start = ((), (), s32[]{:S(2)}) async-start(), calls=%async_computation.10 | async-start | bytes 10027008 | tf_op jit(solution)/shard_map/all_gather | solution.py:72
  14.2 24.6 %all-to-all-start = ((bf16[32,2,3072]{2,1,0:T(2,128)(2,1)}), bf16[32,2,3072]{2,1,0:T(2,128)(2,1)S(1)}, u32[]{:S(2)}, u32[]{:S(2)}) async-start(bf16[32,2,3072]{2,1,0:T(2,128)(2,1)} %reshape.323), calls=%async_computation | async-start | bytes 786432 | tf_op jit(solution)/shard_map/all_to_all | solution.py:87
  38.7 43.8 %all-to-all-start.1 = ((bf16[32,2,3072]{2,1,0:T(2,128)(2,1)}), bf16[32,2,3072]{2,1,0:T(2,128)(2,1)S(1)}, u32[]{:S(2)}, u32[]{:S(2)}) async-start(bf16[32,2,3072]{2,1,0:T(2,128)(2,1)} %reshape.321), calls=%async_computation.1 | async-start | bytes 786432 | tf_op jit(solution)/shard_map/all_to_all | solution.py:88
  82.6 267.1 %all-to-all-start.2 = ((bf16[32,2,3072]{2,1,0:T(2,128)(2,1)}), bf16[32,2,3072]{2,1,0:T(2,128)(2,1)}, u32[]{:S(2)}, u32[]{:S(2)}) async-start(bf16[32,2,3072]{2,1,0:T(2,128)(2,1)} %reshape.319), calls=%async_computation.2 | async-start | bytes 786432 | tf_op jit(solution)/shard_map/all_to_all | solution.py:89
  342.3 54.2 %copy-start.2 = (bf16[1,64,1536]{2,1,0:T(8,128)(2,1)}, bf16[1,64,1536]{2,1,0:T(8,128)(2,1)S(1)}, u32[]{:S(2)}) copy-start(bf16[1,64,1536]{2,1,0:T(8,128)(2,1)S(1)} %copy.193) | copy-start | bytes 589828
  354.9 47.6 %copy-start.3 = (bf16[1,32,4,12,128]{4,3,2,1,0:T(8,128)(2,1)}, bf16[1,32,4,12,128]{4,3,2,1,0:T(8,128)(2,1)S(1)}, u32[]{:S(2)}) copy-start(bf16[1,32,4,12,128]{4,3,2,1,0:T(8,128)(2,1)S(1)} %reshape.282) | copy-start | bytes 1179652
  357.0 0.9 copy-start.13
  357.0 2.4 copy-start.15
  359.4 48.2 %all-to-all-start.3 = ((bf16[1,32,4,1536]{3,2,0,1:T(4,128)(2,1)}), bf16[1,32,4,1536]{3,2,0,1:T(4,128)(2,1)S(1)}, u32[]{:S(2)}, u32[]{:S(2)}) async-start(bf16[1,32,4,1536]{3,2,0,1:T(4,128)(2,1)} %reshape.305), calls=%async_computation.3 | async-start | bytes 786432 | tf_op jit(solution)/shard_map/all_to_all | solution.py:111
  394.0 8.5 %copy-start.10 = (bf16[128,64]{0,1:T(8,128)(2,1)}, bf16[128,64]{0,1:T(8,128)(2,1)S(1)}, u32[]{:S(2)}) copy-start(bf16[128,64]{0,1:T(8,128)(2,1)S(1)} %convolution_convert_fusion.6) | copy-start | bytes 49156
  396.5 6.1 copy-start.11
  407.7 21.7 %all-to-all-start.4 = ((bf16[32,2,3072]{2,1,0:T(2,128)(2,1)}), bf16[32,2,3072]{2,1,0:T(2,128)(2,1)}, u32[]{:S(2)}, u32[]{:S(2)}) async-start(bf16[32,2,3072]{2,1,0:T(2,128)(2,1)} %reshape.317), calls=%async_computation.4 | async-start | bytes 786432 | tf_op jit(solution)/shard_map/all_to_all | solution.py:160
  415.3 111.0 %reduce-scatter.9.cloned.1.call-start = ((), (), s32[]{:S(2)}) async-start(), calls=%async_computation.12 | async-start | bytes 417792
  415.6 21.5 %copy-start.16 = (f32[4,12,32]{2,1,0:T(8,128)S(1)}, f32[4,12,32]{2,1,0:T(8,128)}, u32[]{:S(2)}) copy-start(f32[4,12,32]{2,1,0:T(8,128)} %copy-done.15) | copy-start | bytes 18436
  415.9 0.6 copy-start.9
  418.3 219.6 %reduce-scatter.7.cloned.1.call-start = ((), (), s32[]{:S(2)}) async-start(), calls=%async_computation.11 | async-start | bytes 417792
  419.2 355.0 %copy-start.1 = (bf16[1,64,1536]{2,1,0:T(8,128)(2,1)}, bf16[1,64,1536]{2,1,0:T(8,128)(2,1)S(1)}, u32[]{:S(2)}) copy-start(bf16[1,64,1536]{2,1,0:T(8,128)(2,1)S(1)} %copy.191) | copy-start | bytes 589828
  436.3 0.9 copy-start.8
  440.3 342.2 %all-to-all-start.6 = ((bf16[1,32,4,1536]{3,2,0,1:T(4,128)(2,1)}), bf16[1,32,4,1536]{3,2,0,1:T(4,128)(2,1)}, u32[]{:S(2)}, u32[]{:S(2)}) async-start(bf16[1,32,4,1536]{3,2,0,1:T(4,128)(2,1)} %reshape.307), calls=%async_computation.6 | async-start | bytes 786432 | tf_op jit(solution)/shard_map/all_to_all | solution.py:177
  444.7 348.5 %copy-start.12 = (f32[12,128]{1,0:T(8,128)S(1)}, f32[12,128]{1,0:T(8,128)}, u32[]{:S(2)}) copy-start(f32[12,128]{1,0:T(8,128)} %copy-done.11) | copy-start | bytes 18436
  770.2 26.3 %copy-start.7 = (bf16[1,1,128,1536]{2,3,1,0:T(8,128)(2,1)S(1)}, bf16[1,1,128,1536]{2,3,1,0:T(8,128)(2,1)}, u32[]{:S(2)}) copy-start(bf16[1,1,128,1536]{2,3,1,0:T(8,128)(2,1)} %copy.126) | copy-start | bytes 1179652
  782.5 25.4 %all-to-all-start.5 = ((bf16[1,32,4,1536]{3,2,0,1:T(4,128)(2,1)}), bf16[1,32,4,1536]{3,2,0,1:T(4,128)(2,1)}, u32[]{:S(2)}, u32[]{:S(2)}) async-start(bf16[1,32,4,1536]{3,2,0,1:T(4,128)(2,1)} %reshape.306), calls=%async_computation.5 | async-start | bytes 786432 | tf_op jit(solution)/shard_map/all_to_all | solution.py:176
  799.1 7.2 copy-start.14
  807.9 28.2 %all-to-all-start.7 = ((bf16[1,32,4,1536]{3,2,0,1:T(4,128)(2,1)}), bf16[1,32,4,1536]{3,2,0,1:T(4,128)(2,1)}, u32[]{:S(2)}, u32[]{:S(2)}) async-start(bf16[1,32,4,1536]{3,2,0,1:T(4,128)(2,1)} %reshape.308), calls=%async_computation.7 | async-start | bytes 786432 | tf_op jit(solution)/shard_map/all_to_all | solution.py:178
Sparse Core Ops, SparseCore 0:
  11.1 267.1 all-gather.1
  420.1 106.0 reduce-scatter.8
  531.4 106.3 reduce-scatter.6
where the time goes:
time: 857 us; the launch traced here: 846 us
  blocking collectives  376 us (44%)
  waiting for transfers between devices  243 us (28%)
  starting transfers between devices  84.6 us (10%)
  local copies, waits for them, and re-layouts  64 us (7%)
  matrix products  47.4 us (6%)
  other arithmetic  15.9 us (2%)
  between operations  14.7 us (2%)
    unnamed x5, waiting for transfers between devices  193 us
    all_gather x1, blocking collectives, local(): lax.all_gather(adapter_down_factor, 'dp', axis=1, tiled=True)  158 us
    psum x1, blocking collectives, local(): lax.psum(local_down.astype(jnp.bfloat16), 'seq').astype(jnp.float32)  130 us
    all_gather x1, blocking collectives, local(): lax.all_gather(adapter_up_factor, 'dp', axis=2, tiled=True)  88.2 us
    all_to_all x1, waiting for transfers between devices, local(): lax.all_to_all(attention_keys, 'seq', split_axis=2, concat_axis=1, tiled=...  34.5 us
    all_to_all x1, starting transfers between devices, local(): lax.all_to_all(from_time(temporal_out), 'seq', split_axis=1, concat_axis=...  34.3 us
    unnamed x66, local copies, waits for them, and re-layouts  31.7 us
  transfers between devices with their start and end apart: 11, of which 6 were waited for; matrix products, arithmetic and copies ran while one was open for 14% of the time, Pallas kernels for 0%

commit v1 on v0

v1 whole, which is shorter than its diff:
```python
import functools

import jax
import jax.numpy as jnp
from jax import lax
from jax.experimental import pallas as pl
from jax.experimental.pallas import tpu as pltpu
from jax.sharding import Mesh
from jax.sharding import PartitionSpec as P

HDIM = 128
HEADS = 12
FEATURES = 1536
ROWS = 128
RANK = 64
GAIN = 2.0
SCALE = HDIM ** (-0.5)

AXES = ("x", "zh", "y", "zl", "c")
SIZES = (4, 4, 4, 4, 2)
SEQ = ("y", "zl", "c")
F32 = jnp.float32
BF16 = jnp.bfloat16
VMEM_LIMIT = 40 * 1024 * 1024


def nn(a, b):
    return lax.dot_general(a, b, (((1,), (0,)), ((), ())), preferred_element_type=F32)


def nt(a, b):
    return lax.dot_general(a, b, (((1,), (1,)), ((), ())), preferred_element_type=F32)


def tn(a, b):
    return lax.dot_general(a, b, (((0,), (0,)), ((), ())), preferred_element_type=F32)


def call(kernel, out_shape, in_specs, scratch, flops, nbytes):
    vmem = pl.BlockSpec(memory_space=pltpu.VMEM)
    return pl.pallas_call(
        kernel,
        out_shape=out_shape,
        in_specs=in_specs,
        out_specs=jax.tree.map(lambda _: vmem, out_shape),
        scratch_shapes=scratch,
        compiler_params=pltpu.CompilerParams(vmem_limit_bytes=VMEM_LIMIT),
        cost_estimate=pl.CostEstimate(flops=flops, bytes_accessed=nbytes, transcendentals=0),
    )


VM = pl.BlockSpec(memory_space=pltpu.VMEM)
ANY = pl.BlockSpec(memory_space=pl.ANY)
SM = pl.BlockSpec(memory_space=pltpu.SMEM)


def same_patch():
    rows = lax.broadcasted_iota(jnp.int32, (ROWS, ROWS), 0)
    columns = lax.broadcasted_iota(jnp.int32, (ROWS, ROWS), 1)
    return (rows % 4) == (columns % 4)


def forward_heads(q, k, v, probs_ref, out_ref, mask):
    for h in range(HEADS):
        scores = nt(q(h), k(h)) * SCALE
        if mask is not None:
            scores = jnp.where(mask, scores, -1e30)
        scores = jnp.exp(scores - jnp.max(scores, axis=-1, keepdims=True))
        probs = scores / jnp.sum(scores, axis=-1, keepdims=True)
        probs_ref[h] = probs
        out_ref[:, h * HDIM : (h + 1) * HDIM] = nn(probs.astype(BF16), v(h)).astype(BF16)


def backward_head(q, k, v, probs, up):
    value_term = tn(probs.astype(BF16), up)
    prob_term = nt(up, v)
    centre = jnp.sum(probs * prob_term, axis=-1, keepdims=True)
    score_term = (probs * (prob_term - centre) * SCALE).astype(BF16)
    return nn(score_term, k), tn(score_term, q), value_term


def head(ref, base=0):
    return lambda h: ref[:, base + h * HDIM : base + (h + 1) * HDIM]


def spatial_forward(q, k, v, probs_ref, out_ref):
    forward_heads(head(q), head(k), head(v), probs_ref, out_ref, None)


def temporal_forward(t, probs_ref, out_ref):
    forward_heads(head(t), head(t, FEATURES), head(t, 2 * FEATURES), probs_ref, out_ref, same_patch())


def adapters_kernel(place, pieces, o0, o1, cot, t, du_ref, rank0, rank1, grads, held, sems):
    x = place[0]
    copies = []
    for k in range(4):
        at = pl.multiple_of(((x - k) & 3) * 4, 4)
        for b in range(2):
            for half in range(2):
                copies.append(
                    pltpu.make_async_copy(
                        pieces.at[k, b, :, :, half * 128 : half * 128 + 128],
                        held.at[b, pl.ds(at, 4), half],
                        sems.at[len(copies)],
                    )
                )
    for copy in copies:
        copy.start()
    for copy in copies:
        copy.wait()
    lanes = lax.broadcasted_iota(jnp.int32, (ROWS, 128), 1) < RANK
    wide = lax.broadcasted_iota(jnp.int32, (FEATURES, 128), 1) < RANK
    for b in range(2):
        du = held[b].reshape(FEATURES, 128)
        du_ref[b] = du
        out = (o0, o1)[b][...]
        cotangent = cot[...] if b == 0 else t[:, 3 * FEATURES :]
        low = nn(out, du)
        back = nn(cotangent, du)
        low_back = jnp.where(lanes, low, back).astype(BF16)
        (rank0, rank1)[b][...] = low_back
        from_out = tn(out, low_back)
        from_cotangent = tn(cotangent, low_back)
        grads[b] = (GAIN * jnp.where(wide, from_cotangent, from_out)).astype(BF16)


def load_weight(place, mine, other, weight, sems):
    x, y, c = place[0], place[1], place[2]
    copies = []
    for side, arrays in ((c, mine), (1 - c, other)):
        for m in range(4):
            for k in range(4):
                row = jnp.where(side == 0, x - k, x - m) & 3
                column = jnp.where(side == 0, y - m, y - k) & 3
                copies.append(
                    pltpu.make_async_copy(
                        arrays[m].at[k],
                        weight.at[pl.ds(row * 4, 4), side, :, pl.ds(pl.multiple_of(column * 384, 128), 384)],
                        sems.at[len(copies)],
                    )
                )
    for copy in copies:
        copy.start()
    for copy in copies:
        copy.wait()


BLOCK = 256


def project(out, cotangent, low_back, du, weight, blended_ref, up_ref):
    zero = jnp.zeros((), BF16)

    def step(i, _):
        at = pl.multiple_of(i * BLOCK, BLOCK)
        here = du[pl.ds(at, BLOCK), :]
        low_back_value = low_back[...]
        is_down = lax.broadcasted_iota(jnp.int32, (BLOCK, 128), 1) < RANK
        down = jnp.where(is_down, here, zero)
        upper = jnp.where(is_down, zero, here)
        swapped = jnp.concatenate([low_back_value[:, RANK:], low_back_value[:, :RANK]], axis=1)
        rows = weight[pl.ds(at, BLOCK), :]
        columns = weight[:, pl.ds(at, BLOCK)]
        up = nt(cotangent(), rows) + GAIN * nt(swapped, down)
        blended = nn(out(), columns) + GAIN * nt(swapped, upper)
        up_ref[:, pl.ds(at, BLOCK)] = up.astype(up_ref.dtype)
        blended_ref[:, pl.ds(at, BLOCK)] = blended.astype(blended_ref.dtype)
        return 0

    lax.fori_loop(0, FEATURES // BLOCK, step, 0)


def temporal_project(place, m0, m1, m2, m3, p0, p1, p2, p3, o1, t, rank1, du, blended_ref, up_ref, weight, sems):
    load_weight(place, (m0, m1, m2, m3), (p0, p1, p2, p3), weight, sems)
    whole = weight.reshape(FEATURES, FEATURES)
    project(lambda: o1[...], lambda: t[:, 3 * FEATURES :], rank1, du.at[1], whole, blended_ref, up_ref)


def temporal_backward(t, probs, up, sent):
    for h in range(HEADS):
        terms = backward_head(
            head(t)(h), head(t, FEATURES)(h), head(t, 2 * FEATURES)(h), probs[h], head(up)(h)
        )
        for i, term in enumerate(terms):
            at = i * FEATURES + h * HDIM
            sent[:, at : at + HDIM] = term.astype(BF16)


def spatial_rest(
    place, m0, m1, m2, m3, p0, p1, p2, p3, o0, cot, rank0, du, q, k, v, probs, blended_ref, dq, dk, dv, up, weight, sems
):
    load_weight(place, (m0, m1, m2, m3), (p0, p1, p2, p3), weight, sems)
    whole = weight.reshape(FEATURES, FEATURES)
    project(lambda: o0[...], lambda: cot[...], rank0, du.at[0], whole, blended_ref, up)
    for h in range(HEADS):
        terms = backward_head(head(q)(h), head(k)(h), head(v)(h), probs[h], head(up)(h))
        for ref, term in zip((dq, dk, dv), terms):
            ref[:, h * HDIM : (h + 1) * HDIM] = term


def shape(dims, dtype=BF16):
    return jax.ShapeDtypeStruct(dims, dtype)


def index_of(x, zh, y, zl, c):
    return (((x * 4 + zh) * 4 + y) * 4 + zl) * 2 + c


def everywhere():
    for x in range(4):
        for zh in range(4):
            for y in range(4):
                for zl in range(4):
                    for c in range(2):
                        yield x, zh, y, zl, c


def permute(value, move):
    pairs = []
    for at in everywhere():
        to = move(*at)
        if to is not None:
            pairs.append((index_of(*at), index_of(*to)))
    return lax.ppermute(value, AXES, pairs)


def along_zh(step):
    return lambda x, zh, y, zl, c: (x, (zh + step) % 4, y, zl, c)


def along_first(step):
    return lambda x, zh, y, zl, c: ((x + step) % 4, zh, y, zl, c) if c == 0 else (x, zh, (y + step) % 4, zl, c)


def along_second(step):
    return lambda x, zh, y, zl, c: (x, zh, (y + step) % 4, zl, c) if c == 0 else ((x + step) % 4, zh, y, zl, c)


def other_core(x, zh, y, zl, c):
    return (x, zh, y, zl, 1 - c)


def first_to_second(x, zh, y, zl, c):
    return (x, zh, y, zl, 1) if c == 0 else None


def exchange(value, axes):
    return lax.all_to_all(value, axes, split_axis=0, concat_axis=0, tiled=True)


def local(q, k, v, cot, weight, down, up):
    out_dims = q.shape
    x, zh, y, c = (lax.axis_index(n) for n in ("x", "zh", "y", "c"))
    place = jnp.stack([x, y, c, zh]).astype(jnp.int32)
    q, k, v, cot = (a.reshape(ROWS, FEATURES) for a in (q, k, v, cot))

    piece = lax.dynamic_slice(weight, (0, c * 48, y * 384), (2, 48, 384))
    adapters = jnp.concatenate([down, jnp.swapaxes(up, 1, 2)], axis=2)
    adapters = jnp.concatenate([adapters[:, :48], adapters[:, 48:]], axis=2)
    first = jnp.concatenate([piece, adapters], axis=2)
    arrived = [permute(first, along_zh(s)) for s in (1, 2, 3)]
    turned = jnp.stack([arrived[2], arrived[1], arrived[0], first] * 2, axis=1)
    by_zh = lax.dynamic_slice(turned, (0, 3 - zh, 0, 0), (2, 4, 48, 640))

    t = exchange(jnp.concatenate([q, k, v, cot], axis=1).reshape(32, 4, 4 * FEATURES), SEQ)
    t = t.reshape(ROWS, 4 * FEATURES)

    probs0, o0 = call(
        spatial_forward, (shape((HEADS, ROWS, ROWS), F32), shape((ROWS, FEATURES))), [VM] * 3, [], 10**8, 10**7
    )(q, k, v)

    stage = [by_zh] + [permute(by_zh, along_first(s)) for s in (1, 2, 3)]
    adapter_pieces = jnp.stack([s[..., 384:] for s in stage])
    from_first = permute(adapter_pieces, first_to_second)
    adapter_pieces = jnp.where(c == 0, adapter_pieces, from_first)

    def rest_of_gather(b):
        held = jnp.stack([s[b, :, :, :384] for s in stage])
        mine = [held] + [permute(held, along_second(s)) for s in (1, 2, 3)]
        other = [permute(m, other_core) for m in mine]
        return mine + other

    weight1 = rest_of_gather(1)
    weight0 = rest_of_gather(0)

    probs1, o1 = call(
        temporal_forward, (shape((HEADS, ROWS, ROWS), F32), shape((ROWS, FEATURES))), [VM], [], 10**8, 10**7
    )(t)

    du, rank0, rank1, grads = call(
        adapters_kernel,
        (shape((2, FEATURES, 128)), shape((ROWS, 128)), shape((ROWS, 128)), shape((2, FEATURES, 128))),
        [SM, ANY] + [VM] * 4,
        [pltpu.VMEM((2, 16, 2, 48, 128), BF16), pltpu.SemaphoreType.DMA((16,))],
        10**8,
        10**7,
    )(place, adapter_pieces, o0, o1, cot, t)

    weight_scratch = [pltpu.VMEM((16, 2, 48, FEATURES), BF16), pltpu.SemaphoreType.DMA((32,))]
    blended1, up1 = call(
        temporal_project,
        (shape((ROWS, FEATURES)), shape((ROWS, FEATURES))),
        [SM] + [ANY] * 8 + [VM] * 4,
        weight_scratch,
        12 * 10**8,
        10**7,
    )(place, *weight1, o1, t, rank1, du)
    blended1 = exchange(blended1.reshape(32, 4, FEATURES), SEQ).reshape(ROWS, FEATURES)

    sent = call(temporal_backward, shape((ROWS, 3 * FEATURES)), [VM] * 3, [], 2 * 10**8, 10**7)(t, probs1, up1)
    returned = exchange(sent.reshape(32, 4, 3 * FEATURES), SEQ).reshape(ROWS, 3 * FEATURES)

    blended0, dq, dk, dv = call(
        spatial_rest,
        (shape((ROWS, FEATURES), F32),) * 4,
        [SM] + [ANY] * 8 + [VM] * 8,
        [pltpu.VMEM((ROWS, FEATURES), BF16)] + weight_scratch,
        14 * 10**8,
        2 * 10**7,
    )(place, *weight0, o0, cot, rank0, du, q, k, v, probs0)

    summed = grads.reshape(2, 16, 4, 24, 128).transpose(2, 0, 1, 3, 4).reshape(8, 16 * 24, 128)
    summed = exchange(summed, ("y", "c")).astype(F32).sum(0).astype(BF16)
    summed = exchange(summed.reshape(4, 96, 128), "x").astype(F32).sum(0).astype(BF16)
    summed = jnp.broadcast_to(summed.reshape(4, 1, 24, 128), (4, 4, 24, 128)).reshape(16, 24, 128)
    summed = exchange(summed, ("zh", "zl")).astype(F32).sum(0).astype(BF16)
    summed = exchange(jnp.broadcast_to(summed[None], (8, 24, 128)), ("y", "c"))
    summed = summed.reshape(4, 2, 24, 128).transpose(1, 0, 2, 3).reshape(2, 96, 128).astype(F32)
    grad_up = jnp.swapaxes(summed[:, :, :RANK], 1, 2)
    grad_down = summed[:, :, RANK:]

    def combine(mine, arrived):
        return (mine + arrived.astype(F32)).astype(BF16).reshape(out_dims)

    return (
        combine(blended0, blended1),
        combine(dq, returned[:, :FEATURES]),
        combine(dk, returned[:, FEATURES : 2 * FEATURES]),
        combine(dv, returned[:, 2 * FEATURES :]),
        grad_down,
        grad_up,
    )


def solution(mesh):
    fine = Mesh(mesh.devices.reshape(SIZES), AXES)
    dp, seq = ("x", "zh"), SEQ
    tokens = P(dp, seq, None, None)
    rows, columns = P(None, dp, None), P(None, None, dp)
    return jax.shard_map(
        local,
        mesh=fine,
        in_specs=(tokens,) * 4 + (rows, rows, columns),
        out_specs=(tokens,) * 4 + (rows, columns),
        check_vma=False,
    )
```

time: 857 us -> 279 us (0.33); the launches traced: 846 us -> 277 us
  blocking collectives: 376 us -> 36.8 us
  waiting for transfers between devices: 243 us -> 51.8 us
  matrix products: 47.4 us -> 0 us
  local copies, waits for them, and re-layouts: 64 us -> 33.8 us
  Pallas kernels: 0 us -> 28.9 us
  starting transfers between devices: 84.6 us -> 113 us
  between operations: 14.7 us -> 1.43 us
    all_gather x2 -> x0, blocking collectives: 246 us -> none  [the longest x1 158 us: local(): lax.all_gather(adapter_down_factor, 'dp', axis=1, tiled=True)]
    unnamed x5 -> x0, waiting for transfers between devices: 193 us -> none
    psum x1 -> x0, blocking collectives: 130 us -> none  [local(): lax.psum(local_down.astype(jnp.bfloat16), 'seq').astype(jnp.float32)]
    ppermute x0 -> x21, starting transfers between devices: none -> 77.1 us  [permute(): return lax.ppermute(value, AXES, pairs)]
    all_to_all x8 -> x5, starting transfers between devices: 84.1 us -> 36.1 us  [exchange(): return lax.all_to_all(value, axes, split_axis=0, concat_axis=0, tiled=True)]
    dot_general x26 -> x0, matrix products: 42.8 us -> none  [the longest x6 9.01 us: reduce_trailing(): lax.dot_general(left, right, (((1,), (1,)), ((), ())), preferred_element_...]
    ppermute x0 -> x21, waiting for transfers between devices: none -> 41 us  [permute(): return lax.ppermute(value, AXES, pairs)]
    all_to_all x8 -> x5, waiting for transfers between devices: 50.2 us -> 10.9 us  [exchange(): return lax.all_to_all(value, axes, split_axis=0, concat_axis=0, tiled=True)]
  transfers between devices with their start and end apart: 11 -> 26, of which waited for: 6 -> 7; matrix products, arithmetic and copies ran while one was open for 14% -> 10% of each run, Pallas kernels for 0% -> 10%
where the time goes in v1:
time: 279 us; the launch traced here: 277 us
  starting transfers between devices  113 us (41%)
  waiting for transfers between devices  51.8 us (19%)
  blocking collectives  36.8 us (13%)
  local copies, waits for them, and re-layouts  33.8 us (12%)
  Pallas kernels  28.9 us (10%)
  other arithmetic  10.8 us (4%)
    ppermute x21, starting transfers between devices, permute(): return lax.ppermute(value, AXES, pairs)  77.1 us
    ppermute x21, waiting for transfers between devices, permute(): return lax.ppermute(value, AXES, pairs)  41 us
    all_to_all x2, blocking collectives, exchange(): return lax.all_to_all(value, axes, split_axis=0, concat_axis=0, tiled=True)  36.8 us
    all_to_all x5, starting transfers between devices, exchange(): return lax.all_to_all(value, axes, split_axis=0, concat_axis=0, tiled=True)  36.1 us
    unnamed x81, local copies, waits for them, and re-layouts  10.9 us
    all_to_all x5, waiting for transfers between devices, exchange(): return lax.all_to_all(value, axes, split_axis=0, concat_axis=0, tiled=True)  10.9 us
    pallas_call x1, Pallas kernels, local(): call(spatial_rest, (shape((ROWS, FEATURES), F32),) * 4, [SM] + [ANY] * 8...  8.59 us
    pallas_call x1, Pallas kernels, local(): call(temporal_project, (shape((ROWS, FEATURES)), shape((ROWS, FEATURES)))...  6.72 us
  transfers between devices with their start and end apart: 26, of which 7 were waited for; matrix products, arithmetic and copies ran while one was open for 10% of the time, Pallas kernels for 10%

profile of v1, /device:TPU:1, one launch (start us, length us, event | category | flops | bytes accessed | tf_op | source)
XLA Modules:
  0.0 276.8 jit_solution(10579916884059827243)
XLA Ops:
  0.7 1.2 concatenate.20
  1.9 1.1 concatenate.21
  3.2 1.8 pad_maximum_fusion
  5.0 11.3 %all-to-all-start = ((bf16[32,4,6144]{2,1,0:T(4,128)(2,1)}), bf16[32,4,6144]{2,1,0:T(4,128)(2,1)}, u32[]{:S(2)}, u32[]{:S(2)}) async-start(bf16[32,4,6144]{2,1,0:T(4,128)(2,1)} %pad_maximum_fusion), calls=%async_computation | async-start | bytes 3145728 | tf_op jit(solution)/shard_map/all_to_all | solution.py:249
  16.7 9.0 %collective-permute-start = (bf16[2,48,640]{2,1,0:T(8,128)(2,1)S(1)}, bf16[2,48,640]{2,1,0:T(8,128)(2,1)S(1)}, u32[]{:S(2)}, u32[]{:S(2)}) collective-permute-start(bf16[2,48,640]{2,1,0:T(8,128)(2,1)S(1)} %fusion.4), channel_id=1, source_target_pairs={{0,96},{1,97},{2,98},{3,99},{4,100},{5,101},{6,102},{7,103},{8,104... | collective-permute-start | bytes 368648 | tf_op jit(solution)/shard_map/ppermute | solution.py:225
  25.7 6.1 %collective-permute-start.1 = (bf16[2,48,640]{2,1,0:T(8,128)(2,1)S(1)}, bf16[2,48,640]{2,1,0:T(8,128)(2,1)S(1)}, u32[]{:S(2)}, u32[]{:S(2)}) collective-permute-start(bf16[2,48,640]{2,1,0:T(8,128)(2,1)S(1)} %fusion.4), channel_id=1, source_target_pairs={{0,64},{1,65},{2,66},{3,67},{4,68},{5,69},{6,70},{7,71},{8,72},{9,... | collective-permute-start | bytes 368648 | tf_op jit(solution)/shard_map/ppermute | solution.py:225
  31.8 6.1 %collective-permute-start.2 = (bf16[2,48,640]{2,1,0:T(8,128)(2,1)S(1)}, bf16[2,48,640]{2,1,0:T(8,128)(2,1)S(1)}, u32[]{:S(2)}, u32[]{:S(2)}) collective-permute-start(bf16[2,48,640]{2,1,0:T(8,128)(2,1)S(1)} %fusion.4), channel_id=1, source_target_pairs={{0,32},{1,33},{2,34},{3,35},{4,36},{5,37},{6,38},{7,39},{8,40},{9,... | collective-permute-start | bytes 368648 | tf_op jit(solution)/shard_map/ppermute | solution.py:225
  37.9 27.8 %collective-permute-done.1 = bf16[2,48,640]{2,1,0:T(8,128)(2,1)S(1)} collective-permute-done((bf16[2,48,640]{2,1,0:T(8,128)(2,1)S(1)}, bf16[2,48,640]{2,1,0:T(8,128)(2,1)S(1)}, u32[]{:S(2)}, u32[]{:S(2)}) %collective-permute-start.1) | collective-permute-done | bytes 122912 | tf_op jit(solution)/shard_map/ppermute | solution.py:225
  65.7 2.3 collective-permute-done.2
  68.2 1.0 copy-done.32
  70.0 4.3 %collective-permute-start.5 = (bf16[2,4,48,640]{3,2,1,0:T(8,128)(2,1)}, bf16[2,4,48,640]{3,2,1,0:T(8,128)(2,1)}, u32[]{:S(2)}, u32[]{:S(2)}) collective-permute-start(bf16[2,4,48,640]{3,2,1,0:T(8,128)(2,1)} %constant_dynamic-slice_fusion.2), channel_id=1, source_target_pairs={{0,384},{1,25},{2,386},{3,27},{4,388},{5,29},{6,390},{7,31},{8,392... | collective-permute-start | bytes 1474568 | tf_op jit(solution)/shard_map/ppermute | solution.py:225
  74.3 2.5 collective-permute-start.4
  76.9 4.0 %shard_map.118 = (f32[12,128,128]{2,1,0:T(8,128)S(1)}, bf16[128,1536]{1,0:T(8,128)(2,1)S(1)}) custom-call(bf16[128,1536]{1,0:T(8,128)(2,1)S(1)} %bitcast.65, bf16[128,1536]{1,0:T(8,128)(2,1)S(1)} %bitcast.67, bf16[128,1536]{1,0:T(8,128)(2,1)S(1)} %bitcast.69), custom_call_target="tpu_custom_call" | custom-call | flops 100000000 | bytes 10000000 | tf_op jit(solution)/shard_map/pallas_call | solution.py:269
  80.8 2.5 collective-permute-start.3
  83.3 1.7 constant_dynamic-slice_fusion
  85.0 0.9 dynamic-slice_bitcast_fusion
  86.0 0.9 slice_bitcast_fusion
  86.9 0.9 slice_bitcast_fusion.1
  87.9 4.3 %collective-permute-done.3 = bf16[2,4,48,640]{3,2,1,0:T(8,128)(2,1)S(1)} collective-permute-done((bf16[2,4,48,640]{3,2,1,0:T(8,128)(2,1)}, bf16[2,4,48,640]{3,2,1,0:T(8,128)(2,1)S(1)}, u32[]{:S(2)}, u32[]{:S(2)}) %collective-permute-start.3) | collective-permute-done | bytes 491552 | tf_op jit(solution)/shard_map/ppermute | solution.py:225
  92.3 1.3 collective-permute-start.13
  94.3 1.7 fusion.7
  95.9 1.7 fusion.8
  97.6 0.9 pad_maximum_fusion.3.m0
  98.5 2.8 %collective-permute-start.14 = (bf16[4,4,48,384]{3,2,1,0:T(8,128)(2,1)}, bf16[4,4,48,384]{3,2,1,0:T(8,128)(2,1)}, u32[]{:S(2)}, u32[]{:S(2)}) collective-permute-start(bf16[4,4,48,384]{3,2,1,0:T(8,128)(2,1)} %pad_maximum_fusion.3.m0), channel_id=1, source_target_pairs={{0,8},{1,129},{2,10},{3,131},{4,12},{5,133},{6,14},{7,135},{8,16},... | collective-permute-start | bytes 1769480 | tf_op jit(solution)/shard_map/ppermute | solution.py:225
  101.4 4.4 %collective-permute-start.15 = (bf16[4,4,48,384]{3,2,1,0:T(8,128)(2,1)}, bf16[4,4,48,384]{3,2,1,0:T(8,128)(2,1)}, u32[]{:S(2)}, u32[]{:S(2)}) collective-permute-start(bf16[4,4,48,384]{3,2,1,0:T(8,128)(2,1)} %pad_maximum_fusion.3.m0), channel_id=1, source_target_pairs={{0,16},{1,257},{2,18},{3,259},{4,20},{5,261},{6,22},{7,263},{8,24}... | collective-permute-start | bytes 1769480 | tf_op jit(solution)/shard_map/ppermute | solution.py:225
  105.8 3.1 %collective-permute-start.16 = (bf16[4,4,48,384]{3,2,1,0:T(8,128)(2,1)}, bf16[4,4,48,384]{3,2,1,0:T(8,128)(2,1)}, u32[]{:S(2)}, u32[]{:S(2)}) collective-permute-start(bf16[4,4,48,384]{3,2,1,0:T(8,128)(2,1)} %pad_maximum_fusion.3.m0), channel_id=1, source_target_pairs={{0,24},{1,385},{2,26},{3,387},{4,28},{5,389},{6,30},{7,391},{8,0},... | collective-permute-start | bytes 1769480 | tf_op jit(solution)/shard_map/ppermute | solution.py:225
  108.8 1.1 broadcast_select_fusion.pieces
  109.9 2.7 reshape.85.t
  112.6 4.0 %shard_map.119 = (f32[12,128,128]{2,1,0:T(8,128)S(1)}, bf16[128,1536]{1,0:T(8,128)(2,1)S(1)}) custom-call(bf16[128,6144]{1,0:T(8,128)(2,1)S(1)} %reshape.85.t), custom_call_target="tpu_custom_call" | custom-call | flops 100000000 | bytes 10000000 | tf_op jit(solution)/shard_map/pallas_call | solution.py:287
  117.5 2.1 shard_map.120
  119.7 1.1 copy.41
  120.8 7.7 %all-to-all-start.3 = ((bf16[8,384,128]{2,1,0:T(8,128)(2,1)}), bf16[8,384,128]{2,1,0:T(8,128)(2,1)}, u32[]{:S(2)}, u32[]{:S(2)}) async-start(bf16[8,384,128]{2,1,0:T(8,128)(2,1)} %bitcast.74), calls=%async_computation.3 | async-start | bytes 1572864 | tf_op jit(solution)/shard_map/all_to_all | solution.py:249
  128.4 2.0 collective-permute-start.17
  130.5 2.3 collective-permute-start.18
  132.8 2.1 collective-permute-start.19
  134.9 2.3 collective-permute-start.20
  137.2 3.7 %all-to-all-done.3 = bf16[8,384,128]{2,1,0:T(8,128)(2,1)} async-done(((bf16[8,384,128]{2,1,0:T(8,128)(2,1)}), bf16[8,384,128]{2,1,0:T(8,128)(2,1)}, u32[]{:S(2)}, u32[]{:S(2)}) %all-to-all-start.3) | async-done | bytes 786464 | tf_op jit(solution)/shard_map/all_to_all | solution.py:249
  140.9 1.2 reduce_sum.36
  142.1 7.7 %all_to_all.35 = bf16[4,96,128]{2,1,0:T(8,128)(2,1)} all-to-all(bf16[4,96,128]{2,1,0:T(8,128)(2,1)S(1)} %bitcast.78), channel_id=1, replica_groups=mesh['x'=4,'zh'=4,'y'=4,'zl'=4,'c'=2] {'x'}, dimensions={0} | all-to-all | bytes 196608 | tf_op jit(solution)/shard_map/all_to_all | solution.py:249
  150.7 29.1 %all_to_all.36 = bf16[16,24,128]{2,1,0:T(8,128)(2,1)S(1)} all-to-all(bf16[16,24,128]{2,1,0:T(8,128)(2,1)S(1)} %bitcast.79), channel_id=1, replica_groups=mesh['x'=4,'zh'=4,'y'=4,'zl'=4,'c'=2] {'zh','zl'}, dimensions={0} | all-to-all | bytes 196608 | tf_op jit(solution)/shard_map/all_to_all | solution.py:249
  180.5 6.8 %all-to-all-start.6 = ((bf16[8,24,128]{2,1,0:T(8,128)(2,1)}), bf16[8,24,128]{2,1,0:T(8,128)(2,1)S(1)}, u32[]{:S(2)}, u32[]{:S(2)}) async-start(bf16[8,24,128]{2,1,0:T(8,128)(2,1)} %broadcast_in_dim.15), calls=%async_computation.6 | async-start | bytes 98304 | tf_op jit(solution)/shard_map/all_to_all | solution.py:249
  187.3 6.7 %shard_map.122 = (bf16[128,1536]{1,0:T(8,128)(2,1)S(1)}, bf16[128,1536]{1,0:T(8,128)(2,1)S(1)}) custom-call(s32[4]{0:T(128)S(1)} %pad_add_fusion.place, bf16[4,4,48,384]{3,2,1,0:T(8,128)(2,1)} %pad_maximum_fusion.3.m0, bf16[4,4,48,384]{3,2,1,0:T(8,128)(2,1)} %collective-permute-done.14.m1, bf16[4,4,48,384]{3,2,1,0:T(8,128)(2,1)} %collective-permute-done.15.m2, ...), custom_call_target="tpu_custom_call" | custom-call | flops 1200000000 | bytes 10000000 | tf_op jit(solution)/shard_map/pallas_call | solution.py:301
  195.6 1.8 reshape.86
  197.4 5.9 %all-to-all-start.1 = ((bf16[32,4,1536]{2,1,0:T(4,128)(2,1)}), bf16[32,4,1536]{2,1,0:T(4,128)(2,1)}, u32[]{:S(2)}, u32[]{:S(2)}) async-start(bf16[32,4,1536]{2,1,0:T(4,128)(2,1)} %reshape.86), calls=%async_computation.1 | async-start | bytes 786432 | tf_op jit(solution)/shard_map/all_to_all | solution.py:249
  203.3 1.1 copy-done.28
  204.5 1.0 copy-done.31
  205.5 3.6 %shard_map.123 = bf16[128,4608]{1,0:T(8,128)(2,1)S(1)} custom-call(bf16[128,6144]{1,0:T(8,128)(2,1)S(1)} %reshape.85.t, f32[12,128,128]{2,1,0:T(8,128)S(1)} %copy-done.28, bf16[128,1536]{1,0:T(8,128)(2,1)S(1)} %copy-done.31), custom_call_target="tpu_custom_call" | custom-call | flops 200000000 | bytes 10000000 | tf_op jit(solution)/shard_map/pallas_call | solution.py:311
  209.0 1.2 reshape.88
  210.3 7.2 %all-to-all-done.1 = bf16[32,4,1536]{2,1,0:T(4,128)(2,1)} async-done(((bf16[32,4,1536]{2,1,0:T(4,128)(2,1)}), bf16[32,4,1536]{2,1,0:T(4,128)(2,1)}, u32[]{:S(2)}, u32[]{:S(2)}) %all-to-all-start.1) | async-done | bytes 393248 | tf_op jit(solution)/shard_map/all_to_all | solution.py:249
  217.4 4.5 %all-to-all-start.2 = ((bf16[32,4,4608]{2,1,0:T(4,128)(2,1)}), bf16[32,4,4608]{2,1,0:T(4,128)(2,1)}, u32[]{:S(2)}, u32[]{:S(2)}) async-start(bf16[32,4,4608]{2,1,0:T(4,128)(2,1)} %reshape.88), calls=%async_computation.2 | async-start | bytes 2359296 | tf_op jit(solution)/shard_map/all_to_all | solution.py:249
  221.9 1.3 pad_maximum_fusion.2.m0
  223.2 2.2 collective-permute-start.6
  225.4 3.7 %collective-permute-start.7 = (bf16[4,4,48,384]{3,2,1,0:T(8,128)(2,1)S(1)}, bf16[4,4,48,384]{3,2,1,0:T(8,128)(2,1)S(1)}, u32[]{:S(2)}, u32[]{:S(2)}) collective-permute-start(bf16[4,4,48,384]{3,2,1,0:T(8,128)(2,1)S(1)} %pad_maximum_fusion.2.m0), channel_id=1, source_target_pairs={{0,16},{1,257},{2,18},{3,259},{4,20},{5,261},{6,22},{7,263},{8,24}... | collective-permute-start | bytes 1769480 | tf_op jit(solution)/shard_map/ppermute | solution.py:225
  229.1 2.6 collective-permute-start.8
  231.7 5.3 %collective-permute-start.9 = (bf16[4,4,48,384]{3,2,1,0:T(8,128)(2,1)S(1)}, bf16[4,4,48,384]{3,2,1,0:T(8,128)(2,1)S(1)}, u32[]{:S(2)}, u32[]{:S(2)}) collective-permute-start(bf16[4,4,48,384]{3,2,1,0:T(8,128)(2,1)S(1)} %pad_maximum_fusion.2.m0), channel_id=1, source_target_pairs={{0,1},{1,0},{2,3},{3,2},{4,5},{5,4},{6,7},{7,6},{8,9},{9,8},{10,11... | collective-permute-start | bytes 1769480 | tf_op jit(solution)/shard_map/ppermute | solution.py:225
  237.0 4.7 %collective-permute-done.6.m1 = bf16[4,4,48,384]{3,2,1,0:T(8,128)(2,1)S(1)} collective-permute-done((bf16[4,4,48,384]{3,2,1,0:T(8,128)(2,1)S(1)}, bf16[4,4,48,384]{3,2,1,0:T(8,128)(2,1)S(1)}, u32[]{:S(2)}, u32[]{:S(2)}) %collective-permute-start.6) | collective-permute-done | bytes 589856 | tf_op jit(solution)/shard_map/ppermute | solution.py:225
  241.7 2.2 collective-permute-start.10
  243.9 8.5 %collective-permute-start.11 = (bf16[4,4,48,384]{3,2,1,0:T(8,128)(2,1)S(1)}, bf16[4,4,48,384]{3,2,1,0:T(8,128)(2,1)S(1)}, u32[]{:S(2)}, u32[]{:S(2)}) collective-permute-start(bf16[4,4,48,384]{3,2,1,0:T(8,128)(2,1)S(1)} %collective-permute-done.7.m2), channel_id=1, source_target_pairs={{0,1},{1,0},{2,3},{3,2},{4,5},{5,4},{6,7},{7,6},{8,9},{9,8},{10,11... | collective-permute-start | bytes 1769480 | tf_op jit(solution)/shard_map/ppermute | solution.py:225
  252.5 1.9 collective-permute-start.12
  254.4 1.9 collective-permute-done.12.p3
  256.4 8.6 %shard_map.121 = (f32[128,1536]{1,0:T(8,128)S(1)}, f32[128,1536]{1,0:T(8,128)S(1)}, f32[128,1536]{1,0:T(8,128)S(1)}, f32[128,1536]{1,0:T(8,128)S(1)}) custom-call(s32[4]{0:T(128)S(1)} %pad_add_fusion.place, bf16[4,4,48,384]{3,2,1,0:T(8,128)(2,1)S(1)} %pad_maximum_fusion.2.m0, bf16[4,4,48,384]{3,2,1,0:T(8,128)(2,1)S(1)} %collective-permute-done.6.m1, ...), custom_call_target="tpu_custom_call" | custom-call | flops 1400000000 | bytes 20000000 | tf_op jit(solution)/shard_map/pallas_call | solution.py:314
  270.1 1.0 reshape.97
  272.0 2.4 reshape.89
  274.5 2.4 fusion.3
  (116 shorter events, 12.5 us)
Async XLA Ops:
  0.6 16.0 %copy-start = (bf16[2,96,1536]{2,1,0:T(8,128)(2,1)S(1)}, bf16[2,96,1536]{2,1,0:T(8,128)(2,1)}, u32[]{:S(2)}) copy-start(bf16[2,96,1536]{2,1,0:T(8,128)(2,1)} %param.11) | copy-start | bytes 1769476
  0.6 2.3 copy-start.5
  0.7 2.4 copy-start.7
  5.0 11.3 %copy-start.33 = (bf16[2,64,96]{2,1,0:T(8,128)(2,1)S(1)}, bf16[2,64,96]{2,1,0:T(8,128)(2,1)}, u32[]{:S(2)}) copy-start(bf16[2,64,96]{2,1,0:T(8,128)(2,1)} %param.13) | copy-start | bytes 73732
  5.0 11.4 %copy-start.34 = (bf16[2,96,64]{1,2,0:T(8,128)(2,1)S(1)}, bf16[2,96,64]{1,2,0:T(8,128)(2,1)}, u32[]{:S(2)}) copy-start(bf16[2,96,64]{1,2,0:T(8,128)(2,1)} %param.12) | copy-start | bytes 73732
  5.0 105.0 %all-to-all-start = ((bf16[32,4,6144]{2,1,0:T(4,128)(2,1)}), bf16[32,4,6144]{2,1,0:T(4,128)(2,1)}, u32[]{:S(2)}, u32[]{:S(2)}) async-start(bf16[32,4,6144]{2,1,0:T(4,128)(2,1)} %pad_maximum_fusion), calls=%async_computation | async-start | bytes 3145728 | tf_op jit(solution)/shard_map/all_to_all | solution.py:249
  16.7 60.1 %copy-start.1 = (bf16[1,1,128,1536]{3,2,1,0:T(8,128)(2,1)S(1)}, bf16[1,1,128,1536]{3,2,1,0:T(8,128)(2,1)}, u32[]{:S(2)}) copy-start(bf16[1,1,128,1536]{3,2,1,0:T(8,128)(2,1)} %param.7) | copy-start | bytes 1179652
  16.7 60.1 %copy-start.3 = (bf16[1,1,128,1536]{3,2,1,0:T(8,128)(2,1)S(1)}, bf16[1,1,128,1536]{3,2,1,0:T(8,128)(2,1)}, u32[]{:S(2)}) copy-start(bf16[1,1,128,1536]{3,2,1,0:T(8,128)(2,1)} %param.8) | copy-start | bytes 1179652
  16.7 21.2 %collective-permute-start = (bf16[2,48,640]{2,1,0:T(8,128)(2,1)S(1)}, bf16[2,48,640]{2,1,0:T(8,128)(2,1)S(1)}, u32[]{:S(2)}, u32[]{:S(2)}) collective-permute-start(bf16[2,48,640]{2,1,0:T(8,128)(2,1)S(1)} %fusion.4), channel_id=1, source_target_pairs={{0,96},{1,97},{2,98},{3,99},{4,100},{5,101},{6,102},{7,103},{8,104... | collective-permute-start | bytes 368648 | tf_op jit(solution)/shard_map/ppermute | solution.py:225
  25.7 40.0 %collective-permute-start.1 = (bf16[2,48,640]{2,1,0:T(8,128)(2,1)S(1)}, bf16[2,48,640]{2,1,0:T(8,128)(2,1)S(1)}, u32[]{:S(2)}, u32[]{:S(2)}) collective-permute-start(bf16[2,48,640]{2,1,0:T(8,128)(2,1)S(1)} %fusion.4), channel_id=1, source_target_pairs={{0,64},{1,65},{2,66},{3,67},{4,68},{5,69},{6,70},{7,71},{8,72},{9,... | collective-permute-start | bytes 368648 | tf_op jit(solution)/shard_map/ppermute | solution.py:225
  31.8 36.2 %collective-permute-start.2 = (bf16[2,48,640]{2,1,0:T(8,128)(2,1)S(1)}, bf16[2,48,640]{2,1,0:T(8,128)(2,1)S(1)}, u32[]{:S(2)}, u32[]{:S(2)}) collective-permute-start(bf16[2,48,640]{2,1,0:T(8,128)(2,1)S(1)} %fusion.4), channel_id=1, source_target_pairs={{0,32},{1,33},{2,34},{3,35},{4,36},{5,37},{6,38},{7,39},{8,40},{9,... | collective-permute-start | bytes 368648 | tf_op jit(solution)/shard_map/ppermute | solution.py:225
  68.1 1.0 copy-start.32
  70.0 16.0 %collective-permute-start.5 = (bf16[2,4,48,640]{3,2,1,0:T(8,128)(2,1)}, bf16[2,4,48,640]{3,2,1,0:T(8,128)(2,1)}, u32[]{:S(2)}, u32[]{:S(2)}) collective-permute-start(bf16[2,4,48,640]{3,2,1,0:T(8,128)(2,1)} %constant_dynamic-slice_fusion.2), channel_id=1, source_target_pairs={{0,384},{1,25},{2,386},{3,27},{4,388},{5,29},{6,390},{7,31},{8,392... | collective-permute-start | bytes 1474568 | tf_op jit(solution)/shard_map/ppermute | solution.py:225
  74.3 12.6 %collective-permute-start.4 = (bf16[2,4,48,640]{3,2,1,0:T(8,128)(2,1)}, bf16[2,4,48,640]{3,2,1,0:T(8,128)(2,1)}, u32[]{:S(2)}, u32[]{:S(2)}) collective-permute-start(bf16[2,4,48,640]{3,2,1,0:T(8,128)(2,1)} %constant_dynamic-slice_fusion.2), channel_id=1, source_target_pairs={{0,256},{1,17},{2,258},{3,19},{4,260},{5,21},{6,262},{7,23},{8,264... | collective-permute-start | bytes 1474568 | tf_op jit(solution)/shard_map/ppermute | solution.py:225
  80.8 11.4 %copy-start.12 = (bf16[128,1536]{1,0:T(8,128)(2,1)}, bf16[128,1536]{1,0:T(8,128)(2,1)S(1)}, u32[]{:S(2)}) copy-start(bf16[128,1536]{1,0:T(8,128)(2,1)S(1)} %get-tuple-element.20.o0) | copy-start | bytes 1179652
  80.8 11.4 %copy-start.17 = (f32[12,128,128]{2,1,0:T(8,128)}, f32[12,128,128]{2,1,0:T(8,128)S(1)}, u32[]{:S(2)}) copy-start(f32[12,128,128]{2,1,0:T(8,128)S(1)} %get-tuple-element.24.probs) | copy-start | bytes 2359300
  80.8 11.3 %collective-permute-start.3 = (bf16[2,4,48,640]{3,2,1,0:T(8,128)(2,1)}, bf16[2,4,48,640]{3,2,1,0:T(8,128)(2,1)S(1)}, u32[]{:S(2)}, u32[]{:S(2)}) collective-permute-start(bf16[2,4,48,640]{3,2,1,0:T(8,128)(2,1)} %constant_dynamic-slice_fusion.2), channel_id=1, source_target_pairs={{0,128},{1,9},{2,130},{3,11},{4,132},{5,13},{6,134},{7,15},{8,136}... | collective-permute-start | bytes 1474568 | tf_op jit(solution)/shard_map/ppermute | solution.py:225
  92.3 16.6 %collective-permute-start.13 = (bf16[4,2,4,48,256]{4,3,2,1,0:T(8,128)(2,1)S(1)}, bf16[4,2,4,48,256]{4,3,2,1,0:T(8,128)(2,1)S(1)}, u32[]{:S(2)}, u32[]{:S(2)}) collective-permute-start(bf16[4,2,4,48,256]{4,3,2,1,0:T(8,128)(2,1)S(1)} %pad_maximum_fusion.1), channel_id=1, source_target_pairs={{0,1},{2,3},{4,5},{6,7},{8,9},{10,11},{12,13},{14,15},{16,17},{18,... | collective-permute-start | bytes 2359304 | tf_op jit(solution)/shard_map/ppermute | solution.py:225
  98.5 32.0 %collective-permute-start.14 = (bf16[4,4,48,384]{3,2,1,0:T(8,128)(2,1)}, bf16[4,4,48,384]{3,2,1,0:T(8,128)(2,1)}, u32[]{:S(2)}, u32[]{:S(2)}) collective-permute-start(bf16[4,4,48,384]{3,2,1,0:T(8,128)(2,1)} %pad_maximum_fusion.3.m0), channel_id=1, source_target_pairs={{0,8},{1,129},{2,10},{3,131},{4,12},{5,133},{6,14},{7,135},{8,16},... | collective-permute-start | bytes 1769480 | tf_op jit(solution)/shard_map/ppermute | solution.py:225
  101.4 31.4 %collective-permute-start.15 = (bf16[4,4,48,384]{3,2,1,0:T(8,128)(2,1)}, bf16[4,4,48,384]{3,2,1,0:T(8,128)(2,1)}, u32[]{:S(2)}, u32[]{:S(2)}) collective-permute-start(bf16[4,4,48,384]{3,2,1,0:T(8,128)(2,1)} %pad_maximum_fusion.3.m0), channel_id=1, source_target_pairs={{0,16},{1,257},{2,18},{3,259},{4,20},{5,261},{6,22},{7,263},{8,24}... | collective-permute-start | bytes 1769480 | tf_op jit(solution)/shard_map/ppermute | solution.py:225
  105.8 29.1 %collective-permute-start.16 = (bf16[4,4,48,384]{3,2,1,0:T(8,128)(2,1)}, bf16[4,4,48,384]{3,2,1,0:T(8,128)(2,1)}, u32[]{:S(2)}, u32[]{:S(2)}) collective-permute-start(bf16[4,4,48,384]{3,2,1,0:T(8,128)(2,1)} %pad_maximum_fusion.3.m0), channel_id=1, source_target_pairs={{0,24},{1,385},{2,26},{3,387},{4,28},{5,389},{6,30},{7,391},{8,0},... | collective-permute-start | bytes 1769480 | tf_op jit(solution)/shard_map/ppermute | solution.py:225
  112.6 4.9 %copy-start.11 = (bf16[4,2,4,48,256]{4,3,2,1,0:T(8,128)(2,1)S(1)}, bf16[4,2,4,48,256]{4,3,2,1,0:T(8,128)(2,1)}, u32[]{:S(2)}) copy-start(bf16[4,2,4,48,256]{4,3,2,1,0:T(8,128)(2,1)} %broadcast_select_fusion.pieces) | copy-start | bytes 2359300
  112.6 4.9 %copy-start.13 = (bf16[128,1536]{1,0:T(8,128)(2,1)S(1)}, bf16[128,1536]{1,0:T(8,128)(2,1)}, u32[]{:S(2)}) copy-start(bf16[128,1536]{1,0:T(8,128)(2,1)} %copy-done.12) | copy-start | bytes 1179652
  116.6 0.9 copy-start.27
  117.5 2.2 copy-start.15
  119.7 67.6 %copy-start.9 = (bf16[2,1536,128]{2,1,0:T(8,128)(2,1)}, bf16[2,1536,128]{2,1,0:T(8,128)(2,1)S(1)}, u32[]{:S(2)}) copy-start(bf16[2,1536,128]{2,1,0:T(8,128)(2,1)S(1)} %get-tuple-element.23.du) | copy-start | bytes 2359300
  120.8 66.6 %copy-start.16 = (bf16[128,1536]{1,0:T(8,128)(2,1)S(1)}, bf16[128,1536]{1,0:T(8,128)(2,1)}, u32[]{:S(2)}) copy-start(bf16[128,1536]{1,0:T(8,128)(2,1)} %copy-done.15) | copy-start | bytes 1179652
  120.8 20.1 %all-to-all-start.3 = ((bf16[8,384,128]{2,1,0:T(8,128)(2,1)}), bf16[8,384,128]{2,1,0:T(8,128)(2,1)}, u32[]{:S(2)}, u32[]{:S(2)}) async-start(bf16[8,384,128]{2,1,0:T(8,128)(2,1)} %bitcast.74), calls=%async_computation.3 | async-start | bytes 1572864 | tf_op jit(solution)/shard_map/all_to_all | solution.py:249
  128.4 58.8 %collective-permute-start.17 = (bf16[4,4,48,384]{3,2,1,0:T(8,128)(2,1)}, bf16[4,4,48,384]{3,2,1,0:T(8,128)(2,1)}, u32[]{:S(2)}, u32[]{:S(2)}) collective-permute-start(bf16[4,4,48,384]{3,2,1,0:T(8,128)(2,1)} %pad_maximum_fusion.3.m0), channel_id=1, source_target_pairs={{0,1},{1,0},{2,3},{3,2},{4,5},{5,4},{6,7},{7,6},{8,9},{9,8},{10,11... | collective-permute-start | bytes 1769480 | tf_op jit(solution)/shard_map/ppermute | solution.py:225
  130.5 56.8 %collective-permute-start.18 = (bf16[4,4,48,384]{3,2,1,0:T(8,128)(2,1)}, bf16[4,4,48,384]{3,2,1,0:T(8,128)(2,1)}, u32[]{:S(2)}, u32[]{:S(2)}) collective-permute-start(bf16[4,4,48,384]{3,2,1,0:T(8,128)(2,1)} %collective-permute-done.14.m1), channel_id=1, source_target_pairs={{0,1},{1,0},{2,3},{3,2},{4,5},{5,4},{6,7},{7,6},{8,9},{9,8},{10,11... | collective-permute-start | bytes 1769480 | tf_op jit(solution)/shard_map/ppermute | solution.py:225
  132.8 54.5 %collective-permute-start.19 = (bf16[4,4,48,384]{3,2,1,0:T(8,128)(2,1)}, bf16[4,4,48,384]{3,2,1,0:T(8,128)(2,1)}, u32[]{:S(2)}, u32[]{:S(2)}) collective-permute-start(bf16[4,4,48,384]{3,2,1,0:T(8,128)(2,1)} %collective-permute-done.15.m2), channel_id=1, source_target_pairs={{0,1},{1,0},{2,3},{3,2},{4,5},{5,4},{6,7},{7,6},{8,9},{9,8},{10,11... | collective-permute-start | bytes 1769480 | tf_op jit(solution)/shard_map/ppermute | solution.py:225
  134.9 52.4 %collective-permute-start.20 = (bf16[4,4,48,384]{3,2,1,0:T(8,128)(2,1)}, bf16[4,4,48,384]{3,2,1,0:T(8,128)(2,1)}, u32[]{:S(2)}, u32[]{:S(2)}) collective-permute-start(bf16[4,4,48,384]{3,2,1,0:T(8,128)(2,1)} %collective-permute-done.16.m3), channel_id=1, source_target_pairs={{0,1},{1,0},{2,3},{3,2},{4,5},{5,4},{6,7},{7,6},{8,9},{9,8},{10,11... | collective-permute-start | bytes 1769480 | tf_op jit(solution)/shard_map/ppermute | solution.py:225
  180.5 16.9 %all-to-all-start.6 = ((bf16[8,24,128]{2,1,0:T(8,128)(2,1)}), bf16[8,24,128]{2,1,0:T(8,128)(2,1)S(1)}, u32[]{:S(2)}, u32[]{:S(2)}) async-start(bf16[8,24,128]{2,1,0:T(8,128)(2,1)} %broadcast_in_dim.15), calls=%async_computation.6 | async-start | bytes 98304 | tf_op jit(solution)/shard_map/all_to_all | solution.py:249
  194.1 0.7 copy-start.29
  194.8 0.7 copy-start.30
  197.4 20.0 %all-to-all-start.1 = ((bf16[32,4,1536]{2,1,0:T(4,128)(2,1)}), bf16[32,4,1536]{2,1,0:T(4,128)(2,1)}, u32[]{:S(2)}, u32[]{:S(2)}) async-start(bf16[32,4,1536]{2,1,0:T(4,128)(2,1)} %reshape.86), calls=%async_computation.1 | async-start | bytes 786432 | tf_op jit(solution)/shard_map/all_to_all | solution.py:249
  203.3 1.1 copy-start.28
  204.5 1.0 copy-start.31
  210.2 46.2 %copy-start.2 = (bf16[1,1,128,1536]{3,2,1,0:T(8,128)(2,1)S(1)}, bf16[1,1,128,1536]{3,2,1,0:T(8,128)(2,1)}, u32[]{:S(2)}) copy-start(bf16[1,1,128,1536]{3,2,1,0:T(8,128)(2,1)} %param.7) | copy-start | bytes 1179652
  210.2 46.2 %copy-start.4 = (bf16[1,1,128,1536]{3,2,1,0:T(8,128)(2,1)S(1)}, bf16[1,1,128,1536]{3,2,1,0:T(8,128)(2,1)}, u32[]{:S(2)}) copy-start(bf16[1,1,128,1536]{3,2,1,0:T(8,128)(2,1)} %param.8) | copy-start | bytes 1179652
  210.2 46.2 %copy-start.6 = (bf16[1,1,128,1536]{3,2,1,0:T(8,128)(2,1)S(1)}, bf16[1,1,128,1536]{3,2,1,0:T(8,128)(2,1)}, u32[]{:S(2)}) copy-start(bf16[1,1,128,1536]{3,2,1,0:T(8,128)(2,1)} %param.9) | copy-start | bytes 1179652
  210.2 46.2 %copy-start.8 = (bf16[1,1,128,1536]{3,2,1,0:T(8,128)(2,1)S(1)}, bf16[1,1,128,1536]{3,2,1,0:T(8,128)(2,1)}, u32[]{:S(2)}) copy-start(bf16[1,1,128,1536]{3,2,1,0:T(8,128)(2,1)} %param.10) | copy-start | bytes 1179652
  210.2 46.2 %copy-start.10 = (bf16[2,1536,128]{2,1,0:T(8,128)(2,1)S(1)}, bf16[2,1536,128]{2,1,0:T(8,128)(2,1)}, u32[]{:S(2)}) copy-start(bf16[2,1536,128]{2,1,0:T(8,128)(2,1)} %copy-done.9) | copy-start | bytes 2359300
  210.2 46.2 %copy-start.14 = (bf16[128,1536]{1,0:T(8,128)(2,1)S(1)}, bf16[128,1536]{1,0:T(8,128)(2,1)}, u32[]{:S(2)}) copy-start(bf16[128,1536]{1,0:T(8,128)(2,1)} %copy-done.12) | copy-start | bytes 1179652
  217.4 54.6 %all-to-all-start.2 = ((bf16[32,4,4608]{2,1,0:T(4,128)(2,1)}), bf16[32,4,4608]{2,1,0:T(4,128)(2,1)}, u32[]{:S(2)}, u32[]{:S(2)}) async-start(bf16[32,4,4608]{2,1,0:T(4,128)(2,1)} %reshape.88), calls=%async_computation.2 | async-start | bytes 2359296 | tf_op jit(solution)/shard_map/all_to_all | solution.py:249
  221.9 34.5 %copy-start.18 = (f32[12,128,128]{2,1,0:T(8,128)S(1)}, f32[12,128,128]{2,1,0:T(8,128)}, u32[]{:S(2)}) copy-start(f32[12,128,128]{2,1,0:T(8,128)} %copy-done.17) | copy-start | bytes 2359300
  223.2 18.6 %collective-permute-start.6 = (bf16[4,4,48,384]{3,2,1,0:T(8,128)(2,1)S(1)}, bf16[4,4,48,384]{3,2,1,0:T(8,128)(2,1)S(1)}, u32[]{:S(2)}, u32[]{:S(2)}) collective-permute-start(bf16[4,4,48,384]{3,2,1,0:T(8,128)(2,1)S(1)} %pad_maximum_fusion.2.m0), channel_id=1, source_target_pairs={{0,8},{1,129},{2,10},{3,131},{4,12},{5,133},{6,14},{7,135},{8,16},... | collective-permute-start | bytes 1769480 | tf_op jit(solution)/shard_map/ppermute | solution.py:225
  225.4 18.6 %collective-permute-start.7 = (bf16[4,4,48,384]{3,2,1,0:T(8,128)(2,1)S(1)}, bf16[4,4,48,384]{3,2,1,0:T(8,128)(2,1)S(1)}, u32[]{:S(2)}, u32[]{:S(2)}) collective-permute-start(bf16[4,4,48,384]{3,2,1,0:T(8,128)(2,1)S(1)} %pad_maximum_fusion.2.m0), channel_id=1, source_target_pairs={{0,16},{1,257},{2,18},{3,259},{4,20},{5,261},{6,22},{7,263},{8,24}... | collective-permute-start | bytes 1769480 | tf_op jit(solution)/shard_map/ppermute | solution.py:225
  229.1 23.4 %collective-permute-start.8 = (bf16[4,4,48,384]{3,2,1,0:T(8,128)(2,1)S(1)}, bf16[4,4,48,384]{3,2,1,0:T(8,128)(2,1)S(1)}, u32[]{:S(2)}, u32[]{:S(2)}) collective-permute-start(bf16[4,4,48,384]{3,2,1,0:T(8,128)(2,1)S(1)} %pad_maximum_fusion.2.m0), channel_id=1, source_target_pairs={{0,24},{1,385},{2,26},{3,387},{4,28},{5,389},{6,30},{7,391},{8,0},... | collective-permute-start | bytes 1769480 | tf_op jit(solution)/shard_map/ppermute | solution.py:225
  231.7 22.7 %collective-permute-start.9 = (bf16[4,4,48,384]{3,2,1,0:T(8,128)(2,1)S(1)}, bf16[4,4,48,384]{3,2,1,0:T(8,128)(2,1)S(1)}, u32[]{:S(2)}, u32[]{:S(2)}) collective-permute-start(bf16[4,4,48,384]{3,2,1,0:T(8,128)(2,1)S(1)} %pad_maximum_fusion.2.m0), channel_id=1, source_target_pairs={{0,1},{1,0},{2,3},{3,2},{4,5},{5,4},{6,7},{7,6},{8,9},{9,8},{10,11... | collective-permute-start | bytes 1769480 | tf_op jit(solution)/shard_map/ppermute | solution.py:225
  241.7 12.7 %collective-permute-start.10 = (bf16[4,4,48,384]{3,2,1,0:T(8,128)(2,1)S(1)}, bf16[4,4,48,384]{3,2,1,0:T(8,128)(2,1)S(1)}, u32[]{:S(2)}, u32[]{:S(2)}) collective-permute-start(bf16[4,4,48,384]{3,2,1,0:T(8,128)(2,1)S(1)} %collective-permute-done.6.m1), channel_id=1, source_target_pairs={{0,1},{1,0},{2,3},{3,2},{4,5},{5,4},{6,7},{7,6},{8,9},{9,8},{10,11... | collective-permute-start | bytes 1769480 | tf_op jit(solution)/shard_map/ppermute | solution.py:225
  243.9 10.5 %collective-permute-start.11 = (bf16[4,4,48,384]{3,2,1,0:T(8,128)(2,1)S(1)}, bf16[4,4,48,384]{3,2,1,0:T(8,128)(2,1)S(1)}, u32[]{:S(2)}, u32[]{:S(2)}) collective-permute-start(bf16[4,4,48,384]{3,2,1,0:T(8,128)(2,1)S(1)} %collective-permute-done.7.m2), channel_id=1, source_target_pairs={{0,1},{1,0},{2,3},{3,2},{4,5},{5,4},{6,7},{7,6},{8,9},{9,8},{10,11... | collective-permute-start | bytes 1769480 | tf_op jit(solution)/shard_map/ppermute | solution.py:225
  252.5 3.9 %collective-permute-start.12 = (bf16[4,4,48,384]{3,2,1,0:T(8,128)(2,1)S(1)}, bf16[4,4,48,384]{3,2,1,0:T(8,128)(2,1)S(1)}, u32[]{:S(2)}, u32[]{:S(2)}) collective-permute-start(bf16[4,4,48,384]{3,2,1,0:T(8,128)(2,1)S(1)} %collective-permute-done.8.m3), channel_id=1, source_target_pairs={{0,1},{1,0},{2,3},{3,2},{4,5},{5,4},{6,7},{7,6},{8,9},{9,8},{10,11... | collective-permute-start | bytes 1769480 | tf_op jit(solution)/shard_map/ppermute | solution.py:225
  265.0 0.9 copy-start.19
  265.9 0.9 copy-start.21
  266.8 0.9 copy-start.23
  267.7 0.9 copy-start.25
  268.6 2.6 copy-start.26
  272.0 2.4 copy-start.20
  272.0 2.4 copy-start.22
  272.0 2.4 copy-start.24

commit v2 on v1

v2 whole, which is shorter than its diff:
```python
import jax
import jax.numpy as jnp
from jax import lax
from jax.experimental import pallas as pl
from jax.experimental.pallas import tpu as pltpu
from jax.sharding import Mesh
from jax.sharding import PartitionSpec as P

HDIM = 128
HEADS = 12
FEATURES = 1536
ROWS = 128
BOTH = 2 * ROWS
RANK = 64
GAIN = 2.0
SCALE = HDIM ** (-0.5)
WIDE = 4 * FEATURES
COT = 3 * FEATURES
SLICE = 384
BLOCK = 256

AXES = ("x", "zh", "y", "zl", "c")
SIZES = (4, 4, 4, 4, 2)
F32 = jnp.float32
BF16 = jnp.bfloat16

VM = pl.BlockSpec(memory_space=pltpu.VMEM)
ANY = pl.BlockSpec(memory_space=pl.ANY)
SM = pl.BlockSpec(memory_space=pltpu.SMEM)


def nn(a, b):
    return lax.dot_general(a, b, (((1,), (0,)), ((), ())), preferred_element_type=F32)


def nt(a, b):
    return lax.dot_general(a, b, (((1,), (1,)), ((), ())), preferred_element_type=F32)


def tn(a, b):
    return lax.dot_general(a, b, (((0,), (0,)), ((), ())), preferred_element_type=F32)


def shape(dims, dtype=BF16):
    return jax.ShapeDtypeStruct(dims, dtype)


def call(kernel, out_shape, in_specs, out_specs, scratch, flops, nbytes, vmem_mib=8):
    return pl.pallas_call(
        kernel,
        out_shape=out_shape,
        in_specs=in_specs,
        out_specs=out_specs,
        scratch_shapes=scratch,
        compiler_params=pltpu.CompilerParams(vmem_limit_bytes=vmem_mib * 2**20),
        cost_estimate=pl.CostEstimate(flops=flops, bytes_accessed=nbytes, transcendentals=0),
    )


def head(ref, h, base=0):
    return ref[:, base + h * HDIM : base + (h + 1) * HDIM]


def place_zh(place, s0, s1, s2, s3, held):
    for k, ref in enumerate((s0, s1, s2, s3)):
        held[(place[2] - k) & 3] = ref[...]


def wait_all(copies):
    for copy in copies:
        copy.wait()


def start_rows(place, own_time, own_space, got, rows, sems):
    @pl.when(place[3] == 0)
    def _():
        pltpu.make_async_copy(own_time, rows.at[0:ROWS], sems.at[0]).start()

    @pl.when(place[3] != 0)
    def _():
        pltpu.make_async_copy(own_space, rows.at[0:ROWS], sems.at[0]).start()

    copies = [
        pltpu.make_async_copy(own_time, rows.at[0:ROWS], sems.at[0]),
        pltpu.make_async_copy(got, rows.at[ROWS:BOTH], sems.at[1]),
    ]
    copies[1].start()
    return copies


def forward(place, own_time, own_space, got, probs_out, out, rows, probs, sems):
    wait_all(start_rows(place, own_time, own_space, got, rows, sems))
    time = place[3] == 0
    across = lax.broadcasted_iota(jnp.int32, (BOTH, BOTH), 0)
    along = lax.broadcasted_iota(jnp.int32, (BOTH, BOTH), 1)
    mask = jnp.where(time, across & 7, across >> 7) == jnp.where(time, along & 7, along >> 7)
    copies = []
    for h in range(HEADS):
        scores = nt(head(rows, h), head(rows, h, FEATURES)) * SCALE
        scores = jnp.where(mask, scores, -1e30)
        scores = jnp.exp(scores - jnp.max(scores, axis=-1, keepdims=True))
        value = scores / jnp.sum(scores, axis=-1, keepdims=True)
        probs[h] = value
        copies.append(pltpu.make_async_copy(probs.at[h], probs_out.at[h], sems.at[2 + h]))
        copies[-1].start()
        out[:, h * HDIM : (h + 1) * HDIM] = nn(value.astype(BF16), head(rows, h, 2 * FEATURES)).astype(BF16)
    wait_all(copies)


def adapters_kernel(place, m0, m1, m2, m3, own_time, own_space, got, out, du_out, low_back_out, grads, rows, du, sems):
    arrays = (m0, m1, m2, m3)
    x, y, c = place[0], place[1], place[3]

    def pieces(first_is_x):
        made = []
        for across in range(4):
            for down in (0, 2):
                second, first = (down, across) if first_is_x else (across, down)
                half = ((y - down) & 3) >> 1
                for part in range(3):
                    made.append(
                        pltpu.make_async_copy(
                            arrays[second].at[first, :, 96:112, part * 128 : part * 128 + 128],
                            du.at[pl.ds(((x - across) & 3) * 4, 4), pl.ds(pl.multiple_of(48 * half + 16 * part, 16), 16)],
                            sems.at[2 + len(made)],
                        )
                    )
        return made

    @pl.when(c == 0)
    def _():
        for copy in pieces(True):
            copy.start()

    @pl.when(c != 0)
    def _():
        for copy in pieces(False):
            copy.start()

    others = start_rows(
        place, own_time.at[:, COT:], own_space.at[:, COT:], got.at[:, COT:], rows, sems
    )
    wait_all(others)
    wait_all(pieces(True))
    factors = du[...].reshape(FEATURES, 128)
    du_out[...] = factors
    left = lax.broadcasted_iota(jnp.int32, (BOTH, 128), 1) < RANK
    low_back = jnp.where(left, nn(out[...], factors), nn(rows[...], factors)).astype(BF16)
    low_back_out[...] = low_back
    left = lax.broadcasted_iota(jnp.int32, (FEATURES, 128), 1) < RANK
    grads[...] = (GAIN * jnp.where(left, tn(rows[...], low_back), tn(out[...], low_back))).astype(BF16)


def rest(
    place, m0, m1, m2, m3, own_time, own_space, got, probs_in, out, low_back, du,
    here_out, there_out, weight, rows, probs, up, sent, sems, weight_sems,
):
    arrays = (m0, m1, m2, m3)
    x, y, c = place[0], place[1], place[3]
    copies = []
    for second in range(4):
        for first in range(4):
            row = jnp.where(c == 0, x - first, x - second) & 3
            column = jnp.where(c == 0, y - second, y - first) & 3
            copies.append(
                pltpu.make_async_copy(
                    arrays[second].at[first, :, 0:96, :],
                    weight.at[pl.ds(row * 4, 4), :, pl.ds(pl.multiple_of(column * SLICE, 128), SLICE)],
                    weight_sems.at[len(copies)],
                )
            )
            copies[-1].start()
    copies += start_rows(place, own_time, own_space, got, rows, sems)
    probs_copy = pltpu.make_async_copy(probs_in, probs, sems.at[2])
    probs_copy.start()
    wait_all(copies)
    whole = weight.reshape(FEATURES, FEATURES)
    zero = jnp.zeros((), BF16)

    def project(i, _):
        at = pl.multiple_of(i * BLOCK, BLOCK)
        factors = du[pl.ds(at, BLOCK), :]
        is_down = lax.broadcasted_iota(jnp.int32, (BLOCK, 128), 1) < RANK
        down = jnp.where(is_down, factors, zero)
        upper = jnp.where(is_down, zero, factors)
        swapped = jnp.concatenate([low_back[:, RANK:], low_back[:, :RANK]], axis=1)
        upstream = nt(rows[:, COT:], whole[pl.ds(at, BLOCK), :]) + GAIN * nt(swapped, down)
        up[:, pl.ds(at, BLOCK)] = upstream.astype(BF16)
        blended = nn(out[...], whole[:, pl.ds(at, BLOCK)]) + GAIN * nt(swapped, upper)
        sent[:, pl.ds(pl.multiple_of(COT + at, BLOCK), BLOCK)] = blended.astype(BF16)
        return 0

    lax.fori_loop(0, FEATURES // BLOCK, project, 0)
    probs_copy.wait()
    for h in range(HEADS):
        value = probs[h]
        upstream = head(up, h)
        value_term = tn(value.astype(BF16), upstream)
        prob_term = nt(upstream, head(rows, h, 2 * FEATURES))
        centre = jnp.sum(value * prob_term, axis=-1, keepdims=True)
        score_term = (value * (prob_term - centre) * SCALE).astype(BF16)
        terms = (nn(score_term, head(rows, h, FEATURES)), tn(score_term, head(rows, h)), value_term)
        for i, term in enumerate(terms):
            at = i * FEATURES + h * HDIM
            sent[:, at : at + HDIM] = term.astype(BF16)
    copies = [
        pltpu.make_async_copy(sent.at[0:ROWS], here_out, sems.at[3]),
        pltpu.make_async_copy(sent.at[ROWS:BOTH], there_out, sems.at[4]),
    ]
    for copy in copies:
        copy.start()
    wait_all(copies)


def index_of(x, zh, y, zl, c):
    return (((x * 4 + zh) * 4 + y) * 4 + zl) * 2 + c


def permute(value, move):
    pairs = []
    for x in range(4):
        for zh in range(4):
            for y in range(4):
                for zl in range(4):
                    for c in range(2):
                        pairs.append((index_of(x, zh, y, zl, c), index_of(*move(x, zh, y, zl, c))))
    return lax.ppermute(value, AXES, pairs)


def along_zh(step):
    return lambda x, zh, y, zl, c: (x, (zh + step) % 4, y, zl, c)


def along_first(step):
    return lambda x, zh, y, zl, c: ((x + step) % 4, zh, y, zl, c) if c == 0 else (x, zh, (y + step) % 4, zl, c)


def along_second(step):
    return lambda x, zh, y, zl, c: (x, zh, (y + step) % 4, zl, c) if c == 0 else ((x + step) % 4, zh, y, zl, c)


def other_core(x, zh, y, zl, c):
    return (x, zh, y, zl, 1 - c)


def exchange(value, axes):
    return lax.all_to_all(value, axes, split_axis=0, concat_axis=0, tiled=True)


def local(q, k, v, cot, weight, down, up):
    out_dims = q.shape
    x, zh, y, c = (lax.axis_index(n) for n in ("x", "zh", "y", "c"))
    place = jnp.stack([x, y, zh, c]).astype(jnp.int32)
    space = jnp.concatenate([a.reshape(ROWS, FEATURES) for a in (q, k, v, cot)], axis=1)

    branch = 1 - c
    piece = lax.dynamic_slice(weight, (branch, 0, y * SLICE), (1, 96, SLICE))[0]
    adapters = jnp.concatenate([down, jnp.swapaxes(up, 1, 2)], axis=2)
    adapters = lax.dynamic_slice(adapters, (branch, (y // 2) * 48, 0), (1, 48, 128))
    adapters = adapters.reshape(3, 16, 128).transpose(1, 0, 2).reshape(16, SLICE)
    first = jnp.concatenate([piece, adapters], axis=0)
    arrived = [permute(first, along_zh(s)) for s in (1, 2, 3)]
    held = call(place_zh, shape((4, 112, SLICE)), [SM] + [VM] * 4, VM, [], 10**6, 10**6)(place, first, *arrived)

    space, held = lax.optimization_barrier((space, held))
    time = exchange(space.reshape(16, 8, WIDE), ("y", "zl")).reshape(ROWS, WIDE)
    held = jnp.stack([held] + [permute(held, along_first(s)) for s in (1, 2, 3)])
    gathered = [held] + [permute(held, along_second(s)) for s in (1, 2, 3)]
    got = permute(jnp.where(c == 0, space, time), other_core)

    probs, out = call(
        forward,
        (shape((HEADS, BOTH, BOTH), F32), shape((BOTH, FEATURES))),
        [SM] + [ANY] * 3,
        (ANY, VM),
        [pltpu.VMEM((BOTH, WIDE), BF16), pltpu.VMEM((HEADS, BOTH, BOTH), F32), pltpu.SemaphoreType.DMA((14,))],
        4 * 10**8,
        10**7,
        16,
    )(place, time, space, got)

    du, low_back, grads = call(
        adapters_kernel,
        (shape((FEATURES, 128)), shape((BOTH, 128)), shape((FEATURES, 128))),
        [SM] + [ANY] * 7 + [VM],
        (VM, VM, VM),
        [pltpu.VMEM((BOTH, FEATURES), BF16), pltpu.VMEM((16, 96, 128), BF16), pltpu.SemaphoreType.DMA((26,))],
        4 * 10**8,
        5 * 10**6,
        16,
    )(place, *gathered, time, space, got, out)

    here, there = call(
        rest,
        (shape((ROWS, WIDE)), shape((ROWS, WIDE))),
        [SM] + [ANY] * 8 + [VM] * 3,
        (ANY, ANY),
        [
            pltpu.VMEM((16, 96, FEATURES), BF16),
            pltpu.VMEM((BOTH, WIDE), BF16),
            pltpu.VMEM((HEADS, BOTH, BOTH), F32),
            pltpu.VMEM((BOTH, FEATURES), BF16),
            pltpu.VMEM((BOTH, WIDE), BF16),
            pltpu.SemaphoreType.DMA((5,)),
            pltpu.SemaphoreType.DMA((16,)),
        ],
        3 * 10**9,
        2 * 10**7,
        32,
    )(place, *gathered, time, space, got, probs, out, low_back, du)

    summed = grads.reshape(16, 4, 24, 128).transpose(1, 0, 2, 3).reshape(4, 384, 128)
    summed = exchange(summed, "y").astype(F32).sum(0).astype(BF16)
    summed = exchange(summed.reshape(4, 96, 128), "x").astype(F32).sum(0).astype(BF16)

    other = permute(there, other_core)
    back = jnp.where(c == 0, here, other)
    back, summed = lax.optimization_barrier((back, summed))
    back = exchange(back.reshape(16, 8, WIDE), ("y", "zl")).reshape(ROWS, WIDE)

    summed = lax.psum(summed, "zh")
    summed = lax.dynamic_slice(summed, (zh * 24, 0), (24, 128))
    summed = lax.psum(summed, "zl")
    summed = lax.all_gather(summed, "y", tiled=True)
    pair = permute(summed, other_core)
    summed = jnp.stack([jnp.where(c == 0, pair, summed), jnp.where(c == 0, summed, pair)]).astype(F32)
    grad_up = jnp.swapaxes(summed[:, :, :RANK], 1, 2)
    grad_down = summed[:, :, RANK:]

    mine = jnp.where(c == 0, other, here)
    total = [
        (mine[:, at : at + FEATURES].astype(F32) + back[:, at : at + FEATURES].astype(F32)).astype(BF16).reshape(out_dims)
        for at in (COT, 0, FEATURES, 2 * FEATURES)
    ]
    return (*total, grad_down, grad_up)


def solution(mesh):
    fine = Mesh(mesh.devices.reshape(SIZES), AXES)
    dp, seq = ("x", "zh"), ("y", "zl", "c")
    tokens = P(dp, seq, None, None)
    rows, columns = P(None, dp, None), P(None, None, dp)
    return jax.shard_map(
        local,
        mesh=fine,
        in_specs=(tokens,) * 4 + (rows, rows, columns),
        out_specs=(tokens,) * 4 + (rows, columns),
        check_vma=False,
    )
```

time: 279 us -> 259 us (0.928)
  blocking collectives: 36.8 us -> 87.1 us
  starting transfers between devices: 113 us -> 75.2 us
  local copies, waits for them, and re-layouts: 33.8 us -> 4.52 us
  waiting for transfers between devices: 51.8 us -> 57.6 us
  Pallas kernels: 28.9 us -> 23.8 us
    psum x0 -> x2, blocking collectives: none -> 60.6 us  [the longest x1 40.2 us: local(): summed = lax.psum(summed, 'zh')]
    all_to_all x5 -> x2, starting transfers between devices: 36.1 us -> 14.2 us  [exchange(): return lax.all_to_all(value, axes, split_axis=0, concat_axis=0, tiled=True)]
    all_to_all x2, blocking collectives: 36.8 us -> 17.1 us  [exchange(): return lax.all_to_all(value, axes, split_axis=0, concat_axis=0, tiled=True)]
    all_to_all x5 -> x2, waiting for transfers between devices: 10.9 us -> 29.1 us  [exchange(): return lax.all_to_all(value, axes, split_axis=0, concat_axis=0, tiled=True)]
    ppermute x21 -> x12, starting transfers between devices: 77.1 us -> 60.9 us  [permute(): return lax.ppermute(value, AXES, pairs)]
    ppermute x21 -> x12, waiting for transfers between devices: 41 us -> 28.5 us  [permute(): return lax.ppermute(value, AXES, pairs)]
    all_gather x0 -> x1, blocking collectives: none -> 9.4 us  [local(): summed = lax.all_gather(summed, 'y', tiled=True)]
    reshape x5 -> x2, local copies, waits for them, and re-layouts: 9.21 us -> 0.05 us  [the longest x1 0.04 us: local(): grads.reshape(16, 4, 24, 128).transpose(1, 0, 2, 3).reshape(4, 384, 128)]
  transfers between devices with their start and end apart: 26 -> 14, of which waited for: 7 -> 5; matrix products, arithmetic and copies ran while one was open for 10% -> 2% of each run, Pallas kernels for 10% -> 3%
where the time goes in v2:
time: 259 us
  blocking collectives  87.1 us (34%)
  starting transfers between devices  75.2 us (29%)
  waiting for transfers between devices  57.6 us (22%)
  Pallas kernels  23.8 us (9%)
  other arithmetic  9.32 us (4%)
  local copies, waits for them, and re-layouts  4.52 us (2%)
    ppermute x12, starting transfers between devices, permute(): return lax.ppermute(value, AXES, pairs)  60.9 us
    psum x1, blocking collectives, local(): summed = lax.psum(summed, 'zh')  40.2 us
    all_to_all x2, waiting for transfers between devices, exchange(): return lax.all_to_all(value, axes, split_axis=0, concat_axis=0, tiled=True)  29.1 us
    ppermute x12, waiting for transfers between devices, permute(): return lax.ppermute(value, AXES, pairs)  28.5 us
    psum x1, blocking collectives, local(): summed = lax.psum(summed, 'zl')  20.4 us
    all_to_all x2, blocking collectives, exchange(): return lax.all_to_all(value, axes, split_axis=0, concat_axis=0, tiled=True)  17.1 us
    all_to_all x2, starting transfers between devices, exchange(): return lax.all_to_all(value, axes, split_axis=0, concat_axis=0, tiled=True)  14.2 us
    pallas_call x1, Pallas kernels, local(): call(rest, (shape((ROWS, WIDE)), shape((ROWS, WIDE))), [SM] + [ANY] * 8 +...  12.9 us
  transfers between devices with their start and end apart: 14, of which 5 were waited for; matrix products, arithmetic and copies ran while one was open for 2% of the time, Pallas kernels for 3%

profile of v2, /device:TPU:1, one launch (start us, length us, event | category | flops | bytes accessed | tf_op | source)
XLA Modules:
  0.0 258.5 jit_solution(14147457806404013818)
XLA Ops:
  0.6 0.0 copy-start
  0.7 0.9 copy.24
  1.6 0.9 copy.23
  2.5 0.1 fusion.4
  2.6 0.0 copy-done
  2.6 13.3 %collective-permute-start.2 = (bf16[112,384]{1,0:T(8,128)(2,1)S(1)}, bf16[112,384]{1,0:T(8,128)(2,1)S(1)}, u32[]{:S(2)}, u32[]{:S(2)}) collective-permute-start(bf16[112,384]{1,0:T(8,128)(2,1)S(1)} %pad_maximum_fusion.2.s0), channel_id=1, source_target_pairs={{0,96},{1,97},{2,98},{3,99},{4,100},{5,101},{6,102},{7,103},{8,104... | collective-permute-start | bytes 258056 | tf_op jit(solution)/shard_map/ppermute | solution.py:227
  15.9 4.9 %collective-permute-start.1 = (bf16[112,384]{1,0:T(8,128)(2,1)S(1)}, bf16[112,384]{1,0:T(8,128)(2,1)S(1)}, u32[]{:S(2)}, u32[]{:S(2)}) collective-permute-start(bf16[112,384]{1,0:T(8,128)(2,1)S(1)} %pad_maximum_fusion.2.s0), channel_id=1, source_target_pairs={{0,64},{1,65},{2,66},{3,67},{4,68},{5,69},{6,70},{7,71},{8,72},{9,... | collective-permute-start | bytes 258056 | tf_op jit(solution)/shard_map/ppermute | solution.py:227
  20.8 7.3 %collective-permute-start = (bf16[112,384]{1,0:T(8,128)(2,1)S(1)}, bf16[112,384]{1,0:T(8,128)(2,1)S(1)}, u32[]{:S(2)}, u32[]{:S(2)}) collective-permute-start(bf16[112,384]{1,0:T(8,128)(2,1)S(1)} %pad_maximum_fusion.2.s0), channel_id=1, source_target_pairs={{0,32},{1,33},{2,34},{3,35},{4,36},{5,37},{6,38},{7,39},{8,40},{9,... | collective-permute-start | bytes 258056 | tf_op jit(solution)/shard_map/ppermute | solution.py:227
  28.1 2.7 %pad_maximum_fusion.own_space = bf16[128,6144]{1,0:T(8,128)(2,1)} fusion(bf16[128,1536]{1,0:T(8,128)(2,1)} %bitcast.54, bf16[128,1536]{1,0:T(8,128)(2,1)} %bitcast.55, bf16[128,1536]{1,0:T(8,128)(2,1)} %bitcast.56, bf16[128,1536]{1,0:T(8,128)(2,1)} %bitcast.57), kind=kLoop, calls=%fused_computation | loop fusion | flops 6291456 | bytes 3145728 | tf_op jit(solution)/shard_map/concatenate | solution.py:254
  30.8 0.1 pad_add_fusion.place
  30.8 0.0 collective-permute-done.2.s3
  30.8 0.0 collective-permute-done.1.s2
  30.8 4.6 %collective-permute-done.s1 = bf16[112,384]{1,0:T(8,128)(2,1)S(1)} collective-permute-done((bf16[112,384]{1,0:T(8,128)(2,1)S(1)}, bf16[112,384]{1,0:T(8,128)(2,1)S(1)}, u32[]{:S(2)}, u32[]{:S(2)}) %collective-permute-start) | collective-permute-done | bytes 86048 | tf_op jit(solution)/shard_map/ppermute | solution.py:227
  35.4 0.6 shard_map.118
  36.0 10.5 %all-to-all-start = ((bf16[16,8,6144]{2,1,0:T(8,128)(2,1)}), bf16[16,8,6144]{2,1,0:T(8,128)(2,1)S(1)}, u32[]{:S(2)}, u32[]{:S(2)}) async-start(bf16[16,8,6144]{2,1,0:T(8,128)(2,1)} %bitcast.16), calls=%async_computation | async-start | bytes 3145728 | tf_op jit(solution)/shard_map/all_to_all | solution.py:247
  46.6 4.5 %collective-permute-start.5 = (bf16[4,112,384]{2,1,0:T(8,128)(2,1)S(1)}, bf16[4,112,384]{2,1,0:T(8,128)(2,1)S(1)}, u32[]{:S(2)}, u32[]{:S(2)}) collective-permute-start(bf16[4,112,384]{2,1,0:T(8,128)(2,1)S(1)} %shard_map.118), channel_id=1, source_target_pairs={{0,384},{1,25},{2,386},{3,27},{4,388},{5,29},{6,390},{7,31},{8,392... | collective-permute-start | bytes 1032200 | tf_op jit(solution)/shard_map/ppermute | solution.py:227
  51.0 2.5 collective-permute-start.4
  53.5 2.5 collective-permute-start.3
  56.0 29.1 %all-to-all-done = bf16[16,8,6144]{2,1,0:T(8,128)(2,1)S(1)} async-done(((bf16[16,8,6144]{2,1,0:T(8,128)(2,1)}), bf16[16,8,6144]{2,1,0:T(8,128)(2,1)S(1)}, u32[]{:S(2)}, u32[]{:S(2)}) %all-to-all-start) | async-done | bytes 1572896 | tf_op jit(solution)/shard_map/all_to_all | solution.py:247
  85.1 0.2 broadcast_select_fusion.2
  85.3 4.7 %collective-permute-start.9 = (bf16[128,6144]{1,0:T(8,128)(2,1)S(1)}, bf16[128,6144]{1,0:T(8,128)(2,1)S(1)}, u32[]{:S(2)}, u32[]{:S(2)}) collective-permute-start(bf16[128,6144]{1,0:T(8,128)(2,1)S(1)} %broadcast_select_fusion.2), channel_id=1, source_target_pairs={{0,1},{1,0},{2,3},{3,2},{4,5},{5,4},{6,7},{7,6},{8,9},{9,8},{10,11... | collective-permute-start | bytes 4718600 | tf_op jit(solution)/shard_map/ppermute | solution.py:227
  90.0 0.0 collective-permute-done.5
  90.0 0.0 collective-permute-done.4
  90.0 0.0 collective-permute-done.3
  90.1 0.2 pad_maximum_fusion.1.m0
  90.3 4.4 %collective-permute-start.8 = (bf16[4,4,112,384]{3,2,1,0:T(8,128)(2,1)S(1)}, bf16[4,4,112,384]{3,2,1,0:T(8,128)(2,1)S(1)}, u32[]{:S(2)}, u32[]{:S(2)}) collective-permute-start(bf16[4,4,112,384]{3,2,1,0:T(8,128)(2,1)S(1)} %pad_maximum_fusion.1.m0), channel_id=1, source_target_pairs={{0,24},{1,385},{2,26},{3,387},{4,28},{5,389},{6,30},{7,391},{8,0},... | collective-permute-start | bytes 4128776 | tf_op jit(solution)/shard_map/ppermute | solution.py:227
  94.7 2.4 collective-permute-start.7
  97.1 2.5 collective-permute-start.6
  99.6 0.0 collective-permute-done.9.got
  99.6 7.2 %shard_map.119 = (f32[12,256,256]{2,1,0:T(8,128)S(1)}, bf16[256,1536]{1,0:T(8,128)(2,1)S(1)}) custom-call(s32[4]{0:T(128)S(1)} %pad_add_fusion.place, bf16[128,6144]{1,0:T(8,128)(2,1)S(1)} %bitcast.46, bf16[128,6144]{1,0:T(8,128)(2,1)} %pad_maximum_fusion.own_space, bf16[128,6144]{1,0:T(8,128)(2,1)S(1)} %collective-permute-done.9.got), custom_call_target="tpu_custom_call" | custom-call | flops 400000000 | bytes 10000000 | tf_op jit(solution)/shard_map/pallas_call | solution.py:271
  106.9 17.8 %collective-permute-done.8.m3 = bf16[4,4,112,384]{3,2,1,0:T(8,128)(2,1)S(1)} collective-permute-done((bf16[4,4,112,384]{3,2,1,0:T(8,128)(2,1)S(1)}, bf16[4,4,112,384]{3,2,1,0:T(8,128)(2,1)S(1)}, u32[]{:S(2)}, u32[]{:S(2)}) %collective-permute-start.8) | collective-permute-done | bytes 1376288 | tf_op jit(solution)/shard_map/ppermute | solution.py:227
  124.7 0.0 collective-permute-done.7.m2
  124.7 5.3 %collective-permute-done.6.m1 = bf16[4,4,112,384]{3,2,1,0:T(8,128)(2,1)S(1)} collective-permute-done((bf16[4,4,112,384]{3,2,1,0:T(8,128)(2,1)S(1)}, bf16[4,4,112,384]{3,2,1,0:T(8,128)(2,1)S(1)}, u32[]{:S(2)}, u32[]{:S(2)}) %collective-permute-start.6) | collective-permute-done | bytes 1376288 | tf_op jit(solution)/shard_map/ppermute | solution.py:227
  130.0 3.1 %shard_map.120 = (bf16[1536,128]{1,0:T(8,128)(2,1)S(1)}, bf16[256,128]{1,0:T(8,128)(2,1)S(1)}, bf16[1536,128]{1,0:T(8,128)(2,1)S(1)}) custom-call(s32[4]{0:T(128)S(1)} %pad_add_fusion.place, bf16[4,4,112,384]{3,2,1,0:T(8,128)(2,1)S(1)} %pad_maximum_fusion.1.m0, bf16[4,4,112,384]{3,2,1,0:T(8,128)(2,1)S(1)} %collective-permute-done.6.m1, ...), custom_call_target="tpu_custom_call" | custom-call | flops 400000000 | bytes 5000000 | tf_op jit(solution)/shard_map/pallas_call | solution.py:282
  133.1 12.9 %shard_map.121 = (bf16[128,6144]{1,0:T(8,128)(2,1)S(1)}, bf16[128,6144]{1,0:T(8,128)(2,1)}) custom-call(s32[4]{0:T(128)S(1)} %pad_add_fusion.place, bf16[4,4,112,384]{3,2,1,0:T(8,128)(2,1)S(1)} %pad_maximum_fusion.1.m0, bf16[4,4,112,384]{3,2,1,0:T(8,128)(2,1)S(1)} %collective-permute-done.6.m1, bf16[4,4,112,384]{3,2,1,0:T(8,128)(2,1)S(1)} %collective-permute-done.7.m2, ...), custom_call_target="tpu_custom_call" | custom-call | flops 3000000000 | bytes 20000000 | tf_op jit(solution)/shard_map/pallas_call | solution.py:293
  146.0 0.0 copy-start.1
  146.0 1.1 copy-done.1
  147.1 0.0 copy-start.2
  147.1 2.0 collective-permute-start.10
  149.2 10.1 %all_to_all.20 = bf16[4,384,128]{2,1,0:T(8,128)(2,1)S(1)} all-to-all(bf16[4,384,128]{2,1,0:T(8,128)(2,1)S(1)} %bitcast.53), channel_id=1, replica_groups=mesh['x'=4,'zh'=4,'y'=4,'zl'=4,'c'=2] {'y'}, dimensions={0} | all-to-all | bytes 786432 | tf_op jit(solution)/shard_map/all_to_all | solution.py:247
  159.3 0.1 reduce_sum.24
  159.4 7.0 %all_to_all.21 = bf16[4,96,128]{2,1,0:T(8,128)(2,1)S(1)} all-to-all(bf16[4,96,128]{2,1,0:T(8,128)(2,1)S(1)} %bitcast.58), channel_id=1, replica_groups=mesh['x'=4,'zh'=4,'y'=4,'zl'=4,'c'=2] {'x'}, dimensions={0} | all-to-all | bytes 196608 | tf_op jit(solution)/shard_map/all_to_all | solution.py:247
  166.4 0.0 collective-permute-done.10
  166.4 0.0 copy-done.2
  166.4 3.3 %broadcast_select_fusion.1 = (bf16[128,6144]{1,0:T(8,128)(2,1)}, bf16[128,6144]{1,0:T(8,128)(2,1)}) fusion(bf16[128,6144]{1,0:T(8,128)(2,1)} %collective-permute-done.10, bf16[128,6144]{1,0:T(8,128)(2,1)S(1)} %copy-done.2, pred[]{:T(512)S(6)} %eq.2), kind=kLoop, calls=%fused_computation.2 | loop fusion | flops 1572864 | bytes 6291457 | tf_op jit(solution)/shard_map/jit(_where)/select_n | solution.py:330
  169.7 3.7 %all-to-all-start.3 = ((bf16[16,8,6144]{2,1,0:T(8,128)(2,1)}), bf16[16,8,6144]{2,1,0:T(8,128)(2,1)S(1)}, u32[]{:S(2)}, u32[]{:S(2)}) async-start(bf16[16,8,6144]{2,1,0:T(8,128)(2,1)} %bitcast.52), calls=%async_computation.3 | async-start | bytes 3145728 | tf_op jit(solution)/shard_map/all_to_all | solution.py:247
  173.4 40.2 %psum.14 = bf16[96,128]{1,0:T(8,128)(2,1)S(1)} all-reduce(bf16[96,128]{1,0:T(8,128)(2,1)S(1)} %reduce_sum.25), channel_id=1, replica_groups=mesh['x'=4,'zh'=4,'y'=4,'zl'=4,'c'=2] {'zh'}, use_global_device_ids=true, to_apply=%region_2.3 | all-reduce | flops 12288 | bytes 49152 | tf_op jit(solution)/shard_map/psum | solution.py:321
  213.6 20.4 %psum.15 = bf16[24,128]{1,0:T(8,128)(2,1)S(1)} all-reduce(bf16[24,128]{1,0:T(8,128)(2,1)S(1)} %constant_dynamic-slice_fusion), channel_id=1, replica_groups=mesh['x'=4,'zh'=4,'y'=4,'zl'=4,'c'=2] {'zl'}, use_global_device_ids=true, to_apply=%region_3.4 | all-reduce | flops 3072 | bytes 12288 | tf_op jit(solution)/shard_map/psum | solution.py:323
  234.1 9.4 %all_gather.3 = bf16[96,128]{1,0:T(8,128)(2,1)S(1)} all-gather(bf16[24,128]{1,0:T(8,128)(2,1)S(1)} %psum.15), channel_id=1, replica_groups=mesh['x'=4,'zh'=4,'y'=4,'zl'=4,'c'=2] {'y'}, dimensions={0}, use_global_device_ids=true | all-gather | bytes 30720 | tf_op jit(solution)/shard_map/all_gather | solution.py:324
  243.5 9.9 %collective-permute-start.11 = (bf16[96,128]{1,0:T(8,128)(2,1)S(1)}, bf16[96,128]{1,0:T(8,128)(2,1)S(1)}, u32[]{:S(2)}, u32[]{:S(2)}) collective-permute-start(bf16[96,128]{1,0:T(8,128)(2,1)S(1)} %all_gather.3), channel_id=1, source_target_pairs={{0,1},{1,0},{2,3},{3,2},{4,5},{5,4},{6,7},{7,6},{8,9},{9,8},{10,11... | collective-permute-start | bytes 73736 | tf_op jit(solution)/shard_map/ppermute | solution.py:227
  253.4 0.8 collective-permute-done.11
  254.2 0.1 slice_bitcast_fusion
  254.3 0.7 copy.28
  255.1 0.7 copy.27
  255.8 0.0 all-to-all-done.3
  255.8 2.7 %fusion.3 = (bf16[1,1,128,1536]{3,2,1,0:T(8,128)(2,1)}, bf16[1,1,128,1536]{3,2,1,0:T(8,128)(2,1)}, bf16[1,1,128,1536]{3,2,1,0:T(8,128)(2,1)}, bf16[1,1,128,1536]{3,2,1,0:T(8,128)(2,1)}) fusion(bf16[128,6144]{1,0:T(8,128)(2,1)S(1)} %bitcast.51, bf16[128,6144]{1,0:T(8,128)(2,1)} %get-tuple-element.44), kind=kLoop, calls=%fused_computation.12 | loop fusion | flops 3145728 | bytes 4718592 | tf_op jit(solution)/shard_map/reshape | solution.py:332
  (8 shorter events, 0.1 us)
Async XLA Ops:
  0.6 1.9 copy-start
  2.6 28.2 %collective-permute-start.2 = (bf16[112,384]{1,0:T(8,128)(2,1)S(1)}, bf16[112,384]{1,0:T(8,128)(2,1)S(1)}, u32[]{:S(2)}, u32[]{:S(2)}) collective-permute-start(bf16[112,384]{1,0:T(8,128)(2,1)S(1)} %pad_maximum_fusion.2.s0), channel_id=1, source_target_pairs={{0,96},{1,97},{2,98},{3,99},{4,100},{5,101},{6,102},{7,103},{8,104... | collective-permute-start | bytes 258056 | tf_op jit(solution)/shard_map/ppermute | solution.py:227
  15.9 14.9 %collective-permute-start.1 = (bf16[112,384]{1,0:T(8,128)(2,1)S(1)}, bf16[112,384]{1,0:T(8,128)(2,1)S(1)}, u32[]{:S(2)}, u32[]{:S(2)}) collective-permute-start(bf16[112,384]{1,0:T(8,128)(2,1)S(1)} %pad_maximum_fusion.2.s0), channel_id=1, source_target_pairs={{0,64},{1,65},{2,66},{3,67},{4,68},{5,69},{6,70},{7,71},{8,72},{9,... | collective-permute-start | bytes 258056 | tf_op jit(solution)/shard_map/ppermute | solution.py:227
  20.8 14.6 %collective-permute-start = (bf16[112,384]{1,0:T(8,128)(2,1)S(1)}, bf16[112,384]{1,0:T(8,128)(2,1)S(1)}, u32[]{:S(2)}, u32[]{:S(2)}) collective-permute-start(bf16[112,384]{1,0:T(8,128)(2,1)S(1)} %pad_maximum_fusion.2.s0), channel_id=1, source_target_pairs={{0,32},{1,33},{2,34},{3,35},{4,36},{5,37},{6,38},{7,39},{8,40},{9,... | collective-permute-start | bytes 258056 | tf_op jit(solution)/shard_map/ppermute | solution.py:227
  36.0 49.1 %all-to-all-start = ((bf16[16,8,6144]{2,1,0:T(8,128)(2,1)}), bf16[16,8,6144]{2,1,0:T(8,128)(2,1)S(1)}, u32[]{:S(2)}, u32[]{:S(2)}) async-start(bf16[16,8,6144]{2,1,0:T(8,128)(2,1)} %bitcast.16), calls=%async_computation | async-start | bytes 3145728 | tf_op jit(solution)/shard_map/all_to_all | solution.py:247
  46.6 43.5 %collective-permute-start.5 = (bf16[4,112,384]{2,1,0:T(8,128)(2,1)S(1)}, bf16[4,112,384]{2,1,0:T(8,128)(2,1)S(1)}, u32[]{:S(2)}, u32[]{:S(2)}) collective-permute-start(bf16[4,112,384]{2,1,0:T(8,128)(2,1)S(1)} %shard_map.118), channel_id=1, source_target_pairs={{0,384},{1,25},{2,386},{3,27},{4,388},{5,29},{6,390},{7,31},{8,392... | collective-permute-start | bytes 1032200 | tf_op jit(solution)/shard_map/ppermute | solution.py:227
  51.0 39.0 %collective-permute-start.4 = (bf16[4,112,384]{2,1,0:T(8,128)(2,1)S(1)}, bf16[4,112,384]{2,1,0:T(8,128)(2,1)S(1)}, u32[]{:S(2)}, u32[]{:S(2)}) collective-permute-start(bf16[4,112,384]{2,1,0:T(8,128)(2,1)S(1)} %shard_map.118), channel_id=1, source_target_pairs={{0,256},{1,17},{2,258},{3,19},{4,260},{5,21},{6,262},{7,23},{8,264... | collective-permute-start | bytes 1032200 | tf_op jit(solution)/shard_map/ppermute | solution.py:227
  53.5 36.5 %collective-permute-start.3 = (bf16[4,112,384]{2,1,0:T(8,128)(2,1)S(1)}, bf16[4,112,384]{2,1,0:T(8,128)(2,1)S(1)}, u32[]{:S(2)}, u32[]{:S(2)}) collective-permute-start(bf16[4,112,384]{2,1,0:T(8,128)(2,1)S(1)} %shard_map.118), channel_id=1, source_target_pairs={{0,128},{1,9},{2,130},{3,11},{4,132},{5,13},{6,134},{7,15},{8,136}... | collective-permute-start | bytes 1032200 | tf_op jit(solution)/shard_map/ppermute | solution.py:227
  85.3 14.4 %collective-permute-start.9 = (bf16[128,6144]{1,0:T(8,128)(2,1)S(1)}, bf16[128,6144]{1,0:T(8,128)(2,1)S(1)}, u32[]{:S(2)}, u32[]{:S(2)}) collective-permute-start(bf16[128,6144]{1,0:T(8,128)(2,1)S(1)} %broadcast_select_fusion.2), channel_id=1, source_target_pairs={{0,1},{1,0},{2,3},{3,2},{4,5},{5,4},{6,7},{7,6},{8,9},{9,8},{10,11... | collective-permute-start | bytes 4718600 | tf_op jit(solution)/shard_map/ppermute | solution.py:227
  90.3 34.4 %collective-permute-start.8 = (bf16[4,4,112,384]{3,2,1,0:T(8,128)(2,1)S(1)}, bf16[4,4,112,384]{3,2,1,0:T(8,128)(2,1)S(1)}, u32[]{:S(2)}, u32[]{:S(2)}) collective-permute-start(bf16[4,4,112,384]{3,2,1,0:T(8,128)(2,1)S(1)} %pad_maximum_fusion.1.m0), channel_id=1, source_target_pairs={{0,24},{1,385},{2,26},{3,387},{4,28},{5,389},{6,30},{7,391},{8,0},... | collective-permute-start | bytes 4128776 | tf_op jit(solution)/shard_map/ppermute | solution.py:227
  94.7 30.0 %collective-permute-start.7 = (bf16[4,4,112,384]{3,2,1,0:T(8,128)(2,1)S(1)}, bf16[4,4,112,384]{3,2,1,0:T(8,128)(2,1)S(1)}, u32[]{:S(2)}, u32[]{:S(2)}) collective-permute-start(bf16[4,4,112,384]{3,2,1,0:T(8,128)(2,1)S(1)} %pad_maximum_fusion.1.m0), channel_id=1, source_target_pairs={{0,16},{1,257},{2,18},{3,259},{4,20},{5,261},{6,22},{7,263},{8,24}... | collective-permute-start | bytes 4128776 | tf_op jit(solution)/shard_map/ppermute | solution.py:227
  97.1 32.9 %collective-permute-start.6 = (bf16[4,4,112,384]{3,2,1,0:T(8,128)(2,1)S(1)}, bf16[4,4,112,384]{3,2,1,0:T(8,128)(2,1)S(1)}, u32[]{:S(2)}, u32[]{:S(2)}) collective-permute-start(bf16[4,4,112,384]{3,2,1,0:T(8,128)(2,1)S(1)} %pad_maximum_fusion.1.m0), channel_id=1, source_target_pairs={{0,8},{1,129},{2,10},{3,131},{4,12},{5,133},{6,14},{7,135},{8,16},... | collective-permute-start | bytes 4128776 | tf_op jit(solution)/shard_map/ppermute | solution.py:227
  146.0 1.2 copy-start.1
  147.1 19.3 %copy-start.2 = (bf16[128,6144]{1,0:T(8,128)(2,1)S(1)}, bf16[128,6144]{1,0:T(8,128)(2,1)}, u32[]{:S(2)}) copy-start(bf16[128,6144]{1,0:T(8,128)(2,1)} %copy-done.1) | copy-start | bytes 4718596
  147.1 19.3 %collective-permute-start.10 = (bf16[128,6144]{1,0:T(8,128)(2,1)}, bf16[128,6144]{1,0:T(8,128)(2,1)}, u32[]{:S(2)}, u32[]{:S(2)}) collective-permute-start(bf16[128,6144]{1,0:T(8,128)(2,1)} %get-tuple-element.23), channel_id=1, source_target_pairs={{0,1},{1,0},{2,3},{3,2},{4,5},{5,4},{6,7},{7,6},{8,9},{9,8},{10,11... | collective-permute-start | bytes 4718600 | tf_op jit(solution)/shard_map/ppermute | solution.py:227
  169.7 86.1 %all-to-all-start.3 = ((bf16[16,8,6144]{2,1,0:T(8,128)(2,1)}), bf16[16,8,6144]{2,1,0:T(8,128)(2,1)S(1)}, u32[]{:S(2)}, u32[]{:S(2)}) async-start(bf16[16,8,6144]{2,1,0:T(8,128)(2,1)} %bitcast.52), calls=%async_computation.3 | async-start | bytes 3145728 | tf_op jit(solution)/shard_map/all_to_all | solution.py:247
  243.5 10.8 %collective-permute-start.11 = (bf16[96,128]{1,0:T(8,128)(2,1)S(1)}, bf16[96,128]{1,0:T(8,128)(2,1)S(1)}, u32[]{:S(2)}, u32[]{:S(2)}) collective-permute-start(bf16[96,128]{1,0:T(8,128)(2,1)S(1)} %all_gather.3), channel_id=1, source_target_pairs={{0,1},{1,0},{2,3},{3,2},{4,5},{5,4},{6,7},{7,6},{8,9},{9,8},{10,11... | collective-permute-start | bytes 73736 | tf_op jit(solution)/shard_map/ppermute | solution.py:227

commit v3 on v2

v3 whole, which is shorter than its diff:
```python
import jax
import jax.numpy as jnp
from jax import lax
from jax.experimental import pallas as pl
from jax.experimental.pallas import tpu as pltpu
from jax.sharding import Mesh
from jax.sharding import PartitionSpec as P

HDIM = 128
HEADS = 12
FEATURES = 1536
ROWS = 128
BOTH = 2 * ROWS
RANK = 64
GAIN = 2.0
SCALE = HDIM ** (-0.5)
WIDE = 4 * FEATURES
COT = 3 * FEATURES
SLICE = 384
BLOCK = 256
GROUP = 3

AXES = ("x", "zh", "y", "zl", "c")
SIZES = (4, 4, 4, 4, 2)
F32 = jnp.float32
BF16 = jnp.bfloat16

VM = pl.BlockSpec(memory_space=pltpu.VMEM)
HBM = pl.BlockSpec(memory_space=pltpu.HBM)
SM = pl.BlockSpec(memory_space=pltpu.SMEM)


def nn(a, b):
    return lax.dot_general(a, b, (((1,), (0,)), ((), ())), preferred_element_type=F32)


def nt(a, b):
    return lax.dot_general(a, b, (((1,), (1,)), ((), ())), preferred_element_type=F32)


def tn(a, b):
    return lax.dot_general(a, b, (((0,), (0,)), ((), ())), preferred_element_type=F32)


def shape(dims, dtype=BF16):
    return jax.ShapeDtypeStruct(dims, dtype)


def call(kernel, out_shape, in_specs, out_specs, scratch, flops, nbytes, vmem_mib=62):
    return pl.pallas_call(
        kernel,
        out_shape=out_shape,
        in_specs=in_specs,
        out_specs=out_specs,
        scratch_shapes=scratch,
        compiler_params=pltpu.CompilerParams(vmem_limit_bytes=vmem_mib * 2**20),
        cost_estimate=pl.CostEstimate(flops=flops, bytes_accessed=nbytes, transcendentals=0),
    )


def head(ref, h, base=0):
    return ref[:, base + h * HDIM : base + (h + 1) * HDIM]


def piece_of(arrays, second, first):
    return arrays[second][first // 2].at[first % 2]


def wait_all(copies):
    for copy in copies:
        copy.wait()


def start_rows(place, time, space, other_time, other_space, rows, sems, spans):
    def copies(own, other):
        return [
            (
                pltpu.make_async_copy(own.at[:, at:to], rows.at[0:ROWS, into : into + to - at], sems.at[2 * i]),
                pltpu.make_async_copy(other.at[:, at:to], rows.at[ROWS:BOTH, into : into + to - at], sems.at[2 * i + 1]),
            )
            for i, (at, to, into) in enumerate(spans)
        ]

    @pl.when(place[3] == 0)
    def _():
        for pair in copies(time, other_time):
            wait_none(pair)

    @pl.when(place[3] != 0)
    def _():
        for pair in copies(space, other_space):
            wait_none(pair)

    return copies(time, other_time)


def wait_none(copies):
    for copy in copies:
        copy.start()


def spans_of_heads():
    return [
        (part * FEATURES + at, part * FEATURES + at + GROUP * HDIM, part * FEATURES + at)
        for at in range(0, FEATURES, GROUP * HDIM)
        for part in range(3)
    ]


def forward(
    place, e0, l0, e1, l1, e2, l2, e3, l3, time, space, other_time, other_space,
    probs_out, out_out, du_out, low_back_out, grads_out, rows, probs, out, du, low_back, grads, sems, row_sems, du_sems,
):
    arrays = ((e0, l0), (e1, l1), (e2, l2), (e3, l3))
    x, y, c = place[0], place[1], place[3]

    def pieces(first_is_x):
        made = []
        for across in range(4):
            for steps in (0, 2):
                second, first = (steps, across) if first_is_x else (across, steps)
                half = ((y - steps) & 3) >> 1
                for part in range(3):
                    made.append(
                        pltpu.make_async_copy(
                            piece_of(arrays, second, first).at[:, 96:112, part * 128 : part * 128 + 128],
                            du.at[pl.ds(((x - across) & 3) * 4, 4), pl.ds(pl.multiple_of(48 * half + 16 * part, 16), 16)],
                            du_sems.at[len(made)],
                        )
                    )
        return made

    loads = start_rows(
        place, time, space, other_time, other_space, rows, row_sems, spans_of_heads() + [(COT, WIDE, COT)]
    )

    @pl.when(c == 0)
    def _():
        wait_none(pieces(True))

    @pl.when(c != 0)
    def _():
        wait_none(pieces(False))

    across = lax.broadcasted_iota(jnp.int32, (BOTH, BOTH), 0)
    along = lax.broadcasted_iota(jnp.int32, (BOTH, BOTH), 1)
    mask = jnp.where(c == 0, across & 7, across >> 7) == jnp.where(c == 0, along & 7, along >> 7)
    copies = []
    for h in range(HEADS):
        if h % GROUP == 0:
            for pair in loads[h // GROUP * 3 : h // GROUP * 3 + 3]:
                wait_all(pair)
        scores = nt(head(rows, h), head(rows, h, FEATURES)) * SCALE
        scores = jnp.where(mask, scores, -1e30)
        scores = jnp.exp(scores - jnp.max(scores, axis=-1, keepdims=True))
        value = scores / jnp.sum(scores, axis=-1, keepdims=True)
        probs[h] = value
        copies.append(pltpu.make_async_copy(probs.at[h], probs_out.at[h], sems.at[h]))
        copies[-1].start()
        out[:, h * HDIM : (h + 1) * HDIM] = nn(value.astype(BF16), head(rows, h, 2 * FEATURES)).astype(BF16)
    wait_all(pieces(True))
    wait_all(loads[-1])
    copies += [
        pltpu.make_async_copy(out, out_out, sems.at[HEADS]),
        pltpu.make_async_copy(du, du_out, sems.at[HEADS + 1]),
    ]
    wait_none(copies[-2:])
    factors = du[...].reshape(FEATURES, 128)
    left = lax.broadcasted_iota(jnp.int32, (BOTH, 128), 1) < RANK
    low_back[...] = jnp.where(left, nn(out[...], factors), nn(rows[:, COT:], factors)).astype(BF16)
    left = lax.broadcasted_iota(jnp.int32, (FEATURES, 128), 1) < RANK
    grads[...] = (GAIN * jnp.where(left, tn(rows[:, COT:], low_back[...]), tn(out[...], low_back[...]))).astype(BF16)
    copies += [
        pltpu.make_async_copy(low_back, low_back_out, sems.at[HEADS + 2]),
        pltpu.make_async_copy(grads, grads_out, sems.at[HEADS + 3]),
    ]
    wait_none(copies[-2:])
    wait_all(copies)


def project(
    place, e0, l0, e1, l1, e2, l2, e3, l3, time, space, other_time, other_space, out_in, low_back_in, du_in,
    up_out, blended_out, weight, rows, out, low_back, du, up, blended, sems, row_sems, weight_sems,
):
    x, y, c = place[0], place[1], place[3]
    copies = []
    for second in range(4):
        for first in range(4):
            row = jnp.where(c == 0, x - first, x - second) & 3
            column = jnp.where(c == 0, y - second, y - first) & 3
            copies.append(
                pltpu.make_async_copy(
                    piece_of(((e0, l0), (e1, l1), (e2, l2), (e3, l3)), second, first).at[:, 0:96, :],
                    weight.at[pl.ds(row * 4, 4), :, pl.ds(pl.multiple_of(column * SLICE, 128), SLICE)],
                    weight_sems.at[len(copies)],
                )
            )
            copies[-1].start()
    smaller = [
        pltpu.make_async_copy(source, target, sems.at[i])
        for i, (source, target) in enumerate(((out_in, out), (low_back_in, low_back), (du_in, du)))
    ]
    wait_none(smaller)
    loads = start_rows(place, time, space, other_time, other_space, rows, row_sems, [(COT, WIDE, 0)])
    wait_all(copies + smaller)
    wait_all(loads[0])
    whole = weight.reshape(FEATURES, FEATURES)
    factors_of = du.reshape(FEATURES, 128)
    zero = jnp.zeros((), BF16)

    def step(i, _):
        at = pl.multiple_of(i * BLOCK, BLOCK)
        factors = factors_of[pl.ds(at, BLOCK), :]
        is_down = lax.broadcasted_iota(jnp.int32, (BLOCK, 128), 1) < RANK
        down = jnp.where(is_down, factors, zero)
        upper = jnp.where(is_down, zero, factors)
        swapped = jnp.concatenate([low_back[:, RANK:], low_back[:, :RANK]], axis=1)
        upstream = nt(rows[...], whole[pl.ds(at, BLOCK), :]) + GAIN * nt(swapped, down)
        up[:, pl.ds(at, BLOCK)] = upstream.astype(BF16)
        total = nn(out[...], whole[:, pl.ds(at, BLOCK)]) + GAIN * nt(swapped, upper)
        blended[:, pl.ds(at, BLOCK)] = total.astype(BF16)
        return 0

    lax.fori_loop(0, FEATURES // BLOCK, step, 0)
    copies = [
        pltpu.make_async_copy(up, up_out, sems.at[3]),
        pltpu.make_async_copy(blended, blended_out, sems.at[4]),
    ]
    wait_none(copies)
    wait_all(copies)


def backward(
    place, time, space, other_time, other_space, probs_in, up_in, blended_in,
    here_out, there_out, rows, probs, up, sent, sems, row_sems, out_sems,
):
    load_up = pltpu.make_async_copy(up_in, up, sems.at[0])
    load_blended = pltpu.make_async_copy(blended_in, sent.at[:, COT:], sems.at[1])
    loads = [pltpu.make_async_copy(probs_in.at[h], probs.at[h], sems.at[2 + h]) for h in range(HEADS)]
    load_up.start()
    wait_none(loads[:GROUP])
    load_rows = start_rows(place, time, space, other_time, other_space, rows, row_sems, spans_of_heads())
    wait_none(loads[GROUP:])
    load_blended.start()
    load_up.wait()
    copies = []

    def send(at, to):
        for ref, here, there in ((here_out, 0, ROWS), (there_out, ROWS, BOTH)):
            copies.append(pltpu.make_async_copy(sent.at[here:there, at:to], ref.at[:, at:to], out_sems.at[len(copies)]))
            copies[-1].start()

    for h in range(HEADS):
        if h % GROUP == 0:
            for pair in load_rows[h // GROUP * 3 : h // GROUP * 3 + 3]:
                wait_all(pair)
        loads[h].wait()
        value = probs[h]
        upstream = head(up, h)
        value_term = tn(value.astype(BF16), upstream)
        prob_term = nt(upstream, head(rows, h, 2 * FEATURES))
        centre = jnp.sum(value * prob_term, axis=-1, keepdims=True)
        score_term = (value * (prob_term - centre) * SCALE).astype(BF16)
        terms = (nn(score_term, head(rows, h, FEATURES)), tn(score_term, head(rows, h)), value_term)
        for i, term in enumerate(terms):
            at = i * FEATURES + h * HDIM
            sent[:, at : at + HDIM] = term.astype(BF16)
        if h % GROUP == GROUP - 1:
            for at in range(0, COT, FEATURES):
                send(at + (h + 1 - GROUP) * HDIM, at + (h + 1) * HDIM)
    load_blended.wait()
    send(COT, WIDE)
    wait_all(copies)


def choose(place, on_first, on_second, out, sem):
    @pl.when(place[3] == 0)
    def _():
        pltpu.make_async_copy(on_first, out, sem.at[0]).start()

    @pl.when(place[3] != 0)
    def _():
        pltpu.make_async_copy(on_second, out, sem.at[0]).start()

    pltpu.make_async_copy(on_first, out, sem.at[0]).wait()


def index_of(x, zh, y, zl, c):
    return (((x * 4 + zh) * 4 + y) * 4 + zl) * 2 + c


def permute(value, move):
    pairs = []
    for x in range(4):
        for zh in range(4):
            for y in range(4):
                for zl in range(4):
                    for c in range(2):
                        to = move(x, zh, y, zl, c)
                        if to is not None:
                            pairs.append((index_of(x, zh, y, zl, c), index_of(*to)))
    return lax.ppermute(value, AXES, pairs)


def along_first(step):
    return lambda x, zh, y, zl, c: ((x + step) % 4, zh, y, zl, c) if c == 0 else (x, zh, (y + step) % 4, zl, c)


def along_second(step):
    return lambda x, zh, y, zl, c: (x, zh, (y + step) % 4, zl, c) if c == 0 else ((x + step) % 4, zh, y, zl, c)


def other_core(x, zh, y, zl, c):
    return (x, zh, y, zl, 1 - c)


def to_first_core(x, zh, y, zl, c):
    return (x, zh, y, zl, 0) if c == 1 else None


def to_second_core(x, zh, y, zl, c):
    return (x, zh, y, zl, 1) if c == 0 else None


def exchange(value, axes):
    return lax.all_to_all(value, axes, split_axis=0, concat_axis=0, tiled=True)


def local(q, k, v, cot, weight, down, up):
    out_dims = q.shape
    x, zh, y, c = (lax.axis_index(n) for n in ("x", "zh", "y", "c"))
    place = jnp.stack([x, y, zh, c]).astype(jnp.int32)
    space = jnp.concatenate([a.reshape(ROWS, FEATURES) for a in (q, k, v, cot)], axis=1)

    branch = 1 - c
    piece = lax.dynamic_slice(weight, (branch, 0, y * SLICE), (1, 96, SLICE))[0]
    adapters = jnp.concatenate([down, jnp.swapaxes(up, 1, 2)], axis=2)
    adapters = lax.dynamic_slice(adapters, (branch, (y // 2) * 48, 0), (1, 48, 128))
    adapters = adapters.reshape(3, 16, 128).transpose(1, 0, 2).reshape(16, SLICE)
    first = jnp.concatenate([piece, adapters], axis=0)
    held = lax.all_gather(first, "zh")

    other_space = permute(space, to_second_core)
    space, held = lax.optimization_barrier((space, held))
    arrived = [permute(held, along_first(s)) for s in (1, 2, 3)]
    time = exchange(space.reshape(16, 8, WIDE), ("y", "zl")).reshape(ROWS, WIDE)
    early, late = jnp.stack([held, arrived[0]]), jnp.stack(arrived[1:])
    early_below, late_above = permute(early, along_second(1)), permute(late, along_second(3))
    early_above, late_below = permute(early, along_second(3)), permute(late, along_second(1))
    early_far, late_far = permute(early_below, along_second(1)), permute(late_above, along_second(3))
    gathered = [early, late, early_below, late_below, early_far, late_far, early_above, late_above]
    time, other_space, *gathered = lax.optimization_barrier((time, other_space, *gathered))
    other_time = permute(time, to_first_core)
    tokens = (time, space, other_time, other_space)

    probs, out, du, low_back, grads = call(
        forward,
        (
            shape((HEADS, BOTH, BOTH), F32),
            shape((BOTH, FEATURES)),
            shape((16, 96, 128)),
            shape((BOTH, 128)),
            shape((FEATURES, 128)),
        ),
        [SM] + [HBM] * 12,
        (HBM,) * 5,
        [
            pltpu.VMEM((BOTH, WIDE), BF16),
            pltpu.VMEM((HEADS, BOTH, BOTH), F32),
            pltpu.VMEM((BOTH, FEATURES), BF16),
            pltpu.VMEM((16, 96, 128), BF16),
            pltpu.VMEM((BOTH, 128), BF16),
            pltpu.VMEM((FEATURES, 128), BF16),
            pltpu.SemaphoreType.DMA((16,)),
            pltpu.SemaphoreType.DMA((26,)),
            pltpu.SemaphoreType.DMA((24,)),
        ],
        8 * 10**8,
        10**7,
    )(place, *gathered, *tokens)

    summed = grads.reshape(4, 4, 4, 24, 128).transpose(0, 2, 1, 3, 4).reshape(16, 96, 128)
    summed = exchange(summed, ("x", "y"))

    up, blended = call(
        project,
        (shape((BOTH, FEATURES)), shape((BOTH, FEATURES))),
        [SM] + [HBM] * 15,
        (HBM, HBM),
        [
            pltpu.VMEM((16, 96, FEATURES), BF16),
            pltpu.VMEM((BOTH, FEATURES), BF16),
            pltpu.VMEM((BOTH, FEATURES), BF16),
            pltpu.VMEM((BOTH, 128), BF16),
            pltpu.VMEM((16, 96, 128), BF16),
            pltpu.VMEM((BOTH, FEATURES), BF16),
            pltpu.VMEM((BOTH, FEATURES), BF16),
            pltpu.SemaphoreType.DMA((5,)),
            pltpu.SemaphoreType.DMA((2,)),
            pltpu.SemaphoreType.DMA((16,)),
        ],
        4 * 10**9,
        2 * 10**7,
    )(place, *gathered, *tokens, out, low_back, du)
    up, summed = lax.optimization_barrier((up, summed))

    summed = summed.astype(F32).sum(0).astype(BF16)
    summed = jnp.broadcast_to(summed.reshape(4, 1, 24, 128), (4, 4, 24, 128)).reshape(16, 24, 128)
    summed = exchange(summed, ("zh", "zl"))

    here, there = call(
        backward,
        (shape((ROWS, WIDE)), shape((ROWS, WIDE))),
        [SM] + [HBM] * 7,
        (HBM, HBM),
        [
            pltpu.VMEM((BOTH, COT), BF16),
            pltpu.VMEM((HEADS, BOTH, BOTH), F32),
            pltpu.VMEM((BOTH, FEATURES), BF16),
            pltpu.VMEM((BOTH, WIDE), BF16),
            pltpu.SemaphoreType.DMA((14,)),
            pltpu.SemaphoreType.DMA((24,)),
            pltpu.SemaphoreType.DMA((26,)),
        ],
        4 * 10**9,
        2 * 10**7,
    )(place, *tokens, probs, up, blended)
    there, summed = lax.optimization_barrier((there, summed))

    other = permute(there, other_core)
    back = call(
        choose, shape((ROWS, WIDE)), [SM, HBM, HBM], VM, [pltpu.SemaphoreType.DMA((1,))], 10**6, 3 * 10**6
    )(place, here, other)
    back = exchange(back.reshape(16, 8, WIDE), ("y", "zl")).reshape(ROWS, WIDE)

    summed = summed.astype(F32).sum(0).astype(BF16)
    summed = lax.all_gather(summed, "y", tiled=True)
    pair = permute(summed, other_core)
    summed = jnp.stack([jnp.where(c == 0, pair, summed), jnp.where(c == 0, summed, pair)]).astype(F32)
    grad_up = jnp.swapaxes(summed[:, :, :RANK], 1, 2)
    grad_down = summed[:, :, RANK:]

    mine = jnp.where(c == 0, other, here)
    total = [
        (mine[:, at : at + FEATURES].astype(F32) + back[:, at : at + FEATURES].astype(F32)).astype(BF16).reshape(out_dims)
        for at in (COT, 0, FEATURES, 2 * FEATURES)
    ]
    return (*total, grad_down, grad_up)


def solution(mesh):
    fine = Mesh(mesh.devices.reshape(SIZES), AXES)
    dp, seq = ("x", "zh"), ("y", "zl", "c")
    tokens = P(dp, seq, None, None)
    rows, columns = P(None, dp, None), P(None, None, dp)
    return jax.shard_map(
        local,
        mesh=fine,
        in_specs=(tokens,) * 4 + (rows, rows, columns),
        out_specs=(tokens,) * 4 + (rows, columns),
        check_vma=False,
    )
```

time: 259 us -> 205 us (0.79)
  blocking collectives: 87.1 us -> 43.6 us
  waiting for transfers between devices: 57.6 us -> 41.5 us
  Pallas kernels: 23.8 us -> 30.4 us
  starting transfers between devices: 75.2 us -> 71.3 us
  local copies, waits for them, and re-layouts: 4.52 us -> 7.84 us
    psum x2 -> x0, blocking collectives: 60.6 us -> none  [the longest x1 40.2 us: local(): summed = lax.psum(summed, 'zh')]
    all_gather x0 -> x1, blocking collectives: none -> 26.4 us  [local(): held = lax.all_gather(first, 'zh')]
    all_to_all x2 -> x0, blocking collectives: 17.1 us -> none  [exchange(): return lax.all_to_all(value, axes, split_axis=0, concat_axis=0, tiled=True)]
    ppermute x12 -> x13, starting transfers between devices: 60.9 us -> 45.2 us  [permute(): return lax.ppermute(value, AXES, pairs)]
    all_to_all x2 -> x4, waiting for transfers between devices: 29.1 us -> 13.8 us  [exchange(): return lax.all_to_all(value, axes, split_axis=0, concat_axis=0, tiled=True)]
    all_to_all x2 -> x4, starting transfers between devices: 14.2 us -> 26.2 us  [exchange(): return lax.all_to_all(value, axes, split_axis=0, concat_axis=0, tiled=True)]
    all_gather x1, blocking collectives: 9.4 us -> 17.1 us  [local(): summed = lax.all_gather(summed, 'y', tiled=True)]
    pallas_call x4, Pallas kernels: 23.8 us -> 30.4 us  [the longest x1 10.4 us: local(): call(backward, (shape((ROWS, WIDE)), shape((ROWS, WIDE))), [SM] + [HBM] *...]
  transfers between devices with their start and end apart: 14 -> 17, of which waited for: 5 -> 12; matrix products, arithmetic and copies ran while one was open for 2% -> 2% of each run, Pallas kernels for 3% -> 10%
where the time goes in v3:
time: 205 us; the launch traced here: 204 us
  starting transfers between devices  71.3 us (35%)
  blocking collectives  43.6 us (21%)
  waiting for transfers between devices  41.5 us (20%)
  Pallas kernels  30.4 us (15%)
  other arithmetic  8.23 us (4%)
  local copies, waits for them, and re-layouts  7.84 us (4%)
    ppermute x13, starting transfers between devices, permute(): return lax.ppermute(value, AXES, pairs)  45.2 us
    ppermute x13, waiting for transfers between devices, permute(): return lax.ppermute(value, AXES, pairs)  27.7 us
    all_gather x1, blocking collectives, local(): held = lax.all_gather(first, 'zh')  26.4 us
    all_to_all x4, starting transfers between devices, exchange(): return lax.all_to_all(value, axes, split_axis=0, concat_axis=0, tiled=True)  26.2 us
    all_gather x1, blocking collectives, local(): summed = lax.all_gather(summed, 'y', tiled=True)  17.1 us
    all_to_all x4, waiting for transfers between devices, exchange(): return lax.all_to_all(value, axes, split_axis=0, concat_axis=0, tiled=True)  13.8 us
    pallas_call x1, Pallas kernels, local(): call(backward, (shape((ROWS, WIDE)), shape((ROWS, WIDE))), [SM] + [HBM] *...  10.4 us
    pallas_call x1, Pallas kernels, local(): call(project, (shape((BOTH, FEATURES)), shape((BOTH, FEATURES))), [SM] +...  9.05 us
  transfers between devices with their start and end apart: 17, of which 12 were waited for; matrix products, arithmetic and copies ran while one was open for 2% of the time, Pallas kernels for 10%

profile of v3, /device:TPU:1, one launch (start us, length us, event | category | flops | bytes accessed | tf_op | source)
XLA Modules:
  0.0 203.9 jit_solution(3118017602054521086)
XLA Ops:
  0.6 0.0 copy-start
  0.7 0.9 copy.18
  1.6 0.9 copy.17
  2.5 0.1 fusion.4
  2.6 0.0 copy-done
  2.6 26.4 %all-gather = bf16[448,384]{1,0:T(8,128)(2,1)S(1)} all-gather(bf16[112,384]{1,0:T(8,128)(2,1)S(1)} %pad_maximum_fusion.3), channel_id=2, replica_groups=mesh['x'=4,'zh'=4,'y'=4,'zl'=4,'c'=2] {'zh'}, dimensions={0}, use_global_device_ids=true | all-gather | bytes 430080 | tf_op jit(solution)/shard_map/all_gather | solution.py:341
  29.0 2.7 %pad_maximum_fusion.space = bf16[128,6144]{1,0:T(8,128)(2,1)} fusion(bf16[128,1536]{1,0:T(8,128)(2,1)} %bitcast.56, bf16[128,1536]{1,0:T(8,128)(2,1)} %bitcast.57, bf16[128,1536]{1,0:T(8,128)(2,1)} %bitcast.58, bf16[128,1536]{1,0:T(8,128)(2,1)} %bitcast.59), kind=kLoop, calls=%fused_computation | loop fusion | flops 6291456 | bytes 3145728 | tf_op jit(solution)/shard_map/concatenate | solution.py:333
  31.7 5.2 %all-to-all-start = ((bf16[16,8,6144]{2,1,0:T(8,128)(2,1)}), bf16[16,8,6144]{2,1,0:T(8,128)(2,1)S(1)}, u32[]{:S(2)}, u32[]{:S(2)}) async-start(bf16[16,8,6144]{2,1,0:T(8,128)(2,1)} %bitcast.13), calls=%async_computation | async-start | bytes 3145728 | tf_op jit(solution)/shard_map/all_to_all | solution.py:326
  36.9 3.3 %collective-permute-start.1 = (bf16[4,112,384]{2,1,0:T(8,128)(2,1)S(1)}, bf16[4,112,384]{2,1,0:T(8,128)(2,1)S(1)}, u32[]{:S(2)}, u32[]{:S(2)}) collective-permute-start(bf16[4,112,384]{2,1,0:T(8,128)(2,1)S(1)} %bitcast.52), channel_id=1, source_target_pairs={{0,128},{1,9},{2,130},{3,11},{4,132},{5,13},{6,134},{7,15},{8,136}... | collective-permute-start | bytes 1032200 | tf_op jit(solution)/shard_map/ppermute | solution.py:302
  40.2 3.2 %collective-permute-start.3 = (bf16[4,112,384]{2,1,0:T(8,128)(2,1)S(1)}, bf16[4,112,384]{2,1,0:T(8,128)(2,1)S(1)}, u32[]{:S(2)}, u32[]{:S(2)}) collective-permute-start(bf16[4,112,384]{2,1,0:T(8,128)(2,1)S(1)} %bitcast.53), channel_id=1, source_target_pairs={{0,384},{1,25},{2,386},{3,27},{4,388},{5,29},{6,390},{7,31},{8,392... | collective-permute-start | bytes 1032200 | tf_op jit(solution)/shard_map/ppermute | solution.py:302
  43.4 3.6 %collective-permute-start.2 = (bf16[4,112,384]{2,1,0:T(8,128)(2,1)S(1)}, bf16[4,112,384]{2,1,0:T(8,128)(2,1)S(1)}, u32[]{:S(2)}, u32[]{:S(2)}) collective-permute-start(bf16[4,112,384]{2,1,0:T(8,128)(2,1)S(1)} %bitcast.54), channel_id=1, source_target_pairs={{0,256},{1,17},{2,258},{3,19},{4,260},{5,21},{6,262},{7,23},{8,264... | collective-permute-start | bytes 1032200 | tf_op jit(solution)/shard_map/ppermute | solution.py:302
  47.0 1.3 collective-permute-start
  48.3 10.0 %collective-permute-done.1 = bf16[4,112,384]{2,1,0:T(8,128)(2,1)S(1)} collective-permute-done((bf16[4,112,384]{2,1,0:T(8,128)(2,1)S(1)}, bf16[4,112,384]{2,1,0:T(8,128)(2,1)S(1)}, u32[]{:S(2)}, u32[]{:S(2)}) %collective-permute-start.1) | collective-permute-done | bytes 344096 | tf_op jit(solution)/shard_map/ppermute | solution.py:302
  58.2 0.1 pad_maximum_fusion.1.e0
  58.3 0.0 copy-start.3
  58.3 3.1 %collective-permute-start.4 = (bf16[2,4,112,384]{3,2,1,0:T(8,128)(2,1)S(1)}, bf16[2,4,112,384]{3,2,1,0:T(8,128)(2,1)S(1)}, u32[]{:S(2)}, u32[]{:S(2)}) collective-permute-start(bf16[2,4,112,384]{3,2,1,0:T(8,128)(2,1)S(1)} %pad_maximum_fusion.1.e0), channel_id=1, source_target_pairs={{0,8},{1,129},{2,10},{3,131},{4,12},{5,133},{6,14},{7,135},{8,16},... | collective-permute-start | bytes 2064392 | tf_op jit(solution)/shard_map/ppermute | solution.py:302
  61.4 0.0 collective-permute-done.3
  61.4 2.2 %collective-permute-done.2 = bf16[4,112,384]{2,1,0:T(8,128)(2,1)S(1)} collective-permute-done((bf16[4,112,384]{2,1,0:T(8,128)(2,1)S(1)}, bf16[4,112,384]{2,1,0:T(8,128)(2,1)S(1)}, u32[]{:S(2)}, u32[]{:S(2)}) %collective-permute-start.2) | collective-permute-done | bytes 344096 | tf_op jit(solution)/shard_map/ppermute | solution.py:302
  63.7 0.1 pad_maximum_fusion.2.l0
  63.8 0.0 copy-start.4
  63.8 5.2 %collective-permute-start.7 = (bf16[2,4,112,384]{3,2,1,0:T(8,128)(2,1)S(1)}, bf16[2,4,112,384]{3,2,1,0:T(8,128)(2,1)S(1)}, u32[]{:S(2)}, u32[]{:S(2)}) collective-permute-start(bf16[2,4,112,384]{3,2,1,0:T(8,128)(2,1)S(1)} %pad_maximum_fusion.2.l0), channel_id=1, source_target_pairs={{0,24},{1,385},{2,26},{3,387},{4,28},{5,389},{6,30},{7,391},{8,0},... | collective-permute-start | bytes 2064392 | tf_op jit(solution)/shard_map/ppermute | solution.py:302
  69.0 2.3 %collective-permute-start.9 = (bf16[2,4,112,384]{3,2,1,0:T(8,128)(2,1)S(1)}, bf16[2,4,112,384]{3,2,1,0:T(8,128)(2,1)S(1)}, u32[]{:S(2)}, u32[]{:S(2)}) collective-permute-start(bf16[2,4,112,384]{3,2,1,0:T(8,128)(2,1)S(1)} %pad_maximum_fusion.1.e0), channel_id=1, source_target_pairs={{0,24},{1,385},{2,26},{3,387},{4,28},{5,389},{6,30},{7,391},{8,0},... | collective-permute-start | bytes 2064392 | tf_op jit(solution)/shard_map/ppermute | solution.py:302
  71.3 3.0 %collective-permute-start.5 = (bf16[2,4,112,384]{3,2,1,0:T(8,128)(2,1)S(1)}, bf16[2,4,112,384]{3,2,1,0:T(8,128)(2,1)S(1)}, u32[]{:S(2)}, u32[]{:S(2)}) collective-permute-start(bf16[2,4,112,384]{3,2,1,0:T(8,128)(2,1)S(1)} %pad_maximum_fusion.2.l0), channel_id=1, source_target_pairs={{0,8},{1,129},{2,10},{3,131},{4,12},{5,133},{6,14},{7,135},{8,16},... | collective-permute-start | bytes 2064392 | tf_op jit(solution)/shard_map/ppermute | solution.py:302
  74.3 0.0 collective-permute-done.4.e1
  74.3 0.0 copy-start.6
  74.3 1.9 collective-permute-start.6
  76.3 0.6 collective-permute-done.7.l3
  76.9 5.3 %collective-permute-start.8 = (bf16[2,4,112,384]{3,2,1,0:T(8,128)(2,1)S(1)}, bf16[2,4,112,384]{3,2,1,0:T(8,128)(2,1)}, u32[]{:S(2)}, u32[]{:S(2)}) collective-permute-start(bf16[2,4,112,384]{3,2,1,0:T(8,128)(2,1)S(1)} %collective-permute-done.7.l3), channel_id=1, source_target_pairs={{0,24},{1,385},{2,26},{3,387},{4,28},{5,389},{6,30},{7,391},{8,0},... | collective-permute-start | bytes 2064392 | tf_op jit(solution)/shard_map/ppermute | solution.py:302
  82.2 2.1 %collective-permute-done.9.e3 = bf16[2,4,112,384]{3,2,1,0:T(8,128)(2,1)S(1)} collective-permute-done((bf16[2,4,112,384]{3,2,1,0:T(8,128)(2,1)S(1)}, bf16[2,4,112,384]{3,2,1,0:T(8,128)(2,1)S(1)}, u32[]{:S(2)}, u32[]{:S(2)}) %collective-permute-start.9) | collective-permute-done | bytes 688160 | tf_op jit(solution)/shard_map/ppermute | solution.py:302
  84.2 0.2 collective-permute-done.5.l1
  84.5 0.0 collective-permute-done.other_space
  84.5 7.1 %collective-permute-done.6.e2 = bf16[2,4,112,384]{3,2,1,0:T(8,128)(2,1)S(1)} collective-permute-done((bf16[2,4,112,384]{3,2,1,0:T(8,128)(2,1)S(1)}, bf16[2,4,112,384]{3,2,1,0:T(8,128)(2,1)S(1)}, u32[]{:S(2)}, u32[]{:S(2)}) %collective-permute-start.6) | collective-permute-done | bytes 688160 | tf_op jit(solution)/shard_map/ppermute | solution.py:302
  91.5 0.0 copy-done.6
  91.5 0.0 copy-done.7
  91.6 0.9 copy-done.10
  92.5 0.0 collective-permute-done.8.l2
  92.5 0.0 all-to-all-done
  92.5 1.2 copy-done.2
  93.6 2.5 %collective-permute-start.10 = (bf16[128,6144]{1,0:T(8,128)(2,1)S(1)}, bf16[128,6144]{1,0:T(8,128)(2,1)}, u32[]{:S(2)}, u32[]{:S(2)}) collective-permute-start(bf16[128,6144]{1,0:T(8,128)(2,1)S(1)} %bitcast.48), channel_id=1, source_target_pairs={{1,0},{3,2},{5,4},{7,6},{9,8},{11,10},{13,12},{15,14},{17,16},{19,... | collective-permute-start | bytes 4718600 | tf_op jit(solution)/shard_map/ppermute | solution.py:302
  96.1 0.6 pad_add_fusion.place
  96.7 1.4 collective-permute-done.10.other_time
  98.1 7.7 %shard_map.118 = (f32[12,256,256]{2,1,0:T(8,128)}, bf16[256,1536]{1,0:T(8,128)(2,1)}, bf16[16,96,128]{2,1,0:T(8,128)(2,1)}, bf16[256,128]{1,0:T(8,128)(2,1)}, bf16[1536,128]{1,0:T(8,128)(2,1)}) custom-call(s32[4]{0:T(128)} %pad_add_fusion.place, bf16[2,4,112,384]{3,2,1,0:T(8,128)(2,1)} %copy-done.3, bf16[2,4,112,384]{3,2,1,0:T(8,128)(2,1)} %copy-done.4, ...), custom_call_target="tpu_custom_call" | custom-call | flops 800000000 | bytes 10000000 | tf_op jit(solution)/shard_map/pallas_call | solution.py:356
  105.8 1.8 copy.20
  107.6 5.0 %all-to-all-start.1 = ((bf16[16,96,128]{2,1,0:T(8,128)(2,1)}), bf16[16,96,128]{2,1,0:T(8,128)(2,1)S(1)}, u32[]{:S(2)}, u32[]{:S(2)}) async-start(bf16[16,96,128]{2,1,0:T(8,128)(2,1)} %bitcast.21), calls=%async_computation.1 | async-start | bytes 786432 | tf_op jit(solution)/shard_map/all_to_all | solution.py:326
  112.6 9.0 %shard_map.119 = (bf16[256,1536]{1,0:T(8,128)(2,1)}, bf16[256,1536]{1,0:T(8,128)(2,1)}) custom-call(s32[4]{0:T(128)} %pad_add_fusion.place, bf16[2,4,112,384]{3,2,1,0:T(8,128)(2,1)} %copy-done.3, bf16[2,4,112,384]{3,2,1,0:T(8,128)(2,1)} %copy-done.4, bf16[2,4,112,384]{3,2,1,0:T(8,128)(2,1)} %copy-done.6, bf16[2,4,112,384]{3,2,1,0:T(8,128)(2,1)} %copy-done.9, ...), custom_call_target="tpu_custom_call" | custom-call | flops 4000000000 | bytes 20000000 | tf_op jit(solution)/shard_map/pallas_call | solution.py:385
  121.6 0.2 all-to-all-done.1
  121.8 0.1 reduce_sum.24
  121.9 0.7 broadcast_in_dim.8
  122.6 11.0 %all-to-all-start.2 = ((bf16[16,24,128]{2,1,0:T(8,128)(2,1)}), bf16[16,24,128]{2,1,0:T(8,128)(2,1)S(1)}, u32[]{:S(2)}, u32[]{:S(2)}) async-start(bf16[16,24,128]{2,1,0:T(8,128)(2,1)} %bitcast.23), calls=%async_computation.2 | async-start | bytes 196608 | tf_op jit(solution)/shard_map/all_to_all | solution.py:326
  133.6 10.4 %shard_map.120 = (bf16[128,6144]{1,0:T(8,128)(2,1)}, bf16[128,6144]{1,0:T(8,128)(2,1)}) custom-call(s32[4]{0:T(128)} %pad_add_fusion.place, bf16[128,6144]{1,0:T(8,128)(2,1)} %bitcast.51, bf16[128,6144]{1,0:T(8,128)(2,1)} %pad_maximum_fusion.space, bf16[128,6144]{1,0:T(8,128)(2,1)} %collective-permute-done.10.other_time, bf16[128,6144]{1,0:T(8,128)(2,1)} %copy-done.5, ...), custom_call_target="tpu_custom_call" | custom-call | flops 4000000000 | bytes 20000000 | tf_op jit(solution)/shard_map/pallas_call | solution.py:411
  144.0 1.4 all-to-all-done.2
  145.4 4.9 %collective-permute-start.11 = (bf16[128,6144]{1,0:T(8,128)(2,1)}, bf16[128,6144]{1,0:T(8,128)(2,1)}, u32[]{:S(2)}, u32[]{:S(2)}) collective-permute-start(bf16[128,6144]{1,0:T(8,128)(2,1)} %get-tuple-element.53), channel_id=1, source_target_pairs={{0,1},{1,0},{2,3},{3,2},{4,5},{5,4},{6,7},{7,6},{8,9},{9,8},{10,11... | collective-permute-start | bytes 4718600 | tf_op jit(solution)/shard_map/ppermute | solution.py:302
  150.4 3.4 %collective-permute-done.11.on_second = bf16[128,6144]{1,0:T(8,128)(2,1)} collective-permute-done((bf16[128,6144]{1,0:T(8,128)(2,1)}, bf16[128,6144]{1,0:T(8,128)(2,1)}, u32[]{:S(2)}, u32[]{:S(2)}) %collective-permute-start.11) | collective-permute-done | bytes 1572896 | tf_op jit(solution)/shard_map/ppermute | solution.py:302
  153.7 3.2 %shard_map.121 = bf16[128,6144]{1,0:T(8,128)(2,1)} custom-call(s32[4]{0:T(128)} %pad_add_fusion.place, bf16[128,6144]{1,0:T(8,128)(2,1)} %get-tuple-element.54.on_first, bf16[128,6144]{1,0:T(8,128)(2,1)} %collective-permute-done.11.on_second), custom_call_target="tpu_custom_call" | custom-call | flops 1000000 | bytes 3000000 | tf_op jit(solution)/shard_map/pallas_call | solution.py:431
  157.0 5.0 %all-to-all-start.3 = ((bf16[16,8,6144]{2,1,0:T(8,128)(2,1)}), bf16[16,8,6144]{2,1,0:T(8,128)(2,1)}, u32[]{:S(2)}, u32[]{:S(2)}) async-start(bf16[16,8,6144]{2,1,0:T(8,128)(2,1)} %bitcast.47), calls=%async_computation.3 | async-start | bytes 3145728 | tf_op jit(solution)/shard_map/all_to_all | solution.py:326
  162.0 17.1 %all_gather.11 = bf16[96,128]{1,0:T(8,128)(2,1)S(1)} all-gather(bf16[24,128]{1,0:T(8,128)(2,1)S(1)} %reduce_sum.25), channel_id=1, replica_groups=mesh['x'=4,'zh'=4,'y'=4,'zl'=4,'c'=2] {'y'}, dimensions={0}, use_global_device_ids=true | all-gather | bytes 30720 | tf_op jit(solution)/shard_map/all_gather | solution.py:437
  179.2 5.6 %collective-permute-start.12 = (bf16[96,128]{1,0:T(8,128)(2,1)S(1)}, bf16[96,128]{1,0:T(8,128)(2,1)S(1)}, u32[]{:S(2)}, u32[]{:S(2)}) collective-permute-start(bf16[96,128]{1,0:T(8,128)(2,1)S(1)} %all_gather.11), channel_id=1, source_target_pairs={{0,1},{1,0},{2,3},{3,2},{4,5},{5,4},{6,7},{7,6},{8,9},{9,8},{10,11... | collective-permute-start | bytes 73736 | tf_op jit(solution)/shard_map/ppermute | solution.py:302
  184.8 0.8 collective-permute-done.12
  185.6 0.1 slice_bitcast_fusion
  185.7 0.7 copy.22
  186.4 0.7 copy.21
  187.1 1.4 broadcast_select_fusion
  188.5 12.1 %all-to-all-done.3 = bf16[16,8,6144]{2,1,0:T(8,128)(2,1)} async-done(((bf16[16,8,6144]{2,1,0:T(8,128)(2,1)}), bf16[16,8,6144]{2,1,0:T(8,128)(2,1)}, u32[]{:S(2)}, u32[]{:S(2)}) %all-to-all-start.3) | async-done | bytes 1572896 | tf_op jit(solution)/shard_map/all_to_all | solution.py:326
  200.6 3.2 %fusion.3 = (bf16[1,1,128,1536]{3,2,1,0:T(8,128)(2,1)}, bf16[1,1,128,1536]{3,2,1,0:T(8,128)(2,1)}, bf16[1,1,128,1536]{3,2,1,0:T(8,128)(2,1)}, bf16[1,1,128,1536]{3,2,1,0:T(8,128)(2,1)}) fusion(bf16[128,6144]{1,0:T(8,128)(2,1)} %bitcast.25, bf16[128,6144]{1,0:T(8,128)(2,1)} %broadcast_select_fusion), kind=kLoop, calls=%fused_computation.11 | loop fusion | flops 3145728 | bytes 4718592 | tf_op jit(solution)/shard_map/reshape | solution.py:445
  (19 shorter events, 0.1 us)
Async XLA Ops:
  0.6 1.9 copy-start
  31.7 60.8 %all-to-all-start = ((bf16[16,8,6144]{2,1,0:T(8,128)(2,1)}), bf16[16,8,6144]{2,1,0:T(8,128)(2,1)S(1)}, u32[]{:S(2)}, u32[]{:S(2)}) async-start(bf16[16,8,6144]{2,1,0:T(8,128)(2,1)} %bitcast.13), calls=%async_computation | async-start | bytes 3145728 | tf_op jit(solution)/shard_map/all_to_all | solution.py:326
  36.9 21.3 %collective-permute-start.1 = (bf16[4,112,384]{2,1,0:T(8,128)(2,1)S(1)}, bf16[4,112,384]{2,1,0:T(8,128)(2,1)S(1)}, u32[]{:S(2)}, u32[]{:S(2)}) collective-permute-start(bf16[4,112,384]{2,1,0:T(8,128)(2,1)S(1)} %bitcast.52), channel_id=1, source_target_pairs={{0,128},{1,9},{2,130},{3,11},{4,132},{5,13},{6,134},{7,15},{8,136}... | collective-permute-start | bytes 1032200 | tf_op jit(solution)/shard_map/ppermute | solution.py:302
  40.2 21.3 %collective-permute-start.3 = (bf16[4,112,384]{2,1,0:T(8,128)(2,1)S(1)}, bf16[4,112,384]{2,1,0:T(8,128)(2,1)S(1)}, u32[]{:S(2)}, u32[]{:S(2)}) collective-permute-start(bf16[4,112,384]{2,1,0:T(8,128)(2,1)S(1)} %bitcast.53), channel_id=1, source_target_pairs={{0,384},{1,25},{2,386},{3,27},{4,388},{5,29},{6,390},{7,31},{8,392... | collective-permute-start | bytes 1032200 | tf_op jit(solution)/shard_map/ppermute | solution.py:302
  43.4 20.3 %collective-permute-start.2 = (bf16[4,112,384]{2,1,0:T(8,128)(2,1)S(1)}, bf16[4,112,384]{2,1,0:T(8,128)(2,1)S(1)}, u32[]{:S(2)}, u32[]{:S(2)}) collective-permute-start(bf16[4,112,384]{2,1,0:T(8,128)(2,1)S(1)} %bitcast.54), channel_id=1, source_target_pairs={{0,256},{1,17},{2,258},{3,19},{4,260},{5,21},{6,262},{7,23},{8,264... | collective-permute-start | bytes 1032200 | tf_op jit(solution)/shard_map/ppermute | solution.py:302
  47.0 37.5 %collective-permute-start = (bf16[128,6144]{1,0:T(8,128)(2,1)}, bf16[128,6144]{1,0:T(8,128)(2,1)S(1)}, u32[]{:S(2)}, u32[]{:S(2)}) collective-permute-start(bf16[128,6144]{1,0:T(8,128)(2,1)} %pad_maximum_fusion.space), channel_id=1, source_target_pairs={{0,1},{2,3},{4,5},{6,7},{8,9},{10,11},{12,13},{14,15},{16,17},{18,... | collective-permute-start | bytes 4718600 | tf_op jit(solution)/shard_map/ppermute | solution.py:302
  58.3 39.8 %copy-start.3 = (bf16[2,4,112,384]{3,2,1,0:T(8,128)(2,1)}, bf16[2,4,112,384]{3,2,1,0:T(8,128)(2,1)S(1)}, u32[]{:S(2)}) copy-start(bf16[2,4,112,384]{3,2,1,0:T(8,128)(2,1)S(1)} %pad_maximum_fusion.1.e0) | copy-start | bytes 2064388
  58.3 16.0 %collective-permute-start.4 = (bf16[2,4,112,384]{3,2,1,0:T(8,128)(2,1)S(1)}, bf16[2,4,112,384]{3,2,1,0:T(8,128)(2,1)S(1)}, u32[]{:S(2)}, u32[]{:S(2)}) collective-permute-start(bf16[2,4,112,384]{3,2,1,0:T(8,128)(2,1)S(1)} %pad_maximum_fusion.1.e0), channel_id=1, source_target_pairs={{0,8},{1,129},{2,10},{3,131},{4,12},{5,133},{6,14},{7,135},{8,16},... | collective-permute-start | bytes 2064392 | tf_op jit(solution)/shard_map/ppermute | solution.py:302
  63.8 34.3 %copy-start.4 = (bf16[2,4,112,384]{3,2,1,0:T(8,128)(2,1)}, bf16[2,4,112,384]{3,2,1,0:T(8,128)(2,1)S(1)}, u32[]{:S(2)}) copy-start(bf16[2,4,112,384]{3,2,1,0:T(8,128)(2,1)S(1)} %pad_maximum_fusion.2.l0) | copy-start | bytes 2064388
  63.8 13.1 %collective-permute-start.7 = (bf16[2,4,112,384]{3,2,1,0:T(8,128)(2,1)S(1)}, bf16[2,4,112,384]{3,2,1,0:T(8,128)(2,1)S(1)}, u32[]{:S(2)}, u32[]{:S(2)}) collective-permute-start(bf16[2,4,112,384]{3,2,1,0:T(8,128)(2,1)S(1)} %pad_maximum_fusion.2.l0), channel_id=1, source_target_pairs={{0,24},{1,385},{2,26},{3,387},{4,28},{5,389},{6,30},{7,391},{8,0},... | collective-permute-start | bytes 2064392 | tf_op jit(solution)/shard_map/ppermute | solution.py:302
  69.0 15.2 %collective-permute-start.9 = (bf16[2,4,112,384]{3,2,1,0:T(8,128)(2,1)S(1)}, bf16[2,4,112,384]{3,2,1,0:T(8,128)(2,1)S(1)}, u32[]{:S(2)}, u32[]{:S(2)}) collective-permute-start(bf16[2,4,112,384]{3,2,1,0:T(8,128)(2,1)S(1)} %pad_maximum_fusion.1.e0), channel_id=1, source_target_pairs={{0,24},{1,385},{2,26},{3,387},{4,28},{5,389},{6,30},{7,391},{8,0},... | collective-permute-start | bytes 2064392 | tf_op jit(solution)/shard_map/ppermute | solution.py:302
  71.3 13.2 %collective-permute-start.5 = (bf16[2,4,112,384]{3,2,1,0:T(8,128)(2,1)S(1)}, bf16[2,4,112,384]{3,2,1,0:T(8,128)(2,1)S(1)}, u32[]{:S(2)}, u32[]{:S(2)}) collective-permute-start(bf16[2,4,112,384]{3,2,1,0:T(8,128)(2,1)S(1)} %pad_maximum_fusion.2.l0), channel_id=1, source_target_pairs={{0,8},{1,129},{2,10},{3,131},{4,12},{5,133},{6,14},{7,135},{8,16},... | collective-permute-start | bytes 2064392 | tf_op jit(solution)/shard_map/ppermute | solution.py:302
  74.3 17.2 %copy-start.6 = (bf16[2,4,112,384]{3,2,1,0:T(8,128)(2,1)}, bf16[2,4,112,384]{3,2,1,0:T(8,128)(2,1)S(1)}, u32[]{:S(2)}) copy-start(bf16[2,4,112,384]{3,2,1,0:T(8,128)(2,1)S(1)} %collective-permute-done.4.e1) | copy-start | bytes 2064388
  74.3 17.2 %collective-permute-start.6 = (bf16[2,4,112,384]{3,2,1,0:T(8,128)(2,1)S(1)}, bf16[2,4,112,384]{3,2,1,0:T(8,128)(2,1)S(1)}, u32[]{:S(2)}, u32[]{:S(2)}) collective-permute-start(bf16[2,4,112,384]{3,2,1,0:T(8,128)(2,1)S(1)} %collective-permute-done.4.e1), channel_id=1, source_target_pairs={{0,8},{1,129},{2,10},{3,131},{4,12},{5,133},{6,14},{7,135},{8,16},... | collective-permute-start | bytes 2064392 | tf_op jit(solution)/shard_map/ppermute | solution.py:302
  76.9 14.7 %copy-start.7 = (bf16[2,4,112,384]{3,2,1,0:T(8,128)(2,1)}, bf16[2,4,112,384]{3,2,1,0:T(8,128)(2,1)S(1)}, u32[]{:S(2)}) copy-start(bf16[2,4,112,384]{3,2,1,0:T(8,128)(2,1)S(1)} %collective-permute-done.7.l3) | copy-start | bytes 2064388
  76.9 15.6 %collective-permute-start.8 = (bf16[2,4,112,384]{3,2,1,0:T(8,128)(2,1)S(1)}, bf16[2,4,112,384]{3,2,1,0:T(8,128)(2,1)}, u32[]{:S(2)}, u32[]{:S(2)}) collective-permute-start(bf16[2,4,112,384]{3,2,1,0:T(8,128)(2,1)S(1)} %collective-permute-done.7.l3), channel_id=1, source_target_pairs={{0,24},{1,385},{2,26},{3,387},{4,28},{5,389},{6,30},{7,391},{8,0},... | collective-permute-start | bytes 2064392 | tf_op jit(solution)/shard_map/ppermute | solution.py:302
  84.2 7.3 %copy-start.8 = (bf16[2,4,112,384]{3,2,1,0:T(8,128)(2,1)}, bf16[2,4,112,384]{3,2,1,0:T(8,128)(2,1)S(1)}, u32[]{:S(2)}) copy-start(bf16[2,4,112,384]{3,2,1,0:T(8,128)(2,1)S(1)} %collective-permute-done.9.e3) | copy-start | bytes 2064388
  84.5 7.1 %copy-start.9 = (bf16[2,4,112,384]{3,2,1,0:T(8,128)(2,1)}, bf16[2,4,112,384]{3,2,1,0:T(8,128)(2,1)S(1)}, u32[]{:S(2)}) copy-start(bf16[2,4,112,384]{3,2,1,0:T(8,128)(2,1)S(1)} %collective-permute-done.5.l1) | copy-start | bytes 2064388
  84.5 7.1 %copy-start.5 = (bf16[128,6144]{1,0:T(8,128)(2,1)}, bf16[128,6144]{1,0:T(8,128)(2,1)S(1)}, u32[]{:S(2)}) copy-start(bf16[128,6144]{1,0:T(8,128)(2,1)S(1)} %collective-permute-done.other_space) | copy-start | bytes 4718596
  91.6 0.9 copy-start.10
  92.5 1.2 copy-start.2
  93.6 4.4 %collective-permute-start.10 = (bf16[128,6144]{1,0:T(8,128)(2,1)S(1)}, bf16[128,6144]{1,0:T(8,128)(2,1)}, u32[]{:S(2)}, u32[]{:S(2)}) collective-permute-start(bf16[128,6144]{1,0:T(8,128)(2,1)S(1)} %bitcast.48), channel_id=1, source_target_pairs={{1,0},{3,2},{5,4},{7,6},{9,8},{11,10},{13,12},{15,14},{17,16},{19,... | collective-permute-start | bytes 4718600 | tf_op jit(solution)/shard_map/ppermute | solution.py:302
  107.6 14.2 %all-to-all-start.1 = ((bf16[16,96,128]{2,1,0:T(8,128)(2,1)}), bf16[16,96,128]{2,1,0:T(8,128)(2,1)S(1)}, u32[]{:S(2)}, u32[]{:S(2)}) async-start(bf16[16,96,128]{2,1,0:T(8,128)(2,1)} %bitcast.21), calls=%async_computation.1 | async-start | bytes 786432 | tf_op jit(solution)/shard_map/all_to_all | solution.py:326
  122.6 22.9 %all-to-all-start.2 = ((bf16[16,24,128]{2,1,0:T(8,128)(2,1)}), bf16[16,24,128]{2,1,0:T(8,128)(2,1)S(1)}, u32[]{:S(2)}, u32[]{:S(2)}) async-start(bf16[16,24,128]{2,1,0:T(8,128)(2,1)} %bitcast.23), calls=%async_computation.2 | async-start | bytes 196608 | tf_op jit(solution)/shard_map/all_to_all | solution.py:326
  145.4 8.3 %collective-permute-start.11 = (bf16[128,6144]{1,0:T(8,128)(2,1)}, bf16[128,6144]{1,0:T(8,128)(2,1)}, u32[]{:S(2)}, u32[]{:S(2)}) collective-permute-start(bf16[128,6144]{1,0:T(8,128)(2,1)} %get-tuple-element.53), channel_id=1, source_target_pairs={{0,1},{1,0},{2,3},{3,2},{4,5},{5,4},{6,7},{7,6},{8,9},{9,8},{10,11... | collective-permute-start | bytes 4718600 | tf_op jit(solution)/shard_map/ppermute | solution.py:302
  157.0 30.1 %copy-start.1 = (bf16[128,6144]{1,0:T(8,128)(2,1)S(1)}, bf16[128,6144]{1,0:T(8,128)(2,1)}, u32[]{:S(2)}) copy-start(bf16[128,6144]{1,0:T(8,128)(2,1)} %get-tuple-element.54.on_first) | copy-start | bytes 4718596
  157.0 43.6 %all-to-all-start.3 = ((bf16[16,8,6144]{2,1,0:T(8,128)(2,1)}), bf16[16,8,6144]{2,1,0:T(8,128)(2,1)}, u32[]{:S(2)}, u32[]{:S(2)}) async-start(bf16[16,8,6144]{2,1,0:T(8,128)(2,1)} %bitcast.47), calls=%async_computation.3 | async-start | bytes 3145728 | tf_op jit(solution)/shard_map/all_to_all | solution.py:326
  179.2 6.4 %collective-permute-start.12 = (bf16[96,128]{1,0:T(8,128)(2,1)S(1)}, bf16[96,128]{1,0:T(8,128)(2,1)S(1)}, u32[]{:S(2)}, u32[]{:S(2)}) collective-permute-start(bf16[96,128]{1,0:T(8,128)(2,1)S(1)} %all_gather.11), channel_id=1, source_target_pairs={{0,1},{1,0},{2,3},{3,2},{4,5},{5,4},{6,7},{7,6},{8,9},{9,8},{10,11... | collective-permute-start | bytes 73736 | tf_op jit(solution)/shard_map/ppermute | solution.py:302

commit v4 on v3

--- a/solution.py
+++ b/solution.py
@@ -18,7 +18,6 @@
 COT = 3 * FEATURES
 SLICE = 384
 BLOCK = 256
-GROUP = 3
 
 AXES = ("x", "zh", "y", "zl", "c")
 SIZES = (4, 4, 4, 4, 2)
@@ -97,14 +96,6 @@
 def wait_none(copies):
     for copy in copies:
         copy.start()
-
-
-def spans_of_heads():
-    return [
-        (part * FEATURES + at, part * FEATURES + at + GROUP * HDIM, part * FEATURES + at)
-        for at in range(0, FEATURES, GROUP * HDIM)
-        for part in range(3)
-    ]
 
 
 def forward(
@@ -130,9 +121,7 @@
                     )
         return made
 
-    loads = start_rows(
-        place, time, space, other_time, other_space, rows, row_sems, spans_of_heads() + [(COT, WIDE, COT)]
-    )
+    loads = start_rows(place, time, space, other_time, other_space, rows, row_sems, [(0, WIDE, 0)])
 
     @pl.when(c == 0)
     def _():
@@ -145,34 +134,33 @@
     across = lax.broadcasted_iota(jnp.int32, (BOTH, BOTH), 0)
     along = lax.broadcasted_iota(jnp.int32, (BOTH, BOTH), 1)
     mask = jnp.where(c == 0, across & 7, across >> 7) == jnp.where(c == 0, along & 7, along >> 7)
-    copies = []
+    wait_all(loads[0])
     for h in range(HEADS):
-        if h % GROUP == 0:
-            for pair in loads[h // GROUP * 3 : h // GROUP * 3 + 3]:
-                wait_all(pair)
         scores = nt(head(rows, h), head(rows, h, FEATURES)) * SCALE
         scores = jnp.where(mask, scores, -1e30)
         scores = jnp.exp(scores - jnp.max(scores, axis=-1, keepdims=True))
-        value = scores / jnp.sum(scores, axis=-1, keepdims=True)
+        value = (scores / jnp.sum(scores, axis=-1, keepdims=True)).astype(BF16)
         probs[h] = value
-        copies.append(pltpu.make_async_copy(probs.at[h], probs_out.at[h], sems.at[h]))
-        copies[-1].start()
-        out[:, h * HDIM : (h + 1) * HDIM] = nn(value.astype(BF16), head(rows, h, 2 * FEATURES)).astype(BF16)
+        out[:, h * HDIM : (h + 1) * HDIM] = nn(value, head(rows, h, 2 * FEATURES)).astype(BF16)
     wait_all(pieces(True))
-    wait_all(loads[-1])
-    copies += [
-        pltpu.make_async_copy(out, out_out, sems.at[HEADS]),
-        pltpu.make_async_copy(du, du_out, sems.at[HEADS + 1]),
-    ]
-    wait_none(copies[-2:])
+    copies = [
+        pltpu.make_async_copy(probs, probs_out, sems.at[0]),
+        pltpu.make_async_copy(out, out_out, sems.at[1]),
+        pltpu.make_async_copy(du, du_out, sems.at[2]),
+    ]
+    wait_none(copies)
     factors = du[...].reshape(FEATURES, 128)
     left = lax.broadcasted_iota(jnp.int32, (BOTH, 128), 1) < RANK
     low_back[...] = jnp.where(left, nn(out[...], factors), nn(rows[:, COT:], factors)).astype(BF16)
     left = lax.broadcasted_iota(jnp.int32, (FEATURES, 128), 1) < RANK
-    grads[...] = (GAIN * jnp.where(left, tn(rows[:, COT:], low_back[...]), tn(out[...], low_back[...]))).astype(BF16)
+    total = GAIN * jnp.where(left, tn(rows[:, COT:], low_back[...]), tn(out[...], low_back[...]))
+    total = [
+        total[((x_at * 4 + zh_at) * 4 + y_at) * 24 :][:24] for x_at in range(4) for y_at in range(4) for zh_at in range(4)
+    ]
+    grads[...] = jnp.concatenate(total, axis=0).astype(BF16)
     copies += [
-        pltpu.make_async_copy(low_back, low_back_out, sems.at[HEADS + 2]),
-        pltpu.make_async_copy(grads, grads_out, sems.at[HEADS + 3]),
+        pltpu.make_async_copy(low_back, low_back_out, sems.at[3]),
+        pltpu.make_async_copy(grads, grads_out, sems.at[4]),
     ]
     wait_none(copies[-2:])
     wait_all(copies)
@@ -232,32 +220,22 @@
 
 def backward(
     place, time, space, other_time, other_space, probs_in, up_in, blended_in,
-    here_out, there_out, rows, probs, up, sent, sems, row_sems, out_sems,
+    here_out, there_out, rows, probs, up, sent, sems, row_sems,
 ):
-    load_up = pltpu.make_async_copy(up_in, up, sems.at[0])
-    load_blended = pltpu.make_async_copy(blended_in, sent.at[:, COT:], sems.at[1])
-    loads = [pltpu.make_async_copy(probs_in.at[h], probs.at[h], sems.at[2 + h]) for h in range(HEADS)]
-    load_up.start()
-    wait_none(loads[:GROUP])
-    load_rows = start_rows(place, time, space, other_time, other_space, rows, row_sems, spans_of_heads())
-    wait_none(loads[GROUP:])
-    load_blended.start()
-    load_up.wait()
-    copies = []
-
-    def send(at, to):
-        for ref, here, there in ((here_out, 0, ROWS), (there_out, ROWS, BOTH)):
-            copies.append(pltpu.make_async_copy(sent.at[here:there, at:to], ref.at[:, at:to], out_sems.at[len(copies)]))
-            copies[-1].start()
-
+    loads = [
+        pltpu.make_async_copy(up_in, up, sems.at[0]),
+        pltpu.make_async_copy(probs_in, probs, sems.at[1]),
+        pltpu.make_async_copy(blended_in, sent.at[:, COT:], sems.at[2]),
+    ]
+    wait_none(loads)
+    load_rows = start_rows(place, time, space, other_time, other_space, rows, row_sems, [(0, COT, 0)])
+    wait_all(loads)
+    wait_all(load_rows[0])
     for h in range(HEADS):
-        if h % GROUP == 0:
-            for pair in load_rows[h // GROUP * 3 : h // GROUP * 3 + 3]:
-                wait_all(pair)
-        loads[h].wait()
         value = probs[h]
         upstream = head(up, h)
-        value_term = tn(value.astype(BF16), upstream)
+        value_term = tn(value, upstream)
+        value = value.astype(F32)
         prob_term = nt(upstream, head(rows, h, 2 * FEATURES))
         centre = jnp.sum(value * prob_term, axis=-1, keepdims=True)
         score_term = (value * (prob_term - centre) * SCALE).astype(BF16)
@@ -265,24 +243,33 @@
         for i, term in enumerate(terms):
             at = i * FEATURES + h * HDIM
             sent[:, at : at + HDIM] = term.astype(BF16)
-        if h % GROUP == GROUP - 1:
-            for at in range(0, COT, FEATURES):
-                send(at + (h + 1 - GROUP) * HDIM, at + (h + 1) * HDIM)
-    load_blended.wait()
-    send(COT, WIDE)
+    copies = [
+        pltpu.make_async_copy(sent.at[0:ROWS], here_out, sems.at[3]),
+        pltpu.make_async_copy(sent.at[ROWS:BOTH], there_out, sems.at[4]),
+    ]
+    wait_none(copies)
     wait_all(copies)
 
 
-def choose(place, on_first, on_second, out, sem):
+def choose(place, on_first, on_second, out, held, sems):
+    parts = [pl.ds(at, FEATURES) for at in range(0, WIDE, FEATURES)]
+
+    def loads(source):
+        return [pltpu.make_async_copy(source.at[:, at], held.at[:, at], sems.at[i]) for i, at in enumerate(parts)]
+
     @pl.when(place[3] == 0)
     def _():
-        pltpu.make_async_copy(on_first, out, sem.at[0]).start()
+        wait_none(loads(on_first))
 
     @pl.when(place[3] != 0)
     def _():
-        pltpu.make_async_copy(on_second, out, sem.at[0]).start()
-
-    pltpu.make_async_copy(on_first, out, sem.at[0]).wait()
+        wait_none(loads(on_second))
+
+    stores = [pltpu.make_async_copy(held.at[:, at], out.at[:, at], sems.at[4 + i]) for i, at in enumerate(parts)]
+    for load, store in zip(loads(on_first), stores):
+        load.wait()
+        store.start()
+    wait_all(stores)
 
 
 def index_of(x, zh, y, zl, c):
@@ -356,7 +343,7 @@
     probs, out, du, low_back, grads = call(
         forward,
         (
-            shape((HEADS, BOTH, BOTH), F32),
+            shape((HEADS, BOTH, BOTH)),
             shape((BOTH, FEATURES)),
             shape((16, 96, 128)),
             shape((BOTH, 128)),
@@ -366,20 +353,20 @@
         (HBM,) * 5,
         [
             pltpu.VMEM((BOTH, WIDE), BF16),
-            pltpu.VMEM((HEADS, BOTH, BOTH), F32),
+            pltpu.VMEM((HEADS, BOTH, BOTH), BF16),
             pltpu.VMEM((BOTH, FEATURES), BF16),
             pltpu.VMEM((16, 96, 128), BF16),
             pltpu.VMEM((BOTH, 128), BF16),
             pltpu.VMEM((FEATURES, 128), BF16),
-            pltpu.SemaphoreType.DMA((16,)),
-            pltpu.SemaphoreType.DMA((26,)),
+            pltpu.SemaphoreType.DMA((5,)),
+            pltpu.SemaphoreType.DMA((2,)),
             pltpu.SemaphoreType.DMA((24,)),
         ],
         8 * 10**8,
         10**7,
     )(place, *gathered, *tokens)
 
-    summed = grads.reshape(4, 4, 4, 24, 128).transpose(0, 2, 1, 3, 4).reshape(16, 96, 128)
+    summed = grads.reshape(16, 96, 128)
     summed = exchange(summed, ("x", "y"))
 
     up, blended = call(
@@ -415,12 +402,11 @@
         (HBM, HBM),
         [
             pltpu.VMEM((BOTH, COT), BF16),
-            pltpu.VMEM((HEADS, BOTH, BOTH), F32),
+            pltpu.VMEM((HEADS, BOTH, BOTH), BF16),
             pltpu.VMEM((BOTH, FEATURES), BF16),
             pltpu.VMEM((BOTH, WIDE), BF16),
-            pltpu.SemaphoreType.DMA((14,)),
-            pltpu.SemaphoreType.DMA((24,)),
-            pltpu.SemaphoreType.DMA((26,)),
+            pltpu.SemaphoreType.DMA((5,)),
+            pltpu.SemaphoreType.DMA((2,)),
         ],
         4 * 10**9,
         2 * 10**7,
@@ -429,7 +415,7 @@
 
     other = permute(there, other_core)
     back = call(
-        choose, shape((ROWS, WIDE)), [SM, HBM, HBM], VM, [pltpu.SemaphoreType.DMA((1,))], 10**6, 3 * 10**6
+        choose, shape((ROWS, WIDE)), [SM, HBM, HBM], HBM, [pltpu.VMEM((ROWS, WIDE), BF16), pltpu.SemaphoreType.DMA((8,))], 10**6, 3 * 10**6
     )(place, here, other)
     back = exchange(back.reshape(16, 8, WIDE), ("y", "zl")).reshape(ROWS, WIDE)
 

time: 205 us -> 202 us (0.985)
  transfers between devices with their start and end apart: 17 -> 17, of which waited for: 12 -> 12; matrix products, arithmetic and copies ran while one was open for 2% -> 2% of each run, Pallas kernels for 10% -> 9%
where the time goes in v4:
time: 202 us; the launch traced here: 201 us
  starting transfers between devices  71.4 us (35%)
  blocking collectives  43.5 us (22%)
  waiting for transfers between devices  42.2 us (21%)
  Pallas kernels  28.7 us (14%)
  other arithmetic  8.23 us (4%)
  local copies, waits for them, and re-layouts  6.04 us (3%)
    ppermute x13, starting transfers between devices, permute(): return lax.ppermute(value, AXES, pairs)  45.3 us
    ppermute x13, waiting for transfers between devices, permute(): return lax.ppermute(value, AXES, pairs)  27.7 us
    all_gather x1, blocking collectives, local(): held = lax.all_gather(first, 'zh')  26.4 us
    all_to_all x4, starting transfers between devices, exchange(): return lax.all_to_all(value, axes, split_axis=0, concat_axis=0, tiled=True)  26.2 us
    all_gather x1, blocking collectives, local(): summed = lax.all_gather(summed, 'y', tiled=True)  17.1 us
    all_to_all x4, waiting for transfers between devices, exchange(): return lax.all_to_all(value, axes, split_axis=0, concat_axis=0, tiled=True)  14.4 us
    pallas_call x1, Pallas kernels, local(): call(backward, (shape((ROWS, WIDE)), shape((ROWS, WIDE))), [SM] + [HBM] *...  9.65 us
    pallas_call x1, Pallas kernels, local(): call(project, (shape((BOTH, FEATURES)), shape((BOTH, FEATURES))), [SM] +...  9.1 us
  transfers between devices with their start and end apart: 17, of which 12 were waited for; matrix products, arithmetic and copies ran while one was open for 2% of the time, Pallas kernels for 9%

profile of v4, /device:TPU:1, one launch (start us, length us, event | category | flops | bytes accessed | tf_op | source)
XLA Modules:
  0.0 201.1 jit_solution(14283420814999860012)
XLA Ops:
  0.6 0.0 copy-start
  0.7 0.9 copy.17
  1.6 0.9 copy.16
  2.5 0.1 fusion.4
  2.6 0.0 copy-done
  2.6 26.4 %all-gather = bf16[448,384]{1,0:T(8,128)(2,1)S(1)} all-gather(bf16[112,384]{1,0:T(8,128)(2,1)S(1)} %pad_maximum_fusion.3), channel_id=2, replica_groups=mesh['x'=4,'zh'=4,'y'=4,'zl'=4,'c'=2] {'zh'}, dimensions={0}, use_global_device_ids=true | all-gather | bytes 430080 | tf_op jit(solution)/shard_map/all_gather | solution.py:328
  29.0 2.7 %pad_maximum_fusion.space = bf16[128,6144]{1,0:T(8,128)(2,1)} fusion(bf16[128,1536]{1,0:T(8,128)(2,1)} %bitcast.53, bf16[128,1536]{1,0:T(8,128)(2,1)} %bitcast.54, bf16[128,1536]{1,0:T(8,128)(2,1)} %bitcast.55, bf16[128,1536]{1,0:T(8,128)(2,1)} %bitcast.56), kind=kLoop, calls=%fused_computation | loop fusion | flops 6291456 | bytes 3145728 | tf_op jit(solution)/shard_map/concatenate | solution.py:320
  31.7 5.2 %all-to-all-start = ((bf16[16,8,6144]{2,1,0:T(8,128)(2,1)}), bf16[16,8,6144]{2,1,0:T(8,128)(2,1)S(1)}, u32[]{:S(2)}, u32[]{:S(2)}) async-start(bf16[16,8,6144]{2,1,0:T(8,128)(2,1)} %bitcast.13), calls=%async_computation | async-start | bytes 3145728 | tf_op jit(solution)/shard_map/all_to_all | solution.py:313
  36.9 3.3 %collective-permute-start.1 = (bf16[4,112,384]{2,1,0:T(8,128)(2,1)S(1)}, bf16[4,112,384]{2,1,0:T(8,128)(2,1)S(1)}, u32[]{:S(2)}, u32[]{:S(2)}) collective-permute-start(bf16[4,112,384]{2,1,0:T(8,128)(2,1)S(1)} %bitcast.49), channel_id=1, source_target_pairs={{0,128},{1,9},{2,130},{3,11},{4,132},{5,13},{6,134},{7,15},{8,136}... | collective-permute-start | bytes 1032200 | tf_op jit(solution)/shard_map/ppermute | solution.py:289
  40.2 3.2 %collective-permute-start.3 = (bf16[4,112,384]{2,1,0:T(8,128)(2,1)S(1)}, bf16[4,112,384]{2,1,0:T(8,128)(2,1)S(1)}, u32[]{:S(2)}, u32[]{:S(2)}) collective-permute-start(bf16[4,112,384]{2,1,0:T(8,128)(2,1)S(1)} %bitcast.50), channel_id=1, source_target_pairs={{0,384},{1,25},{2,386},{3,27},{4,388},{5,29},{6,390},{7,31},{8,392... | collective-permute-start | bytes 1032200 | tf_op jit(solution)/shard_map/ppermute | solution.py:289
  43.4 3.6 %collective-permute-start.2 = (bf16[4,112,384]{2,1,0:T(8,128)(2,1)S(1)}, bf16[4,112,384]{2,1,0:T(8,128)(2,1)S(1)}, u32[]{:S(2)}, u32[]{:S(2)}) collective-permute-start(bf16[4,112,384]{2,1,0:T(8,128)(2,1)S(1)} %bitcast.51), channel_id=1, source_target_pairs={{0,256},{1,17},{2,258},{3,19},{4,260},{5,21},{6,262},{7,23},{8,264... | collective-permute-start | bytes 1032200 | tf_op jit(solution)/shard_map/ppermute | solution.py:289
  47.0 1.3 collective-permute-start
  48.3 10.0 %collective-permute-done.1 = bf16[4,112,384]{2,1,0:T(8,128)(2,1)S(1)} collective-permute-done((bf16[4,112,384]{2,1,0:T(8,128)(2,1)S(1)}, bf16[4,112,384]{2,1,0:T(8,128)(2,1)S(1)}, u32[]{:S(2)}, u32[]{:S(2)}) %collective-permute-start.1) | collective-permute-done | bytes 344096 | tf_op jit(solution)/shard_map/ppermute | solution.py:289
  58.2 0.1 pad_maximum_fusion.1.e0
  58.3 0.0 copy-start.3
  58.3 3.1 %collective-permute-start.4 = (bf16[2,4,112,384]{3,2,1,0:T(8,128)(2,1)S(1)}, bf16[2,4,112,384]{3,2,1,0:T(8,128)(2,1)S(1)}, u32[]{:S(2)}, u32[]{:S(2)}) collective-permute-start(bf16[2,4,112,384]{3,2,1,0:T(8,128)(2,1)S(1)} %pad_maximum_fusion.1.e0), channel_id=1, source_target_pairs={{0,8},{1,129},{2,10},{3,131},{4,12},{5,133},{6,14},{7,135},{8,16},... | collective-permute-start | bytes 2064392 | tf_op jit(solution)/shard_map/ppermute | solution.py:289
  61.4 0.0 collective-permute-done.3
  61.4 2.2 %collective-permute-done.2 = bf16[4,112,384]{2,1,0:T(8,128)(2,1)S(1)} collective-permute-done((bf16[4,112,384]{2,1,0:T(8,128)(2,1)S(1)}, bf16[4,112,384]{2,1,0:T(8,128)(2,1)S(1)}, u32[]{:S(2)}, u32[]{:S(2)}) %collective-permute-start.2) | collective-permute-done | bytes 344096 | tf_op jit(solution)/shard_map/ppermute | solution.py:289
  63.7 0.1 pad_maximum_fusion.2.l0
  63.8 0.0 copy-start.4
  63.8 5.2 %collective-permute-start.7 = (bf16[2,4,112,384]{3,2,1,0:T(8,128)(2,1)S(1)}, bf16[2,4,112,384]{3,2,1,0:T(8,128)(2,1)S(1)}, u32[]{:S(2)}, u32[]{:S(2)}) collective-permute-start(bf16[2,4,112,384]{3,2,1,0:T(8,128)(2,1)S(1)} %pad_maximum_fusion.2.l0), channel_id=1, source_target_pairs={{0,24},{1,385},{2,26},{3,387},{4,28},{5,389},{6,30},{7,391},{8,0},... | collective-permute-start | bytes 2064392 | tf_op jit(solution)/shard_map/ppermute | solution.py:289
  69.0 2.3 %collective-permute-start.9 = (bf16[2,4,112,384]{3,2,1,0:T(8,128)(2,1)S(1)}, bf16[2,4,112,384]{3,2,1,0:T(8,128)(2,1)S(1)}, u32[]{:S(2)}, u32[]{:S(2)}) collective-permute-start(bf16[2,4,112,384]{3,2,1,0:T(8,128)(2,1)S(1)} %pad_maximum_fusion.1.e0), channel_id=1, source_target_pairs={{0,24},{1,385},{2,26},{3,387},{4,28},{5,389},{6,30},{7,391},{8,0},... | collective-permute-start | bytes 2064392 | tf_op jit(solution)/shard_map/ppermute | solution.py:289
  71.3 3.0 %collective-permute-start.5 = (bf16[2,4,112,384]{3,2,1,0:T(8,128)(2,1)S(1)}, bf16[2,4,112,384]{3,2,1,0:T(8,128)(2,1)S(1)}, u32[]{:S(2)}, u32[]{:S(2)}) collective-permute-start(bf16[2,4,112,384]{3,2,1,0:T(8,128)(2,1)S(1)} %pad_maximum_fusion.2.l0), channel_id=1, source_target_pairs={{0,8},{1,129},{2,10},{3,131},{4,12},{5,133},{6,14},{7,135},{8,16},... | collective-permute-start | bytes 2064392 | tf_op jit(solution)/shard_map/ppermute | solution.py:289
  74.3 0.0 collective-permute-done.4.e1
  74.3 0.0 copy-start.6
  74.3 1.9 collective-permute-start.6
  76.3 0.6 collective-permute-done.7.l3
  76.9 5.3 %collective-permute-start.8 = (bf16[2,4,112,384]{3,2,1,0:T(8,128)(2,1)S(1)}, bf16[2,4,112,384]{3,2,1,0:T(8,128)(2,1)}, u32[]{:S(2)}, u32[]{:S(2)}) collective-permute-start(bf16[2,4,112,384]{3,2,1,0:T(8,128)(2,1)S(1)} %collective-permute-done.7.l3), channel_id=1, source_target_pairs={{0,24},{1,385},{2,26},{3,387},{4,28},{5,389},{6,30},{7,391},{8,0},... | collective-permute-start | bytes 2064392 | tf_op jit(solution)/shard_map/ppermute | solution.py:289
  82.2 2.1 %collective-permute-done.9.e3 = bf16[2,4,112,384]{3,2,1,0:T(8,128)(2,1)S(1)} collective-permute-done((bf16[2,4,112,384]{3,2,1,0:T(8,128)(2,1)S(1)}, bf16[2,4,112,384]{3,2,1,0:T(8,128)(2,1)S(1)}, u32[]{:S(2)}, u32[]{:S(2)}) %collective-permute-start.9) | collective-permute-done | bytes 688160 | tf_op jit(solution)/shard_map/ppermute | solution.py:289
  84.2 0.2 collective-permute-done.5.l1
  84.5 0.0 collective-permute-done.other_space
  84.5 7.1 %collective-permute-done.6.e2 = bf16[2,4,112,384]{3,2,1,0:T(8,128)(2,1)S(1)} collective-permute-done((bf16[2,4,112,384]{3,2,1,0:T(8,128)(2,1)S(1)}, bf16[2,4,112,384]{3,2,1,0:T(8,128)(2,1)S(1)}, u32[]{:S(2)}, u32[]{:S(2)}) %collective-permute-start.6) | collective-permute-done | bytes 688160 | tf_op jit(solution)/shard_map/ppermute | solution.py:289
  91.5 0.0 copy-done.6
  91.5 0.0 copy-done.7
  91.6 0.0 copy-done.8
  91.6 0.9 copy-done.10
  92.4 0.0 collective-permute-done.8.l2
  92.4 0.0 all-to-all-done
  92.5 1.2 copy-done.2
  93.6 2.5 %collective-permute-start.10 = (bf16[128,6144]{1,0:T(8,128)(2,1)S(1)}, bf16[128,6144]{1,0:T(8,128)(2,1)}, u32[]{:S(2)}, u32[]{:S(2)}) collective-permute-start(bf16[128,6144]{1,0:T(8,128)(2,1)S(1)} %bitcast.45), channel_id=1, source_target_pairs={{1,0},{3,2},{5,4},{7,6},{9,8},{11,10},{13,12},{15,14},{17,16},{19,... | collective-permute-start | bytes 4718600 | tf_op jit(solution)/shard_map/ppermute | solution.py:289
  96.1 0.6 pad_add_fusion.place
  96.7 1.4 collective-permute-done.10.other_time
  98.1 7.0 %shard_map.118 = (bf16[12,256,256]{2,1,0:T(8,128)(2,1)}, bf16[256,1536]{1,0:T(8,128)(2,1)}, bf16[16,96,128]{2,1,0:T(8,128)(2,1)}, bf16[256,128]{1,0:T(8,128)(2,1)}, bf16[1536,128]{1,0:T(8,128)(2,1)}) custom-call(s32[4]{0:T(128)} %pad_add_fusion.place, bf16[2,4,112,384]{3,2,1,0:T(8,128)(2,1)} %copy-done.3, bf16[2,4,112,384]{3,2,1,0:T(8,128)(2,1)} %copy-done.4, ...), custom_call_target="tpu_custom_call" | custom-call | flops 800000000 | bytes 10000000 | tf_op jit(solution)/shard_map/pallas_call | solution.py:343
  105.1 5.0 %all-to-all-start.1 = ((bf16[16,96,128]{2,1,0:T(8,128)(2,1)}), bf16[16,96,128]{2,1,0:T(8,128)(2,1)S(1)}, u32[]{:S(2)}, u32[]{:S(2)}) async-start(bf16[16,96,128]{2,1,0:T(8,128)(2,1)} %bitcast.57), calls=%async_computation.1 | async-start | bytes 786432 | tf_op jit(solution)/shard_map/all_to_all | solution.py:313
  110.1 9.1 %shard_map.119 = (bf16[256,1536]{1,0:T(8,128)(2,1)}, bf16[256,1536]{1,0:T(8,128)(2,1)}) custom-call(s32[4]{0:T(128)} %pad_add_fusion.place, bf16[2,4,112,384]{3,2,1,0:T(8,128)(2,1)} %copy-done.3, bf16[2,4,112,384]{3,2,1,0:T(8,128)(2,1)} %copy-done.4, bf16[2,4,112,384]{3,2,1,0:T(8,128)(2,1)} %copy-done.6, bf16[2,4,112,384]{3,2,1,0:T(8,128)(2,1)} %copy-done.9, ...), custom_call_target="tpu_custom_call" | custom-call | flops 4000000000 | bytes 20000000 | tf_op jit(solution)/shard_map/pallas_call | solution.py:372
  119.2 0.1 all-to-all-done.1
  119.4 0.1 reduce_sum.24
  119.4 0.7 broadcast_in_dim.8
  120.1 11.0 %all-to-all-start.2 = ((bf16[16,24,128]{2,1,0:T(8,128)(2,1)}), bf16[16,24,128]{2,1,0:T(8,128)(2,1)S(1)}, u32[]{:S(2)}, u32[]{:S(2)}) async-start(bf16[16,24,128]{2,1,0:T(8,128)(2,1)} %bitcast.21), calls=%async_computation.2 | async-start | bytes 196608 | tf_op jit(solution)/shard_map/all_to_all | solution.py:313
  131.1 9.7 %shard_map.120 = (bf16[128,6144]{1,0:T(8,128)(2,1)}, bf16[128,6144]{1,0:T(8,128)(2,1)}) custom-call(s32[4]{0:T(128)} %pad_add_fusion.place, bf16[128,6144]{1,0:T(8,128)(2,1)} %bitcast.48, bf16[128,6144]{1,0:T(8,128)(2,1)} %pad_maximum_fusion.space, bf16[128,6144]{1,0:T(8,128)(2,1)} %collective-permute-done.10.other_time, bf16[128,6144]{1,0:T(8,128)(2,1)} %copy-done.5, ...), custom_call_target="tpu_custom_call" | custom-call | flops 4000000000 | bytes 20000000 | tf_op jit(solution)/shard_map/pallas_call | solution.py:398
  140.7 2.2 %all-to-all-done.2 = bf16[16,24,128]{2,1,0:T(8,128)(2,1)S(1)} async-done(((bf16[16,24,128]{2,1,0:T(8,128)(2,1)}), bf16[16,24,128]{2,1,0:T(8,128)(2,1)S(1)}, u32[]{:S(2)}, u32[]{:S(2)}) %all-to-all-start.2) | async-done | bytes 98336 | tf_op jit(solution)/shard_map/all_to_all | solution.py:313
  142.9 5.0 %collective-permute-start.11 = (bf16[128,6144]{1,0:T(8,128)(2,1)}, bf16[128,6144]{1,0:T(8,128)(2,1)}, u32[]{:S(2)}, u32[]{:S(2)}) collective-permute-start(bf16[128,6144]{1,0:T(8,128)(2,1)} %get-tuple-element.53), channel_id=1, source_target_pairs={{0,1},{1,0},{2,3},{3,2},{4,5},{5,4},{6,7},{7,6},{8,9},{9,8},{10,11... | collective-permute-start | bytes 4718600 | tf_op jit(solution)/shard_map/ppermute | solution.py:289
  147.9 3.4 %collective-permute-done.11.on_second = bf16[128,6144]{1,0:T(8,128)(2,1)} collective-permute-done((bf16[128,6144]{1,0:T(8,128)(2,1)}, bf16[128,6144]{1,0:T(8,128)(2,1)}, u32[]{:S(2)}, u32[]{:S(2)}) %collective-permute-start.11) | collective-permute-done | bytes 1572896 | tf_op jit(solution)/shard_map/ppermute | solution.py:289
  151.3 2.9 %shard_map.121 = bf16[128,6144]{1,0:T(8,128)(2,1)} custom-call(s32[4]{0:T(128)} %pad_add_fusion.place, bf16[128,6144]{1,0:T(8,128)(2,1)} %get-tuple-element.54.on_first, bf16[128,6144]{1,0:T(8,128)(2,1)} %collective-permute-done.11.on_second), custom_call_target="tpu_custom_call" | custom-call | flops 1000000 | bytes 3000000 | tf_op jit(solution)/shard_map/pallas_call | solution.py:417
  154.2 5.0 %all-to-all-start.3 = ((bf16[16,8,6144]{2,1,0:T(8,128)(2,1)}), bf16[16,8,6144]{2,1,0:T(8,128)(2,1)}, u32[]{:S(2)}, u32[]{:S(2)}) async-start(bf16[16,8,6144]{2,1,0:T(8,128)(2,1)} %bitcast.44), calls=%async_computation.3 | async-start | bytes 3145728 | tf_op jit(solution)/shard_map/all_to_all | solution.py:313
  159.2 17.1 %all_gather.11 = bf16[96,128]{1,0:T(8,128)(2,1)S(1)} all-gather(bf16[24,128]{1,0:T(8,128)(2,1)S(1)} %reduce_sum.25), channel_id=1, replica_groups=mesh['x'=4,'zh'=4,'y'=4,'zl'=4,'c'=2] {'y'}, dimensions={0}, use_global_device_ids=true | all-gather | bytes 30720 | tf_op jit(solution)/shard_map/all_gather | solution.py:423
  176.3 5.6 %collective-permute-start.12 = (bf16[96,128]{1,0:T(8,128)(2,1)S(1)}, bf16[96,128]{1,0:T(8,128)(2,1)S(1)}, u32[]{:S(2)}, u32[]{:S(2)}) collective-permute-start(bf16[96,128]{1,0:T(8,128)(2,1)S(1)} %all_gather.11), channel_id=1, source_target_pairs={{0,1},{1,0},{2,3},{3,2},{4,5},{5,4},{6,7},{7,6},{8,9},{9,8},{10,11... | collective-permute-start | bytes 73736 | tf_op jit(solution)/shard_map/ppermute | solution.py:289
  182.0 0.8 collective-permute-done.12
  182.8 0.1 slice_bitcast_fusion
  182.9 0.7 copy.20
  183.6 0.7 copy.19
  184.3 1.4 broadcast_select_fusion
  185.7 12.1 %all-to-all-done.3 = bf16[16,8,6144]{2,1,0:T(8,128)(2,1)} async-done(((bf16[16,8,6144]{2,1,0:T(8,128)(2,1)}), bf16[16,8,6144]{2,1,0:T(8,128)(2,1)}, u32[]{:S(2)}, u32[]{:S(2)}) %all-to-all-start.3) | async-done | bytes 1572896 | tf_op jit(solution)/shard_map/all_to_all | solution.py:313
  197.8 3.2 %fusion.3 = (bf16[1,1,128,1536]{3,2,1,0:T(8,128)(2,1)}, bf16[1,1,128,1536]{3,2,1,0:T(8,128)(2,1)}, bf16[1,1,128,1536]{3,2,1,0:T(8,128)(2,1)}, bf16[1,1,128,1536]{3,2,1,0:T(8,128)(2,1)}) fusion(bf16[128,6144]{1,0:T(8,128)(2,1)} %bitcast.23, bf16[128,6144]{1,0:T(8,128)(2,1)} %broadcast_select_fusion), kind=kLoop, calls=%fused_computation.11 | loop fusion | flops 3145728 | bytes 4718592 | tf_op jit(solution)/shard_map/reshape | solution.py:431
  (18 shorter events, 0.1 us)
Async XLA Ops:
  0.6 1.9 copy-start
  31.7 60.7 %all-to-all-start = ((bf16[16,8,6144]{2,1,0:T(8,128)(2,1)}), bf16[16,8,6144]{2,1,0:T(8,128)(2,1)S(1)}, u32[]{:S(2)}, u32[]{:S(2)}) async-start(bf16[16,8,6144]{2,1,0:T(8,128)(2,1)} %bitcast.13), calls=%async_computation | async-start | bytes 3145728 | tf_op jit(solution)/shard_map/all_to_all | solution.py:313
  36.9 21.3 %collective-permute-start.1 = (bf16[4,112,384]{2,1,0:T(8,128)(2,1)S(1)}, bf16[4,112,384]{2,1,0:T(8,128)(2,1)S(1)}, u32[]{:S(2)}, u32[]{:S(2)}) collective-permute-start(bf16[4,112,384]{2,1,0:T(8,128)(2,1)S(1)} %bitcast.49), channel_id=1, source_target_pairs={{0,128},{1,9},{2,130},{3,11},{4,132},{5,13},{6,134},{7,15},{8,136}... | collective-permute-start | bytes 1032200 | tf_op jit(solution)/shard_map/ppermute | solution.py:289
  40.2 21.3 %collective-permute-start.3 = (bf16[4,112,384]{2,1,0:T(8,128)(2,1)S(1)}, bf16[4,112,384]{2,1,0:T(8,128)(2,1)S(1)}, u32[]{:S(2)}, u32[]{:S(2)}) collective-permute-start(bf16[4,112,384]{2,1,0:T(8,128)(2,1)S(1)} %bitcast.50), channel_id=1, source_target_pairs={{0,384},{1,25},{2,386},{3,27},{4,388},{5,29},{6,390},{7,31},{8,392... | collective-permute-start | bytes 1032200 | tf_op jit(solution)/shard_map/ppermute | solution.py:289
  43.4 20.3 %collective-permute-start.2 = (bf16[4,112,384]{2,1,0:T(8,128)(2,1)S(1)}, bf16[4,112,384]{2,1,0:T(8,128)(2,1)S(1)}, u32[]{:S(2)}, u32[]{:S(2)}) collective-permute-start(bf16[4,112,384]{2,1,0:T(8,128)(2,1)S(1)} %bitcast.51), channel_id=1, source_target_pairs={{0,256},{1,17},{2,258},{3,19},{4,260},{5,21},{6,262},{7,23},{8,264... | collective-permute-start | bytes 1032200 | tf_op jit(solution)/shard_map/ppermute | solution.py:289
  47.0 37.5 %collective-permute-start = (bf16[128,6144]{1,0:T(8,128)(2,1)}, bf16[128,6144]{1,0:T(8,128)(2,1)S(1)}, u32[]{:S(2)}, u32[]{:S(2)}) collective-permute-start(bf16[128,6144]{1,0:T(8,128)(2,1)} %pad_maximum_fusion.space), channel_id=1, source_target_pairs={{0,1},{2,3},{4,5},{6,7},{8,9},{10,11},{12,13},{14,15},{16,17},{18,... | collective-permute-start | bytes 4718600 | tf_op jit(solution)/shard_map/ppermute | solution.py:289
  58.3 39.8 %copy-start.3 = (bf16[2,4,112,384]{3,2,1,0:T(8,128)(2,1)}, bf16[2,4,112,384]{3,2,1,0:T(8,128)(2,1)S(1)}, u32[]{:S(2)}) copy-start(bf16[2,4,112,384]{3,2,1,0:T(8,128)(2,1)S(1)} %pad_maximum_fusion.1.e0) | copy-start | bytes 2064388
  58.3 16.0 %collective-permute-start.4 = (bf16[2,4,112,384]{3,2,1,0:T(8,128)(2,1)S(1)}, bf16[2,4,112,384]{3,2,1,0:T(8,128)(2,1)S(1)}, u32[]{:S(2)}, u32[]{:S(2)}) collective-permute-start(bf16[2,4,112,384]{3,2,1,0:T(8,128)(2,1)S(1)} %pad_maximum_fusion.1.e0), channel_id=1, source_target_pairs={{0,8},{1,129},{2,10},{3,131},{4,12},{5,133},{6,14},{7,135},{8,16},... | collective-permute-start | bytes 2064392 | tf_op jit(solution)/shard_map/ppermute | solution.py:289
  63.8 34.3 %copy-start.4 = (bf16[2,4,112,384]{3,2,1,0:T(8,128)(2,1)}, bf16[2,4,112,384]{3,2,1,0:T(8,128)(2,1)S(1)}, u32[]{:S(2)}) copy-start(bf16[2,4,112,384]{3,2,1,0:T(8,128)(2,1)S(1)} %pad_maximum_fusion.2.l0) | copy-start | bytes 2064388
  63.8 13.1 %collective-permute-start.7 = (bf16[2,4,112,384]{3,2,1,0:T(8,128)(2,1)S(1)}, bf16[2,4,112,384]{3,2,1,0:T(8,128)(2,1)S(1)}, u32[]{:S(2)}, u32[]{:S(2)}) collective-permute-start(bf16[2,4,112,384]{3,2,1,0:T(8,128)(2,1)S(1)} %pad_maximum_fusion.2.l0), channel_id=1, source_target_pairs={{0,24},{1,385},{2,26},{3,387},{4,28},{5,389},{6,30},{7,391},{8,0},... | collective-permute-start | bytes 2064392 | tf_op jit(solution)/shard_map/ppermute | solution.py:289
  69.0 15.2 %collective-permute-start.9 = (bf16[2,4,112,384]{3,2,1,0:T(8,128)(2,1)S(1)}, bf16[2,4,112,384]{3,2,1,0:T(8,128)(2,1)S(1)}, u32[]{:S(2)}, u32[]{:S(2)}) collective-permute-start(bf16[2,4,112,384]{3,2,1,0:T(8,128)(2,1)S(1)} %pad_maximum_fusion.1.e0), channel_id=1, source_target_pairs={{0,24},{1,385},{2,26},{3,387},{4,28},{5,389},{6,30},{7,391},{8,0},... | collective-permute-start | bytes 2064392 | tf_op jit(solution)/shard_map/ppermute | solution.py:289
  71.3 13.2 %collective-permute-start.5 = (bf16[2,4,112,384]{3,2,1,0:T(8,128)(2,1)S(1)}, bf16[2,4,112,384]{3,2,1,0:T(8,128)(2,1)S(1)}, u32[]{:S(2)}, u32[]{:S(2)}) collective-permute-start(bf16[2,4,112,384]{3,2,1,0:T(8,128)(2,1)S(1)} %pad_maximum_fusion.2.l0), channel_id=1, source_target_pairs={{0,8},{1,129},{2,10},{3,131},{4,12},{5,133},{6,14},{7,135},{8,16},... | collective-permute-start | bytes 2064392 | tf_op jit(solution)/shard_map/ppermute | solution.py:289
  74.3 17.2 %copy-start.6 = (bf16[2,4,112,384]{3,2,1,0:T(8,128)(2,1)}, bf16[2,4,112,384]{3,2,1,0:T(8,128)(2,1)S(1)}, u32[]{:S(2)}) copy-start(bf16[2,4,112,384]{3,2,1,0:T(8,128)(2,1)S(1)} %collective-permute-done.4.e1) | copy-start | bytes 2064388
  74.3 17.2 %collective-permute-start.6 = (bf16[2,4,112,384]{3,2,1,0:T(8,128)(2,1)S(1)}, bf16[2,4,112,384]{3,2,1,0:T(8,128)(2,1)S(1)}, u32[]{:S(2)}, u32[]{:S(2)}) collective-permute-start(bf16[2,4,112,384]{3,2,1,0:T(8,128)(2,1)S(1)} %collective-permute-done.4.e1), channel_id=1, source_target_pairs={{0,8},{1,129},{2,10},{3,131},{4,12},{5,133},{6,14},{7,135},{8,16},... | collective-permute-start | bytes 2064392 | tf_op jit(solution)/shard_map/ppermute | solution.py:289
  76.9 14.7 %copy-start.7 = (bf16[2,4,112,384]{3,2,1,0:T(8,128)(2,1)}, bf16[2,4,112,384]{3,2,1,0:T(8,128)(2,1)S(1)}, u32[]{:S(2)}) copy-start(bf16[2,4,112,384]{3,2,1,0:T(8,128)(2,1)S(1)} %collective-permute-done.7.l3) | copy-start | bytes 2064388
  76.9 15.6 %collective-permute-start.8 = (bf16[2,4,112,384]{3,2,1,0:T(8,128)(2,1)S(1)}, bf16[2,4,112,384]{3,2,1,0:T(8,128)(2,1)}, u32[]{:S(2)}, u32[]{:S(2)}) collective-permute-start(bf16[2,4,112,384]{3,2,1,0:T(8,128)(2,1)S(1)} %collective-permute-done.7.l3), channel_id=1, source_target_pairs={{0,24},{1,385},{2,26},{3,387},{4,28},{5,389},{6,30},{7,391},{8,0},... | collective-permute-start | bytes 2064392 | tf_op jit(solution)/shard_map/ppermute | solution.py:289
  84.2 7.3 %copy-start.8 = (bf16[2,4,112,384]{3,2,1,0:T(8,128)(2,1)}, bf16[2,4,112,384]{3,2,1,0:T(8,128)(2,1)S(1)}, u32[]{:S(2)}) copy-start(bf16[2,4,112,384]{3,2,1,0:T(8,128)(2,1)S(1)} %collective-permute-done.9.e3) | copy-start | bytes 2064388
  84.5 7.1 %copy-start.9 = (bf16[2,4,112,384]{3,2,1,0:T(8,128)(2,1)}, bf16[2,4,112,384]{3,2,1,0:T(8,128)(2,1)S(1)}, u32[]{:S(2)}) copy-start(bf16[2,4,112,384]{3,2,1,0:T(8,128)(2,1)S(1)} %collective-permute-done.5.l1) | copy-start | bytes 2064388
  84.5 7.1 %copy-start.5 = (bf16[128,6144]{1,0:T(8,128)(2,1)}, bf16[128,6144]{1,0:T(8,128)(2,1)S(1)}, u32[]{:S(2)}) copy-start(bf16[128,6144]{1,0:T(8,128)(2,1)S(1)} %collective-permute-done.other_space) | copy-start | bytes 4718596
  91.6 0.9 copy-start.10
  92.4 1.2 copy-start.2
  93.6 4.4 %collective-permute-start.10 = (bf16[128,6144]{1,0:T(8,128)(2,1)S(1)}, bf16[128,6144]{1,0:T(8,128)(2,1)}, u32[]{:S(2)}, u32[]{:S(2)}) collective-permute-start(bf16[128,6144]{1,0:T(8,128)(2,1)S(1)} %bitcast.45), channel_id=1, source_target_pairs={{1,0},{3,2},{5,4},{7,6},{9,8},{11,10},{13,12},{15,14},{17,16},{19,... | collective-permute-start | bytes 4718600 | tf_op jit(solution)/shard_map/ppermute | solution.py:289
  105.1 14.2 %all-to-all-start.1 = ((bf16[16,96,128]{2,1,0:T(8,128)(2,1)}), bf16[16,96,128]{2,1,0:T(8,128)(2,1)S(1)}, u32[]{:S(2)}, u32[]{:S(2)}) async-start(bf16[16,96,128]{2,1,0:T(8,128)(2,1)} %bitcast.57), calls=%async_computation.1 | async-start | bytes 786432 | tf_op jit(solution)/shard_map/all_to_all | solution.py:313
  120.1 22.9 %all-to-all-start.2 = ((bf16[16,24,128]{2,1,0:T(8,128)(2,1)}), bf16[16,24,128]{2,1,0:T(8,128)(2,1)S(1)}, u32[]{:S(2)}, u32[]{:S(2)}) async-start(bf16[16,24,128]{2,1,0:T(8,128)(2,1)} %bitcast.21), calls=%async_computation.2 | async-start | bytes 196608 | tf_op jit(solution)/shard_map/all_to_all | solution.py:313
  142.9 8.3 %collective-permute-start.11 = (bf16[128,6144]{1,0:T(8,128)(2,1)}, bf16[128,6144]{1,0:T(8,128)(2,1)}, u32[]{:S(2)}, u32[]{:S(2)}) collective-permute-start(bf16[128,6144]{1,0:T(8,128)(2,1)} %get-tuple-element.53), channel_id=1, source_target_pairs={{0,1},{1,0},{2,3},{3,2},{4,5},{5,4},{6,7},{7,6},{8,9},{9,8},{10,11... | collective-permute-start | bytes 4718600 | tf_op jit(solution)/shard_map/ppermute | solution.py:289
  154.2 30.1 %copy-start.1 = (bf16[128,6144]{1,0:T(8,128)(2,1)S(1)}, bf16[128,6144]{1,0:T(8,128)(2,1)}, u32[]{:S(2)}) copy-start(bf16[128,6144]{1,0:T(8,128)(2,1)} %get-tuple-element.54.on_first) | copy-start | bytes 4718596
  154.2 43.6 %all-to-all-start.3 = ((bf16[16,8,6144]{2,1,0:T(8,128)(2,1)}), bf16[16,8,6144]{2,1,0:T(8,128)(2,1)}, u32[]{:S(2)}, u32[]{:S(2)}) async-start(bf16[16,8,6144]{2,1,0:T(8,128)(2,1)} %bitcast.44), calls=%async_computation.3 | async-start | bytes 3145728 | tf_op jit(solution)/shard_map/all_to_all | solution.py:313
  176.3 6.5 %collective-permute-start.12 = (bf16[96,128]{1,0:T(8,128)(2,1)S(1)}, bf16[96,128]{1,0:T(8,128)(2,1)S(1)}, u32[]{:S(2)}, u32[]{:S(2)}) collective-permute-start(bf16[96,128]{1,0:T(8,128)(2,1)S(1)} %all_gather.11), channel_id=1, source_target_pairs={{0,1},{1,0},{2,3},{3,2},{4,5},{5,4},{6,7},{7,6},{8,9},{9,8},{10,11... | collective-permute-start | bytes 73736 | tf_op jit(solution)/shard_map/ppermute | solution.py:289

commit v5 on v4

--- a/solution.py
+++ b/solution.py
@@ -414,19 +414,29 @@
     there, summed = lax.optimization_barrier((there, summed))
 
     other = permute(there, other_core)
-    back = call(
-        choose, shape((ROWS, WIDE)), [SM, HBM, HBM], HBM, [pltpu.VMEM((ROWS, WIDE), BF16), pltpu.SemaphoreType.DMA((8,))], 10**6, 3 * 10**6
-    )(place, here, other)
+    def by_core(on_first, on_second):
+        return call(
+            choose,
+            shape((ROWS, WIDE)),
+            [SM, HBM, HBM],
+            HBM,
+            [pltpu.VMEM((ROWS, WIDE), BF16), pltpu.SemaphoreType.DMA((8,))],
+            10**6,
+            3 * 10**6,
+        )(place, on_first, on_second)
+
+    back = by_core(here, other)
     back = exchange(back.reshape(16, 8, WIDE), ("y", "zl")).reshape(ROWS, WIDE)
 
     summed = summed.astype(F32).sum(0).astype(BF16)
     summed = lax.all_gather(summed, "y", tiled=True)
+    here, other, summed = lax.optimization_barrier((here, other, summed))
+    mine = by_core(other, here)
     pair = permute(summed, other_core)
     summed = jnp.stack([jnp.where(c == 0, pair, summed), jnp.where(c == 0, summed, pair)]).astype(F32)
     grad_up = jnp.swapaxes(summed[:, :, :RANK], 1, 2)
     grad_down = summed[:, :, RANK:]
 
-    mine = jnp.where(c == 0, other, here)
     total = [
         (mine[:, at : at + FEATURES].astype(F32) + back[:, at : at + FEATURES].astype(F32)).astype(BF16).reshape(out_dims)
         for at in (COT, 0, FEATURES, 2 * FEATURES)

time: 202 us -> 202 us (level)
  Pallas kernels: 28.7 us -> 31.7 us
    pallas_call x1 -> x2, Pallas kernels: 2.92 us -> 5.87 us  [by_core(): call(choose, shape((ROWS, WIDE)), [SM, HBM, HBM], HBM, [pltpu.VMEM((ROWS,...]
    unnamed x26 -> x24, local copies, waits for them, and re-layouts: 5.27 us -> 5.27 us
  transfers between devices with their start and end apart: 17 -> 17, of which waited for: 12 -> 11; matrix products, arithmetic and copies ran while one was open for 2% -> 1% of each run, Pallas kernels for 9% -> 11%
where the time goes in v5:
time: 202 us; the launch traced here: 201 us
  starting transfers between devices  71.3 us (35%)
  blocking collectives  43.5 us (22%)
  waiting for transfers between devices  40.6 us (20%)
  Pallas kernels  31.7 us (16%)
  other arithmetic  6.87 us (3%)
  local copies, waits for them, and re-layouts  6.03 us (3%)
    ppermute x13, starting transfers between devices, permute(): return lax.ppermute(value, AXES, pairs)  45.3 us
    ppermute x13, waiting for transfers between devices, permute(): return lax.ppermute(value, AXES, pairs)  26.9 us
    all_gather x1, blocking collectives, local(): held = lax.all_gather(first, 'zh')  26.4 us
    all_to_all x4, starting transfers between devices, exchange(): return lax.all_to_all(value, axes, split_axis=0, concat_axis=0, tiled=True)  26.1 us
    all_gather x1, blocking collectives, local(): summed = lax.all_gather(summed, 'y', tiled=True)  17.1 us
    all_to_all x4, waiting for transfers between devices, exchange(): return lax.all_to_all(value, axes, split_axis=0, concat_axis=0, tiled=True)  13.7 us
    pallas_call x1, Pallas kernels, local(): call(backward, (shape((ROWS, WIDE)), shape((ROWS, WIDE))), [SM] + [HBM] *...  9.64 us
    pallas_call x1, Pallas kernels, local(): call(project, (shape((BOTH, FEATURES)), shape((BOTH, FEATURES))), [SM] +...  9.11 us
  transfers between devices with their start and end apart: 17, of which 11 were waited for; matrix products, arithmetic and copies ran while one was open for 1% of the time, Pallas kernels for 11%

profile of v5, /device:TPU:1, one launch (start us, length us, event | category | flops | bytes accessed | tf_op | source)
XLA Modules:
  0.0 201.0 jit_solution(17386426991789223361)
XLA Ops:
  0.6 0.0 copy-start
  0.7 0.9 copy.17
  1.6 0.9 copy.16
  2.5 0.1 fusion.4
  2.6 0.0 copy-done
  2.6 26.4 %all-gather = bf16[448,384]{1,0:T(8,128)(2,1)S(1)} all-gather(bf16[112,384]{1,0:T(8,128)(2,1)S(1)} %pad_maximum_fusion.3), channel_id=2, replica_groups=mesh['x'=4,'zh'=4,'y'=4,'zl'=4,'c'=2] {'zh'}, dimensions={0}, use_global_device_ids=true | all-gather | bytes 430080 | tf_op jit(solution)/shard_map/all_gather | solution.py:328
  29.0 2.7 %pad_maximum_fusion.space = bf16[128,6144]{1,0:T(8,128)(2,1)} fusion(bf16[128,1536]{1,0:T(8,128)(2,1)} %bitcast.53, bf16[128,1536]{1,0:T(8,128)(2,1)} %bitcast.54, bf16[128,1536]{1,0:T(8,128)(2,1)} %bitcast.55, bf16[128,1536]{1,0:T(8,128)(2,1)} %bitcast.56), kind=kLoop, calls=%fused_computation | loop fusion | flops 6291456 | bytes 3145728 | tf_op jit(solution)/shard_map/concatenate | solution.py:320
  31.7 5.2 %all-to-all-start = ((bf16[16,8,6144]{2,1,0:T(8,128)(2,1)}), bf16[16,8,6144]{2,1,0:T(8,128)(2,1)S(1)}, u32[]{:S(2)}, u32[]{:S(2)}) async-start(bf16[16,8,6144]{2,1,0:T(8,128)(2,1)} %bitcast.13), calls=%async_computation | async-start | bytes 3145728 | tf_op jit(solution)/shard_map/all_to_all | solution.py:313
  36.9 3.3 %collective-permute-start.1 = (bf16[4,112,384]{2,1,0:T(8,128)(2,1)S(1)}, bf16[4,112,384]{2,1,0:T(8,128)(2,1)S(1)}, u32[]{:S(2)}, u32[]{:S(2)}) collective-permute-start(bf16[4,112,384]{2,1,0:T(8,128)(2,1)S(1)} %bitcast.49), channel_id=1, source_target_pairs={{0,128},{1,9},{2,130},{3,11},{4,132},{5,13},{6,134},{7,15},{8,136}... | collective-permute-start | bytes 1032200 | tf_op jit(solution)/shard_map/ppermute | solution.py:289
  40.2 3.2 %collective-permute-start.3 = (bf16[4,112,384]{2,1,0:T(8,128)(2,1)S(1)}, bf16[4,112,384]{2,1,0:T(8,128)(2,1)S(1)}, u32[]{:S(2)}, u32[]{:S(2)}) collective-permute-start(bf16[4,112,384]{2,1,0:T(8,128)(2,1)S(1)} %bitcast.50), channel_id=1, source_target_pairs={{0,384},{1,25},{2,386},{3,27},{4,388},{5,29},{6,390},{7,31},{8,392... | collective-permute-start | bytes 1032200 | tf_op jit(solution)/shard_map/ppermute | solution.py:289
  43.4 3.6 %collective-permute-start.2 = (bf16[4,112,384]{2,1,0:T(8,128)(2,1)S(1)}, bf16[4,112,384]{2,1,0:T(8,128)(2,1)S(1)}, u32[]{:S(2)}, u32[]{:S(2)}) collective-permute-start(bf16[4,112,384]{2,1,0:T(8,128)(2,1)S(1)} %bitcast.51), channel_id=1, source_target_pairs={{0,256},{1,17},{2,258},{3,19},{4,260},{5,21},{6,262},{7,23},{8,264... | collective-permute-start | bytes 1032200 | tf_op jit(solution)/shard_map/ppermute | solution.py:289
  47.0 1.3 collective-permute-start
  48.3 10.0 %collective-permute-done.1 = bf16[4,112,384]{2,1,0:T(8,128)(2,1)S(1)} collective-permute-done((bf16[4,112,384]{2,1,0:T(8,128)(2,1)S(1)}, bf16[4,112,384]{2,1,0:T(8,128)(2,1)S(1)}, u32[]{:S(2)}, u32[]{:S(2)}) %collective-permute-start.1) | collective-permute-done | bytes 344096 | tf_op jit(solution)/shard_map/ppermute | solution.py:289
  58.2 0.1 pad_maximum_fusion.1.e0
  58.3 0.0 copy-start.2
  58.3 3.1 %collective-permute-start.4 = (bf16[2,4,112,384]{3,2,1,0:T(8,128)(2,1)S(1)}, bf16[2,4,112,384]{3,2,1,0:T(8,128)(2,1)S(1)}, u32[]{:S(2)}, u32[]{:S(2)}) collective-permute-start(bf16[2,4,112,384]{3,2,1,0:T(8,128)(2,1)S(1)} %pad_maximum_fusion.1.e0), channel_id=1, source_target_pairs={{0,8},{1,129},{2,10},{3,131},{4,12},{5,133},{6,14},{7,135},{8,16},... | collective-permute-start | bytes 2064392 | tf_op jit(solution)/shard_map/ppermute | solution.py:289
  61.4 0.0 collective-permute-done.3
  61.5 2.2 %collective-permute-done.2 = bf16[4,112,384]{2,1,0:T(8,128)(2,1)S(1)} collective-permute-done((bf16[4,112,384]{2,1,0:T(8,128)(2,1)S(1)}, bf16[4,112,384]{2,1,0:T(8,128)(2,1)S(1)}, u32[]{:S(2)}, u32[]{:S(2)}) %collective-permute-start.2) | collective-permute-done | bytes 344096 | tf_op jit(solution)/shard_map/ppermute | solution.py:289
  63.7 0.1 pad_maximum_fusion.2.l0
  63.8 0.0 copy-start.3
  63.8 5.2 %collective-permute-start.7 = (bf16[2,4,112,384]{3,2,1,0:T(8,128)(2,1)S(1)}, bf16[2,4,112,384]{3,2,1,0:T(8,128)(2,1)S(1)}, u32[]{:S(2)}, u32[]{:S(2)}) collective-permute-start(bf16[2,4,112,384]{3,2,1,0:T(8,128)(2,1)S(1)} %pad_maximum_fusion.2.l0), channel_id=1, source_target_pairs={{0,24},{1,385},{2,26},{3,387},{4,28},{5,389},{6,30},{7,391},{8,0},... | collective-permute-start | bytes 2064392 | tf_op jit(solution)/shard_map/ppermute | solution.py:289
  69.0 2.3 %collective-permute-start.9 = (bf16[2,4,112,384]{3,2,1,0:T(8,128)(2,1)S(1)}, bf16[2,4,112,384]{3,2,1,0:T(8,128)(2,1)S(1)}, u32[]{:S(2)}, u32[]{:S(2)}) collective-permute-start(bf16[2,4,112,384]{3,2,1,0:T(8,128)(2,1)S(1)} %pad_maximum_fusion.1.e0), channel_id=1, source_target_pairs={{0,24},{1,385},{2,26},{3,387},{4,28},{5,389},{6,30},{7,391},{8,0},... | collective-permute-start | bytes 2064392 | tf_op jit(solution)/shard_map/ppermute | solution.py:289
  71.3 3.0 %collective-permute-start.5 = (bf16[2,4,112,384]{3,2,1,0:T(8,128)(2,1)S(1)}, bf16[2,4,112,384]{3,2,1,0:T(8,128)(2,1)S(1)}, u32[]{:S(2)}, u32[]{:S(2)}) collective-permute-start(bf16[2,4,112,384]{3,2,1,0:T(8,128)(2,1)S(1)} %pad_maximum_fusion.2.l0), channel_id=1, source_target_pairs={{0,8},{1,129},{2,10},{3,131},{4,12},{5,133},{6,14},{7,135},{8,16},... | collective-permute-start | bytes 2064392 | tf_op jit(solution)/shard_map/ppermute | solution.py:289
  74.3 0.0 collective-permute-done.4.e1
  74.3 0.0 copy-start.5
  74.3 1.9 collective-permute-start.6
  76.3 0.6 collective-permute-done.7.l3
  76.9 5.3 %collective-permute-start.8 = (bf16[2,4,112,384]{3,2,1,0:T(8,128)(2,1)S(1)}, bf16[2,4,112,384]{3,2,1,0:T(8,128)(2,1)}, u32[]{:S(2)}, u32[]{:S(2)}) collective-permute-start(bf16[2,4,112,384]{3,2,1,0:T(8,128)(2,1)S(1)} %collective-permute-done.7.l3), channel_id=1, source_target_pairs={{0,24},{1,385},{2,26},{3,387},{4,28},{5,389},{6,30},{7,391},{8,0},... | collective-permute-start | bytes 2064392 | tf_op jit(solution)/shard_map/ppermute | solution.py:289
  82.2 2.1 %collective-permute-done.9.e3 = bf16[2,4,112,384]{3,2,1,0:T(8,128)(2,1)S(1)} collective-permute-done((bf16[2,4,112,384]{3,2,1,0:T(8,128)(2,1)S(1)}, bf16[2,4,112,384]{3,2,1,0:T(8,128)(2,1)S(1)}, u32[]{:S(2)}, u32[]{:S(2)}) %collective-permute-start.9) | collective-permute-done | bytes 688160 | tf_op jit(solution)/shard_map/ppermute | solution.py:289
  84.2 0.2 collective-permute-done.5.l1
  84.5 0.0 collective-permute-done.other_space
  84.5 7.1 %collective-permute-done.6.e2 = bf16[2,4,112,384]{3,2,1,0:T(8,128)(2,1)S(1)} collective-permute-done((bf16[2,4,112,384]{3,2,1,0:T(8,128)(2,1)S(1)}, bf16[2,4,112,384]{3,2,1,0:T(8,128)(2,1)S(1)}, u32[]{:S(2)}, u32[]{:S(2)}) %collective-permute-start.6) | collective-permute-done | bytes 688160 | tf_op jit(solution)/shard_map/ppermute | solution.py:289
  91.6 0.0 copy-done.5
  91.6 0.0 copy-done.6
  91.6 0.0 copy-done.7
  91.6 0.8 copy-done.9
  92.4 0.0 collective-permute-done.8.l2
  92.4 0.0 all-to-all-done
  92.4 1.2 copy-done.1
  93.6 2.5 %collective-permute-start.10 = (bf16[128,6144]{1,0:T(8,128)(2,1)S(1)}, bf16[128,6144]{1,0:T(8,128)(2,1)}, u32[]{:S(2)}, u32[]{:S(2)}) collective-permute-start(bf16[128,6144]{1,0:T(8,128)(2,1)S(1)} %bitcast.45), channel_id=1, source_target_pairs={{1,0},{3,2},{5,4},{7,6},{9,8},{11,10},{13,12},{15,14},{17,16},{19,... | collective-permute-start | bytes 4718600 | tf_op jit(solution)/shard_map/ppermute | solution.py:289
  96.1 0.6 pad_add_fusion.place
  96.7 1.4 collective-permute-done.10.other_time
  98.1 7.0 %shard_map.118 = (bf16[12,256,256]{2,1,0:T(8,128)(2,1)}, bf16[256,1536]{1,0:T(8,128)(2,1)}, bf16[16,96,128]{2,1,0:T(8,128)(2,1)}, bf16[256,128]{1,0:T(8,128)(2,1)}, bf16[1536,128]{1,0:T(8,128)(2,1)}) custom-call(s32[4]{0:T(128)} %pad_add_fusion.place, bf16[2,4,112,384]{3,2,1,0:T(8,128)(2,1)} %copy-done.2, bf16[2,4,112,384]{3,2,1,0:T(8,128)(2,1)} %copy-done.3, ...), custom_call_target="tpu_custom_call" | custom-call | flops 800000000 | bytes 10000000 | tf_op jit(solution)/shard_map/pallas_call | solution.py:343
  105.1 5.0 %all-to-all-start.1 = ((bf16[16,96,128]{2,1,0:T(8,128)(2,1)}), bf16[16,96,128]{2,1,0:T(8,128)(2,1)S(1)}, u32[]{:S(2)}, u32[]{:S(2)}) async-start(bf16[16,96,128]{2,1,0:T(8,128)(2,1)} %bitcast.57), calls=%async_computation.1 | async-start | bytes 786432 | tf_op jit(solution)/shard_map/all_to_all | solution.py:313
  110.1 9.1 %shard_map.119 = (bf16[256,1536]{1,0:T(8,128)(2,1)}, bf16[256,1536]{1,0:T(8,128)(2,1)}) custom-call(s32[4]{0:T(128)} %pad_add_fusion.place, bf16[2,4,112,384]{3,2,1,0:T(8,128)(2,1)} %copy-done.2, bf16[2,4,112,384]{3,2,1,0:T(8,128)(2,1)} %copy-done.3, bf16[2,4,112,384]{3,2,1,0:T(8,128)(2,1)} %copy-done.5, bf16[2,4,112,384]{3,2,1,0:T(8,128)(2,1)} %copy-done.8, ...), custom_call_target="tpu_custom_call" | custom-call | flops 4000000000 | bytes 20000000 | tf_op jit(solution)/shard_map/pallas_call | solution.py:372
  119.3 0.1 all-to-all-done.1
  119.4 0.1 reduce_sum.24
  119.4 0.7 broadcast_in_dim.8
  120.1 11.0 %all-to-all-start.2 = ((bf16[16,24,128]{2,1,0:T(8,128)(2,1)}), bf16[16,24,128]{2,1,0:T(8,128)(2,1)S(1)}, u32[]{:S(2)}, u32[]{:S(2)}) async-start(bf16[16,24,128]{2,1,0:T(8,128)(2,1)} %bitcast.21), calls=%async_computation.2 | async-start | bytes 196608 | tf_op jit(solution)/shard_map/all_to_all | solution.py:313
  131.1 9.6 %shard_map.120 = (bf16[128,6144]{1,0:T(8,128)(2,1)}, bf16[128,6144]{1,0:T(8,128)(2,1)}) custom-call(s32[4]{0:T(128)} %pad_add_fusion.place, bf16[128,6144]{1,0:T(8,128)(2,1)} %bitcast.48, bf16[128,6144]{1,0:T(8,128)(2,1)} %pad_maximum_fusion.space, bf16[128,6144]{1,0:T(8,128)(2,1)} %collective-permute-done.10.other_time, bf16[128,6144]{1,0:T(8,128)(2,1)} %copy-done.4, ...), custom_call_target="tpu_custom_call" | custom-call | flops 4000000000 | bytes 20000000 | tf_op jit(solution)/shard_map/pallas_call | solution.py:398
  140.8 2.2 %all-to-all-done.2 = bf16[16,24,128]{2,1,0:T(8,128)(2,1)S(1)} async-done(((bf16[16,24,128]{2,1,0:T(8,128)(2,1)}), bf16[16,24,128]{2,1,0:T(8,128)(2,1)S(1)}, u32[]{:S(2)}, u32[]{:S(2)}) %all-to-all-start.2) | async-done | bytes 98336 | tf_op jit(solution)/shard_map/all_to_all | solution.py:313
  143.0 5.0 %collective-permute-start.11 = (bf16[128,6144]{1,0:T(8,128)(2,1)}, bf16[128,6144]{1,0:T(8,128)(2,1)}, u32[]{:S(2)}, u32[]{:S(2)}) collective-permute-start(bf16[128,6144]{1,0:T(8,128)(2,1)} %get-tuple-element.57), channel_id=1, source_target_pairs={{0,1},{1,0},{2,3},{3,2},{4,5},{5,4},{6,7},{7,6},{8,9},{9,8},{10,11... | collective-permute-start | bytes 4718600 | tf_op jit(solution)/shard_map/ppermute | solution.py:289
  147.9 3.4 %collective-permute-done.11.on_first.on_second = bf16[128,6144]{1,0:T(8,128)(2,1)} collective-permute-done((bf16[128,6144]{1,0:T(8,128)(2,1)}, bf16[128,6144]{1,0:T(8,128)(2,1)}, u32[]{:S(2)}, u32[]{:S(2)}) %collective-permute-start.11) | collective-permute-done | bytes 1572896 | tf_op jit(solution)/shard_map/ppermute | solution.py:289
  151.3 2.9 %shard_map.122 = bf16[128,6144]{1,0:T(8,128)(2,1)} custom-call(s32[4]{0:T(128)} %pad_add_fusion.place, bf16[128,6144]{1,0:T(8,128)(2,1)} %get-tuple-element.60.on_second.on_first, bf16[128,6144]{1,0:T(8,128)(2,1)} %collective-permute-done.11.on_first.on_second), custom_call_target="tpu_custom_call" | custom-call | flops 1000000 | bytes 3000000 | tf_op jit(solution)/shard_map/pallas_call | solution.py:418
  154.2 4.9 %all-to-all-start.3 = ((bf16[16,8,6144]{2,1,0:T(8,128)(2,1)}), bf16[16,8,6144]{2,1,0:T(8,128)(2,1)}, u32[]{:S(2)}, u32[]{:S(2)}) async-start(bf16[16,8,6144]{2,1,0:T(8,128)(2,1)} %bitcast.44), calls=%async_computation.3 | async-start | bytes 3145728 | tf_op jit(solution)/shard_map/all_to_all | solution.py:313
  159.1 17.1 %all_gather.11 = bf16[96,128]{1,0:T(8,128)(2,1)S(1)} all-gather(bf16[24,128]{1,0:T(8,128)(2,1)S(1)} %reduce_sum.25), channel_id=1, replica_groups=mesh['x'=4,'zh'=4,'y'=4,'zl'=4,'c'=2] {'y'}, dimensions={0}, use_global_device_ids=true | all-gather | bytes 30720 | tf_op jit(solution)/shard_map/all_gather | solution.py:432
  176.2 5.6 %collective-permute-start.12 = (bf16[96,128]{1,0:T(8,128)(2,1)S(1)}, bf16[96,128]{1,0:T(8,128)(2,1)S(1)}, u32[]{:S(2)}, u32[]{:S(2)}) collective-permute-start(bf16[96,128]{1,0:T(8,128)(2,1)S(1)} %all_gather.11), channel_id=1, source_target_pairs={{0,1},{1,0},{2,3},{3,2},{4,5},{5,4},{6,7},{7,6},{8,9},{9,8},{10,11... | collective-permute-start | bytes 73736 | tf_op jit(solution)/shard_map/ppermute | solution.py:289
  181.9 2.9 %shard_map.121 = bf16[128,6144]{1,0:T(8,128)(2,1)} custom-call(s32[4]{0:T(128)} %pad_add_fusion.place, bf16[128,6144]{1,0:T(8,128)(2,1)} %collective-permute-done.11.on_first.on_second, bf16[128,6144]{1,0:T(8,128)(2,1)} %get-tuple-element.60.on_second.on_first), custom_call_target="tpu_custom_call" | custom-call | flops 1000000 | bytes 3000000 | tf_op jit(solution)/shard_map/pallas_call | solution.py:418
  184.8 0.0 collective-permute-done.12
  184.9 0.1 slice_bitcast_fusion
  185.0 0.7 copy.20
  185.7 0.7 copy.19
  186.4 11.3 %all-to-all-done.3 = bf16[16,8,6144]{2,1,0:T(8,128)(2,1)} async-done(((bf16[16,8,6144]{2,1,0:T(8,128)(2,1)}), bf16[16,8,6144]{2,1,0:T(8,128)(2,1)}, u32[]{:S(2)}, u32[]{:S(2)}) %all-to-all-start.3) | async-done | bytes 1572896 | tf_op jit(solution)/shard_map/all_to_all | solution.py:313
  197.7 3.2 %fusion.3 = (bf16[1,1,128,1536]{3,2,1,0:T(8,128)(2,1)}, bf16[1,1,128,1536]{3,2,1,0:T(8,128)(2,1)}, bf16[1,1,128,1536]{3,2,1,0:T(8,128)(2,1)}, bf16[1,1,128,1536]{3,2,1,0:T(8,128)(2,1)}) fusion(bf16[128,6144]{1,0:T(8,128)(2,1)} %bitcast.23, bf16[128,6144]{1,0:T(8,128)(2,1)} %shard_map.121), kind=kLoop, calls=%fused_computation.10 | loop fusion | flops 3145728 | bytes 4718592 | tf_op jit(solution)/shard_map/reshape | solution.py:441
  (16 shorter events, 0.1 us)
Async XLA Ops:
  0.6 1.9 copy-start
  31.7 60.7 %all-to-all-start = ((bf16[16,8,6144]{2,1,0:T(8,128)(2,1)}), bf16[16,8,6144]{2,1,0:T(8,128)(2,1)S(1)}, u32[]{:S(2)}, u32[]{:S(2)}) async-start(bf16[16,8,6144]{2,1,0:T(8,128)(2,1)} %bitcast.13), calls=%async_computation | async-start | bytes 3145728 | tf_op jit(solution)/shard_map/all_to_all | solution.py:313
  36.9 21.3 %collective-permute-start.1 = (bf16[4,112,384]{2,1,0:T(8,128)(2,1)S(1)}, bf16[4,112,384]{2,1,0:T(8,128)(2,1)S(1)}, u32[]{:S(2)}, u32[]{:S(2)}) collective-permute-start(bf16[4,112,384]{2,1,0:T(8,128)(2,1)S(1)} %bitcast.49), channel_id=1, source_target_pairs={{0,128},{1,9},{2,130},{3,11},{4,132},{5,13},{6,134},{7,15},{8,136}... | collective-permute-start | bytes 1032200 | tf_op jit(solution)/shard_map/ppermute | solution.py:289
  40.2 21.3 %collective-permute-start.3 = (bf16[4,112,384]{2,1,0:T(8,128)(2,1)S(1)}, bf16[4,112,384]{2,1,0:T(8,128)(2,1)S(1)}, u32[]{:S(2)}, u32[]{:S(2)}) collective-permute-start(bf16[4,112,384]{2,1,0:T(8,128)(2,1)S(1)} %bitcast.50), channel_id=1, source_target_pairs={{0,384},{1,25},{2,386},{3,27},{4,388},{5,29},{6,390},{7,31},{8,392... | collective-permute-start | bytes 1032200 | tf_op jit(solution)/shard_map/ppermute | solution.py:289
  43.4 20.3 %collective-permute-start.2 = (bf16[4,112,384]{2,1,0:T(8,128)(2,1)S(1)}, bf16[4,112,384]{2,1,0:T(8,128)(2,1)S(1)}, u32[]{:S(2)}, u32[]{:S(2)}) collective-permute-start(bf16[4,112,384]{2,1,0:T(8,128)(2,1)S(1)} %bitcast.51), channel_id=1, source_target_pairs={{0,256},{1,17},{2,258},{3,19},{4,260},{5,21},{6,262},{7,23},{8,264... | collective-permute-start | bytes 1032200 | tf_op jit(solution)/shard_map/ppermute | solution.py:289
  47.0 37.5 %collective-permute-start = (bf16[128,6144]{1,0:T(8,128)(2,1)}, bf16[128,6144]{1,0:T(8,128)(2,1)S(1)}, u32[]{:S(2)}, u32[]{:S(2)}) collective-permute-start(bf16[128,6144]{1,0:T(8,128)(2,1)} %pad_maximum_fusion.space), channel_id=1, source_target_pairs={{0,1},{2,3},{4,5},{6,7},{8,9},{10,11},{12,13},{14,15},{16,17},{18,... | collective-permute-start | bytes 4718600 | tf_op jit(solution)/shard_map/ppermute | solution.py:289
  58.3 39.8 %copy-start.2 = (bf16[2,4,112,384]{3,2,1,0:T(8,128)(2,1)}, bf16[2,4,112,384]{3,2,1,0:T(8,128)(2,1)S(1)}, u32[]{:S(2)}) copy-start(bf16[2,4,112,384]{3,2,1,0:T(8,128)(2,1)S(1)} %pad_maximum_fusion.1.e0) | copy-start | bytes 2064388
  58.3 16.0 %collective-permute-start.4 = (bf16[2,4,112,384]{3,2,1,0:T(8,128)(2,1)S(1)}, bf16[2,4,112,384]{3,2,1,0:T(8,128)(2,1)S(1)}, u32[]{:S(2)}, u32[]{:S(2)}) collective-permute-start(bf16[2,4,112,384]{3,2,1,0:T(8,128)(2,1)S(1)} %pad_maximum_fusion.1.e0), channel_id=1, source_target_pairs={{0,8},{1,129},{2,10},{3,131},{4,12},{5,133},{6,14},{7,135},{8,16},... | collective-permute-start | bytes 2064392 | tf_op jit(solution)/shard_map/ppermute | solution.py:289
  63.8 34.3 %copy-start.3 = (bf16[2,4,112,384]{3,2,1,0:T(8,128)(2,1)}, bf16[2,4,112,384]{3,2,1,0:T(8,128)(2,1)S(1)}, u32[]{:S(2)}) copy-start(bf16[2,4,112,384]{3,2,1,0:T(8,128)(2,1)S(1)} %pad_maximum_fusion.2.l0) | copy-start | bytes 2064388
  63.8 13.1 %collective-permute-start.7 = (bf16[2,4,112,384]{3,2,1,0:T(8,128)(2,1)S(1)}, bf16[2,4,112,384]{3,2,1,0:T(8,128)(2,1)S(1)}, u32[]{:S(2)}, u32[]{:S(2)}) collective-permute-start(bf16[2,4,112,384]{3,2,1,0:T(8,128)(2,1)S(1)} %pad_maximum_fusion.2.l0), channel_id=1, source_target_pairs={{0,24},{1,385},{2,26},{3,387},{4,28},{5,389},{6,30},{7,391},{8,0},... | collective-permute-start | bytes 2064392 | tf_op jit(solution)/shard_map/ppermute | solution.py:289
  69.0 15.2 %collective-permute-start.9 = (bf16[2,4,112,384]{3,2,1,0:T(8,128)(2,1)S(1)}, bf16[2,4,112,384]{3,2,1,0:T(8,128)(2,1)S(1)}, u32[]{:S(2)}, u32[]{:S(2)}) collective-permute-start(bf16[2,4,112,384]{3,2,1,0:T(8,128)(2,1)S(1)} %pad_maximum_fusion.1.e0), channel_id=1, source_target_pairs={{0,24},{1,385},{2,26},{3,387},{4,28},{5,389},{6,30},{7,391},{8,0},... | collective-permute-start | bytes 2064392 | tf_op jit(solution)/shard_map/ppermute | solution.py:289
  71.3 13.2 %collective-permute-start.5 = (bf16[2,4,112,384]{3,2,1,0:T(8,128)(2,1)S(1)}, bf16[2,4,112,384]{3,2,1,0:T(8,128)(2,1)S(1)}, u32[]{:S(2)}, u32[]{:S(2)}) collective-permute-start(bf16[2,4,112,384]{3,2,1,0:T(8,128)(2,1)S(1)} %pad_maximum_fusion.2.l0), channel_id=1, source_target_pairs={{0,8},{1,129},{2,10},{3,131},{4,12},{5,133},{6,14},{7,135},{8,16},... | collective-permute-start | bytes 2064392 | tf_op jit(solution)/shard_map/ppermute | solution.py:289
  74.3 17.2 %copy-start.5 = (bf16[2,4,112,384]{3,2,1,0:T(8,128)(2,1)}, bf16[2,4,112,384]{3,2,1,0:T(8,128)(2,1)S(1)}, u32[]{:S(2)}) copy-start(bf16[2,4,112,384]{3,2,1,0:T(8,128)(2,1)S(1)} %collective-permute-done.4.e1) | copy-start | bytes 2064388
  74.3 17.2 %collective-permute-start.6 = (bf16[2,4,112,384]{3,2,1,0:T(8,128)(2,1)S(1)}, bf16[2,4,112,384]{3,2,1,0:T(8,128)(2,1)S(1)}, u32[]{:S(2)}, u32[]{:S(2)}) collective-permute-start(bf16[2,4,112,384]{3,2,1,0:T(8,128)(2,1)S(1)} %collective-permute-done.4.e1), channel_id=1, source_target_pairs={{0,8},{1,129},{2,10},{3,131},{4,12},{5,133},{6,14},{7,135},{8,16},... | collective-permute-start | bytes 2064392 | tf_op jit(solution)/shard_map/ppermute | solution.py:289
  76.9 14.7 %copy-start.6 = (bf16[2,4,112,384]{3,2,1,0:T(8,128)(2,1)}, bf16[2,4,112,384]{3,2,1,0:T(8,128)(2,1)S(1)}, u32[]{:S(2)}) copy-start(bf16[2,4,112,384]{3,2,1,0:T(8,128)(2,1)S(1)} %collective-permute-done.7.l3) | copy-start | bytes 2064388
  76.9 15.6 %collective-permute-start.8 = (bf16[2,4,112,384]{3,2,1,0:T(8,128)(2,1)S(1)}, bf16[2,4,112,384]{3,2,1,0:T(8,128)(2,1)}, u32[]{:S(2)}, u32[]{:S(2)}) collective-permute-start(bf16[2,4,112,384]{3,2,1,0:T(8,128)(2,1)S(1)} %collective-permute-done.7.l3), channel_id=1, source_target_pairs={{0,24},{1,385},{2,26},{3,387},{4,28},{5,389},{6,30},{7,391},{8,0},... | collective-permute-start | bytes 2064392 | tf_op jit(solution)/shard_map/ppermute | solution.py:289
  84.2 7.3 %copy-start.7 = (bf16[2,4,112,384]{3,2,1,0:T(8,128)(2,1)}, bf16[2,4,112,384]{3,2,1,0:T(8,128)(2,1)S(1)}, u32[]{:S(2)}) copy-start(bf16[2,4,112,384]{3,2,1,0:T(8,128)(2,1)S(1)} %collective-permute-done.9.e3) | copy-start | bytes 2064388
  84.5 7.1 %copy-start.8 = (bf16[2,4,112,384]{3,2,1,0:T(8,128)(2,1)}, bf16[2,4,112,384]{3,2,1,0:T(8,128)(2,1)S(1)}, u32[]{:S(2)}) copy-start(bf16[2,4,112,384]{3,2,1,0:T(8,128)(2,1)S(1)} %collective-permute-done.5.l1) | copy-start | bytes 2064388
  84.5 7.1 %copy-start.4 = (bf16[128,6144]{1,0:T(8,128)(2,1)}, bf16[128,6144]{1,0:T(8,128)(2,1)S(1)}, u32[]{:S(2)}) copy-start(bf16[128,6144]{1,0:T(8,128)(2,1)S(1)} %collective-permute-done.other_space) | copy-start | bytes 4718596
  91.6 0.8 copy-start.9
  92.4 1.2 copy-start.1
  93.6 4.4 %collective-permute-start.10 = (bf16[128,6144]{1,0:T(8,128)(2,1)S(1)}, bf16[128,6144]{1,0:T(8,128)(2,1)}, u32[]{:S(2)}, u32[]{:S(2)}) collective-permute-start(bf16[128,6144]{1,0:T(8,128)(2,1)S(1)} %bitcast.45), channel_id=1, source_target_pairs={{1,0},{3,2},{5,4},{7,6},{9,8},{11,10},{13,12},{15,14},{17,16},{19,... | collective-permute-start | bytes 4718600 | tf_op jit(solution)/shard_map/ppermute | solution.py:289
  105.1 14.3 %all-to-all-start.1 = ((bf16[16,96,128]{2,1,0:T(8,128)(2,1)}), bf16[16,96,128]{2,1,0:T(8,128)(2,1)S(1)}, u32[]{:S(2)}, u32[]{:S(2)}) async-start(bf16[16,96,128]{2,1,0:T(8,128)(2,1)} %bitcast.57), calls=%async_computation.1 | async-start | bytes 786432 | tf_op jit(solution)/shard_map/all_to_all | solution.py:313
  120.1 22.9 %all-to-all-start.2 = ((bf16[16,24,128]{2,1,0:T(8,128)(2,1)}), bf16[16,24,128]{2,1,0:T(8,128)(2,1)S(1)}, u32[]{:S(2)}, u32[]{:S(2)}) async-start(bf16[16,24,128]{2,1,0:T(8,128)(2,1)} %bitcast.21), calls=%async_computation.2 | async-start | bytes 196608 | tf_op jit(solution)/shard_map/all_to_all | solution.py:313
  143.0 8.3 %collective-permute-start.11 = (bf16[128,6144]{1,0:T(8,128)(2,1)}, bf16[128,6144]{1,0:T(8,128)(2,1)}, u32[]{:S(2)}, u32[]{:S(2)}) collective-permute-start(bf16[128,6144]{1,0:T(8,128)(2,1)} %get-tuple-element.57), channel_id=1, source_target_pairs={{0,1},{1,0},{2,3},{3,2},{4,5},{5,4},{6,7},{7,6},{8,9},{9,8},{10,11... | collective-permute-start | bytes 4718600 | tf_op jit(solution)/shard_map/ppermute | solution.py:289
  154.2 43.5 %all-to-all-start.3 = ((bf16[16,8,6144]{2,1,0:T(8,128)(2,1)}), bf16[16,8,6144]{2,1,0:T(8,128)(2,1)}, u32[]{:S(2)}, u32[]{:S(2)}) async-start(bf16[16,8,6144]{2,1,0:T(8,128)(2,1)} %bitcast.44), calls=%async_computation.3 | async-start | bytes 3145728 | tf_op jit(solution)/shard_map/all_to_all | solution.py:313
  176.2 8.6 %collective-permute-start.12 = (bf16[96,128]{1,0:T(8,128)(2,1)S(1)}, bf16[96,128]{1,0:T(8,128)(2,1)S(1)}, u32[]{:S(2)}, u32[]{:S(2)}) collective-permute-start(bf16[96,128]{1,0:T(8,128)(2,1)S(1)} %all_gather.11), channel_id=1, source_target_pairs={{0,1},{1,0},{2,3},{3,2},{4,5},{5,4},{6,7},{7,6},{8,9},{9,8},{10,11... | collective-permute-start | bytes 73736 | tf_op jit(solution)/shard_map/ppermute | solution.py:289
